TPU v7x, 512 devices: a whole 4x8x8 slice. The times are simulated.
512 devices in a mesh: dp: 32 (over x, z), seq: 16 (over y, core).
Axes of the slice: x: 4, y: 8, z: 8, core: 2. Of those that a mesh axis runs over, the one named last changes fastest.
Arguments:
- projected: bfloat16 [32, 2048, 3, 1536], P('dp', 'seq'), may hold values from -6 to 6
- cotangent: bfloat16 [32, 2048, 1152], P('dp', 'seq'), may hold values from -6 to 6
- out_weight: bfloat16 [1536, 1152], P('seq'), may hold values from -0.15625 to 0.15625
- norm_gain: float32 [1536], replicated, may hold values from 0.1 to 1.9
- conv_taps: float32 [9, 1536], replicated, may hold values from -2.5 to 2.5
- feature_seeds: int32 [48], replicated, may hold values from 0 to 1073741823
- packing: int32 [32, 5, 2048], P('dp', None, 'seq'), may hold values from 0 to 68, as said below
Outputs:
- block_out: bfloat16 [32, 2048, 1152], P('dp', 'seq')
- grad_projected: bfloat16 [32, 2048, 3, 1536], P('dp', 'seq')
- grad_out_weight: float32 [1536, 1152], P('seq')
- grad_norm_gain: float32 [1536], replicated
- grad_conv_taps: float32 [9, 1536], replicated
Inputs may be any that keep to these rules, and one draw needn't show every extreme that they name: `packing`: in each pack, images 0 to 2 follow one another, each contiguous and row-major; rows 1 and 2 give a token's row and column in its image, rows 3 and 4 the image's width and height. Widths are multiples of 16 up to 64; image 1 of every pack is 64 wide and directly precedes the last image; the last image of every pack is 16 wide and holds the pack's last 1088 tokens; heights are at least 2; every pack holds 3 images and no padding.
All inputs are finite; a program needn't handle non-finite values.
Results may differ from a plain program's by a relative error of at most 0.012.
Values may be sent and summed in bfloat16 or wider, within the bound.
No kernel may reach another device: no remote copies, remote signals or barrier semaphores. Data moves between devices by JAX's collectives and lax.ppermute only.
A program may use at most 128 MiB of HBM per device.

v0:
```python
import math

import jax
import jax.numpy as jnp
from jax import lax
from jax.sharding import PartitionSpec as P

HEAD = 32
FEAT = 256
IMGS = 3
WMAX = 64


feature_floor = 0.1
epsilon = 1e-06
highest = lax.Precision.HIGHEST


def with_halo(shard, sides, width):
    for axis, dim in sides:
        devices, length = (lax.axis_size(axis), shard.shape[dim])
        up = [(i, (i + 1) % devices) for i in range(devices - 1)]
        down = [(j, i) for i, j in up]
        last = lax.slice_in_dim(shard, length - width, length, axis=dim)
        initial = lax.slice_in_dim(shard, 0, width, axis=dim)
        before = lax.ppermute(last, axis, up)
        after = lax.ppermute(initial, axis, down)
        shard = jnp.concatenate([before, shard, after], axis=dim)
    return shard


def feature_matrix(seed_list):
    counter = jnp.arange(HEAD * FEAT, dtype=jnp.int32).reshape(1, HEAD, FEAT)
    hashed = seed_list[:, None, None] * -1640531535 + counter
    hashed = hashed ^ hashed >> 16 & 65535
    hashed = hashed * -2048144789
    hashed = hashed ^ hashed >> 13 & 524287
    hashed = hashed * -1028477387
    hashed = hashed ^ hashed >> 16 & 65535
    top_bits = hashed >> 8 & 16777215
    uniform = top_bits.astype(jnp.float32) * (1.0 / 16777216.0)
    return (1.7320508 * (2.0 * uniform - 1.0)).astype(jnp.bfloat16)


def neighbour(padded, margin, packing_rows, tap_index, direction):
    row_count = packing_rows.shape[1]
    step_row = tap_index // 3 - 1
    step_col = tap_index % 3 - 1
    position = jnp.arange(row_count, dtype=jnp.int32)
    row_width = packing_rows[3]
    new_row = packing_rows[1] + direction * step_row
    new_col = packing_rows[2] + direction * step_col
    inside = (new_row >= 0) & (new_row < packing_rows[4]) & (new_col >= 0) & (new_col < row_width)
    source = position + margin + direction * (step_row * row_width + step_col)
    return jnp.where(inside[:, None], jnp.take(padded, source, axis=0), jnp.zeros((), padded.dtype))


def depthwise(padded, margin, packing_rows, tap_table, direction):
    running = jnp.zeros((packing_rows.shape[1], padded.shape[1]), jnp.float32)
    for tap_index in range(9):
        running = running + tap_table[tap_index][None, :] * neighbour(
            padded, margin, packing_rows, tap_index, direction
        ).astype(jnp.float32)
    return running


def tap_grads(grad_conv, padded, margin, packing_rows):
    grad_float = grad_conv.astype(jnp.float32)
    return jnp.stack(
        [
            jnp.sum(
                grad_float
                * neighbour(padded, margin, packing_rows, tap_index, 1).astype(jnp.float32),
                axis=0,
            )
            for tap_index in range(9)
        ]
    )


def heads_last(rows_matrix, head_count):
    return rows_matrix.reshape(rows_matrix.shape[0], head_count, HEAD).transpose(1, 2, 0)


def rows_first(head_matrix):
    return head_matrix.transpose(2, 0, 1).reshape(
        head_matrix.shape[2], head_matrix.shape[0] * head_matrix.shape[1]
    )


def local(projected, cotangent, out_weight, norm_gain, conv_taps, feature_seeds, packing):
    groups = lax.axis_size("seq")
    member = lax.axis_index("seq")
    pack_count = lax.axis_size("dp")
    tokens_in = projected[0]
    grad_in = cotangent[0]
    rows_local = packing[0]
    tok_rows = tokens_in.shape[0]
    width_all = tokens_in.shape[2]
    local_width = width_all // groups
    head_count = local_width // HEAD
    all_rows = tok_rows * groups
    margin = WMAX + 1
    feature_scale = 1.0 / math.sqrt(HEAD)
    rows_all = lax.all_gather(rows_local, "seq", axis=1, tiled=True)
    padded_values = with_halo(tokens_in[:, 2], (("seq", 0),), margin)
    conv_tokens = depthwise(padded_values, margin, rows_local, conv_taps, 1).astype(jnp.bfloat16)
    outgoing = jnp.stack([tokens_in[:, 0], tokens_in[:, 1], conv_tokens], axis=1)
    arrived = lax.all_to_all(
        outgoing.reshape(tok_rows, 3, groups, local_width),
        "seq",
        split_axis=2,
        concat_axis=0,
        tiled=True,
    )
    arrived = arrived.reshape(all_rows, 3, local_width)
    conv_heads = arrived[:, 2]
    omegas = feature_matrix(
        lax.dynamic_slice_in_dim(feature_seeds, member * head_count, head_count, 0)
    )
    queries = heads_last(arrived[:, 0], head_count)
    keys_in = heads_last(arrived[:, 1], head_count)
    values_c = heads_last(conv_heads, head_count)
    onehot_float = (jnp.arange(IMGS, dtype=jnp.int32)[:, None] == rows_all[0][None, :]).astype(
        jnp.float32
    )
    onehot_half = onehot_float.astype(jnp.bfloat16)
    pre_query = (
        jnp.einsum("het,hef->hft", queries, omegas, preferred_element_type=jnp.float32)
        * feature_scale
    )
    pre_key = (
        jnp.einsum("het,hef->hft", keys_in, omegas, preferred_element_type=jnp.float32)
        * feature_scale
    )
    feat_query = (jax.nn.relu(pre_query) + feature_floor).astype(jnp.bfloat16)
    feat_key = (jax.nn.relu(pre_key) + feature_floor).astype(jnp.bfloat16)
    masked_values = onehot_half[None, :, None, :] * values_c[:, None]
    states = jnp.einsum(
        "hft,hiet->hife", feat_key, masked_values, preferred_element_type=jnp.float32
    ).astype(jnp.bfloat16)
    totals = jnp.einsum(
        "hft,it->hif", feat_key, onehot_half, preferred_element_type=jnp.float32
    ).astype(jnp.bfloat16)
    numerator = jnp.sum(
        jnp.einsum("hft,hife->hiet", feat_query, states, preferred_element_type=jnp.float32)
        * onehot_float[None, :, None, :],
        axis=1,
    )
    denominator = jnp.sum(
        jnp.einsum("hft,hif->hit", feat_query, totals, preferred_element_type=jnp.float32)
        * onehot_float[None],
        axis=1,
    )
    attention_heads = rows_first(
        (numerator / denominator[:, None, :]).astype(jnp.bfloat16)
    ).reshape(all_rows, 1, local_width)
    attention = lax.all_to_all(
        attention_heads, "seq", split_axis=0, concat_axis=1, tiled=True
    ).reshape(tok_rows, width_all)
    attn_float = attention.astype(jnp.float32)
    inv_rms = lax.rsqrt(jnp.mean(attn_float * attn_float, axis=1) + epsilon)
    normed = (attn_float * norm_gain[None, :] * inv_rms[:, None]).astype(jnp.bfloat16)
    weight_all = lax.all_gather(out_weight, "seq", axis=0, tiled=True)
    block_sum = jnp.dot(normed, weight_all, preferred_element_type=jnp.float32)
    grad_normed = jnp.einsum("td,ad->ta", grad_in, weight_all, preferred_element_type=jnp.float32)
    pack_gain = jnp.sum(grad_normed * attn_float * inv_rms[:, None], axis=0)
    inner_sum = jnp.sum(norm_gain[None, :] * grad_normed * attn_float, axis=1)
    grad_attention = (
        inv_rms[:, None] * norm_gain[None, :] * grad_normed
        - attn_float * (inv_rms**3 * inner_sum / width_all)[:, None]
    ).astype(jnp.bfloat16)
    grad_arrived, normed_heads = (
        lax.all_to_all(
            grad_attention.reshape(tok_rows, groups, local_width),
            "seq",
            split_axis=1,
            concat_axis=0,
            tiled=True,
        ),
        lax.all_to_all(
            normed.reshape(tok_rows, groups, local_width),
            "seq",
            split_axis=1,
            concat_axis=0,
            tiled=True,
        ),
    )
    normed_rows = normed_heads.reshape(all_rows, local_width)
    weight_local = jnp.einsum(
        "tc,td->cd",
        normed_rows,
        lax.all_gather(grad_in, "seq", axis=0, tiled=True),
        preferred_element_type=jnp.float32,
    )
    weight_sum = lax.psum(weight_local, "dp") / pack_count
    grad_float = heads_last(grad_arrived.reshape(all_rows, local_width), head_count).astype(
        jnp.float32
    )
    grad_numer = (grad_float / denominator[:, None, :]).astype(jnp.bfloat16)
    grad_denom = -jnp.sum(grad_float * numerator, axis=1) / (denominator * denominator)
    masked_grad = onehot_half[None, :, None, :] * grad_numer[:, None]
    weighted = onehot_float[None, :, :] * grad_denom[:, None, :]
    grad_states = jnp.einsum(
        "hft,hiet->hife", feat_query, masked_grad, preferred_element_type=jnp.float32
    ).astype(jnp.bfloat16)
    grad_totals = jnp.einsum(
        "hft,hit->hif", feat_query.astype(jnp.float32), weighted, precision=highest
    ).astype(jnp.bfloat16)
    grad_fq = jnp.einsum("hiet,hife->hft", masked_grad, states, preferred_element_type=jnp.float32)
    grad_fq = grad_fq + jnp.einsum(
        "hit,hif->hft", weighted, totals.astype(jnp.float32), precision=highest
    )
    gate_query = jnp.where(pre_query > 0, grad_fq, 0.0).astype(jnp.bfloat16)
    grad_queries = (
        jnp.einsum("hft,hef->het", gate_query, omegas, preferred_element_type=jnp.float32)
        * feature_scale
    ).astype(jnp.bfloat16)
    grad_fk = jnp.einsum(
        "hiet,hife->hft", masked_values, grad_states, preferred_element_type=jnp.float32
    )
    grad_fk = grad_fk + jnp.einsum(
        "it,hif->hft", onehot_float, grad_totals.astype(jnp.float32), precision=highest
    )
    gate_key = jnp.where(pre_key > 0, grad_fk, 0.0).astype(jnp.bfloat16)
    grad_keys = (
        jnp.einsum("hft,hef->het", gate_key, omegas, preferred_element_type=jnp.float32)
        * feature_scale
    ).astype(jnp.bfloat16)
    grad_conv = jnp.sum(
        jnp.einsum("hft,hife->hiet", feat_key, grad_states, preferred_element_type=jnp.float32)
        * onehot_float[None, :, None, :],
        axis=1,
    )
    grad_conv = rows_first(grad_conv.astype(jnp.bfloat16))
    grad_queries = rows_first(grad_queries)
    grad_keys = rows_first(grad_keys)
    returned = lax.all_to_all(
        jnp.stack([grad_queries, grad_keys, grad_conv], axis=1).reshape(
            all_rows, 3, 1, local_width
        ),
        "seq",
        split_axis=0,
        concat_axis=2,
        tiled=True,
    )
    returned = returned.reshape(tok_rows, 3, width_all)
    conv_grad_tokens = returned[:, 2]
    padded_grads = with_halo(conv_grad_tokens, (("seq", 0),), margin)
    grad_values = depthwise(padded_grads, margin, rows_local, conv_taps, -1).astype(jnp.bfloat16)
    taps_grad = tap_grads(conv_grad_tokens, padded_values, margin, rows_local)
    grad_tokens = jnp.stack([returned[:, 0], returned[:, 1], grad_values], axis=1)
    gain_sum, taps_sum = lax.psum((pack_gain, taps_grad), ("dp", "seq"))
    return (
        block_sum.astype(jnp.bfloat16)[None],
        grad_tokens[None],
        weight_sum,
        gain_sum / pack_count,
        taps_sum / pack_count,
    )


def solution(mesh):
    in_specs = (
        P("dp", "seq", None, None),
        P("dp", "seq", None),
        P("seq", None),
        P(),
        P(),
        P(),
        P("dp", None, "seq"),
    )
    out_specs = (P("dp", "seq", None), P("dp", "seq", None, None), P("seq", None), P(), P())
    return jax.shard_map(local, mesh=mesh, in_specs=in_specs, out_specs=out_specs, check_vma=False)
```

profile of v0, /device:TPU:1, one launch (start us, length us, event | category | flops | bytes accessed | tf_op | source)
XLA Modules:
  0.0 517.5 jit_solution(8278285979322742595)
XLA Ops:
  9.0 8.8 %collective-permute-start.1 = (bf16[65,1536]{1,0:T(8,128)(2,1)S(1)}, bf16[65,1536]{1,0:T(8,128)(2,1)S(1)}, u32[]{:S(2)}, u32[]{:S(2)}) collective-permute-start(bf16[65,1536]{1,0:T(8,128)(2,1)S(1)} %get-tuple-element.93), channel_id=1, source_target_pairs={{1,0},{2,1},{3,2},{4,3},{5,4},{6,5},{7,6},{8,7},{9,8},{10,9},{11,1... | collective-permute-start | bytes 599048 | tf_op jit(solution)/shard_map/ppermute | solution.py:27
  17.8 1.9 collective-permute-start
  25.5 1.7 gather_fusion.1
  27.1 1.6 gather_fusion.2
  28.8 1.6 gather_fusion.3
  35.3 3.3 fusion.69
  41.0 4.0 all-to-all-start
  45.8 44.2 %all-gather = s32[1,5,2048]{2,0,1:T(1,128)S(1)} all-gather(s32[1,5,128]{2,0,1:T(1,128)S(1)} %copy-done.60), channel_id=2, replica_groups=mesh['dp'=32,'seq'=16] {'seq'}, dimensions={2}, use_global_device_ids=true | all-gather | bytes 43520 | tf_op jit(solution)/shard_map/all_gather | solution.py:105
  91.3 2.5 fusion.32
  93.8 4.5 add_convert_fusion
  103.3 1.9 reduce.27
  106.2 1.8 reshape.592
  108.0 19.7 %all_to_all.63 = bf16[16,2,6144]{2,1,0:T(2,128)(2,1)} all-to-all(bf16[16,2,6144]{2,1,0:T(2,128)(2,1)S(1)} %reshape.592), channel_id=1, replica_groups=mesh['dp'=32,'seq'=16] {'seq'}, dimensions={0} | all-to-all | bytes 786432 | tf_op jit(solution)/shard_map/all_to_all | solution.py:158
  127.7 3.6 reshape.593
  131.3 2.3 copy.149
  135.9 2.3 copy.151
  138.3 4.3 multiply_reduce_fusion
  144.5 4.6 all-to-all-start.2
  151.2 5.1 fusion.31
  157.4 6.1 %all-to-all-done.2 = bf16[128,16,96]{0,2,1:T(8,128)(2,1)S(1)} async-done(((bf16[128,16,96]{0,2,1:T(8,128)(2,1)}), bf16[128,16,96]{0,2,1:T(8,128)(2,1)S(1)}, u32[]{:S(2)}, u32[]{:S(2)}) %all-to-all-start.2) | async-done | bytes 393248 | tf_op jit(solution)/shard_map/all_to_all | solution.py:174
  164.3 4.1 all-to-all-start.4
  170.9 2.2 reshape.368
  173.0 1.6 fusion.85
  174.6 2.5 convolution_convert_fusion.1
  178.3 3.7 fusion.121
  182.1 4.5 fusion.107
  186.7 4.8 fusion.20
  191.5 4.7 fusion.21
  196.3 4.0 fusion.33
  200.4 2.5 copy.156
  203.0 6.3 %all-to-all-start.3 = ((bf16[2048,3,1,96]{3,1,2,0:T(4,128)(2,1)}), bf16[2048,3,1,96]{3,1,2,0:T(4,128)(2,1)}, u32[]{:S(2)}, u32[]{:S(2)}) async-start(bf16[2048,3,1,96]{3,1,2,0:T(4,128)(2,1)} %copy.156), calls=%async_computation.3 | async-start | bytes 4194304 | tf_op jit(solution)/shard_map/all_to_all | solution.py:238
  209.5 1.9 copy.165
  211.5 4.3 fusion.4
  218.3 2.6 fusion.22
  220.9 150.5 %all-reduce.3.cloned.1.call-done = f32[96,1152]{1,0:T(8,128)} async-done(((f32[96,1152]{1,0:T(8,128)}), f32[96,1152]{1,0:T(8,128)}) %all-reduce.3.cloned.1.call-update) | async-done | bytes 442384 | tf_op jit(solution)/shard_map/psum | solution.py:196
  371.4 1.8 broadcast_multiply_fusion
  373.2 2.9 copy.173
  380.6 2.2 fusion.79
  382.8 1.8 fusion.74
  384.8 7.0 %collective-permute-start.3 = (bf16[65,1536]{1,0:T(8,128)(2,1)S(1)}, bf16[65,1536]{1,0:T(8,128)(2,1)S(1)}, u32[]{:S(2)}, u32[]{:S(2)}) collective-permute-start(bf16[65,1536]{1,0:T(8,128)(2,1)S(1)} %bitcast.347), channel_id=1, source_target_pairs={{1,0},{2,1},{3,2},{4,3},{5,4},{6,5},{7,6},{8,7},{9,8},{10,9},{11,1... | collective-permute-start | bytes 599048 | tf_op jit(solution)/shard_map/ppermute | solution.py:27
  392.1 3.0 collective-permute-start.2
  395.3 96.1 %all-reduce = (f32[1536]{0:T(1024)S(1)}, f32[9,1536]{1,0:T(8,128)S(1)}) all-reduce(f32[1536]{0:T(1024)S(1)} %copy-done.58, f32[9,1536]{1,0:T(8,128)S(1)} %stack.64), channel_id=1, replica_groups=mesh['dp'=32,'seq'=16] {'dp','seq'}, use_global_device_ids=true, to_apply=%region_9.11 | all-reduce | flops 15360 | bytes 122880 | tf_op jit(solution)/shard_map/psum | solution.py:253
  496.9 1.8 gather_fusion.10
  498.7 1.8 gather_fusion.17
  500.4 1.8 gather_fusion.15
  502.4 1.8 gather_fusion.11
  504.2 1.8 gather_fusion.9
  506.2 2.8 fusion.103
  (355 shorter events, 48.8 us)
Async XLA Ops:
  7.2 14.9 %copy-start.60 = (s32[1,5,128]{2,0,1:T(1,128)S(1)}, s32[1,5,128]{2,0,1:T(1,128)}, u32[]{:S(2)}) copy-start(s32[1,5,128]{2,0,1:T(1,128)} %param.15) | copy-start | bytes 7684
  7.2 17.0 %copy-start.59 = (f32[9,1536]{1,0:T(8,128)S(1)}, f32[9,1536]{1,0:T(8,128)}, u32[]{:S(2)}) copy-start(f32[9,1536]{1,0:T(8,128)} %param.13) | copy-start | bytes 165892
  7.2 131.1 %all-gather.5.cloned.1.call-start = ((), (), s32[]{:S(2)}) async-start(), calls=%async_computation.5 | async-start | bytes 3760128 | tf_op jit(solution)/shard_map/all_gather | solution.py:164
  9.0 15.4 %collective-permute-start.1 = (bf16[65,1536]{1,0:T(8,128)(2,1)S(1)}, bf16[65,1536]{1,0:T(8,128)(2,1)S(1)}, u32[]{:S(2)}, u32[]{:S(2)}) collective-permute-start(bf16[65,1536]{1,0:T(8,128)(2,1)S(1)} %get-tuple-element.93), channel_id=1, source_target_pairs={{1,0},{2,1},{3,2},{4,3},{5,4},{6,5},{7,6},{8,7},{9,8},{10,9},{11,1... | collective-permute-start | bytes 599048 | tf_op jit(solution)/shard_map/ppermute | solution.py:27
  17.8 6.6 %collective-permute-start = (bf16[65,1536]{1,0:T(8,128)(2,1)S(1)}, bf16[65,1536]{1,0:T(8,128)(2,1)S(1)}, u32[]{:S(2)}, u32[]{:S(2)}) collective-permute-start(bf16[65,1536]{1,0:T(8,128)(2,1)S(1)} %get-tuple-element.92), channel_id=1, source_target_pairs={{0,1},{1,2},{2,3},{3,4},{4,5},{5,6},{6,7},{7,8},{8,9},{9,10},{10,1... | collective-permute-start | bytes 599048 | tf_op jit(solution)/shard_map/ppermute | solution.py:26
  22.1 12.8 %copy-start.100 = (pred[128]{0:T(512)(128)(4,1)}, pred[128]{0:T(512)(128)(4,1)S(1)}, u32[]{:S(2)}) copy-start(pred[128]{0:T(512)(128)(4,1)S(1)} %get-tuple-element.140) | copy-start | bytes 388
  22.1 12.8 %copy-start.103 = (pred[128]{0:T(512)(128)(4,1)}, pred[128]{0:T(512)(128)(4,1)S(1)}, u32[]{:S(2)}) copy-start(pred[128]{0:T(512)(128)(4,1)S(1)} %get-tuple-element.141) | copy-start | bytes 388
  22.8 12.2 %copy-start.66 = (pred[128]{0:T(512)(128)(4,1)}, pred[128]{0:T(512)(128)(4,1)S(1)}, u32[]{:S(2)}) copy-start(pred[128]{0:T(512)(128)(4,1)S(1)} %get-tuple-element.112) | copy-start | bytes 388
  22.8 12.2 %copy-start.68 = (pred[128]{0:T(512)(128)(4,1)}, pred[128]{0:T(512)(128)(4,1)S(1)}, u32[]{:S(2)}) copy-start(pred[128]{0:T(512)(128)(4,1)S(1)} %get-tuple-element.114) | copy-start | bytes 388
  22.8 12.2 %copy-start.70 = (pred[128]{0:T(512)(128)(4,1)}, pred[128]{0:T(512)(128)(4,1)S(1)}, u32[]{:S(2)}) copy-start(pred[128]{0:T(512)(128)(4,1)S(1)} %get-tuple-element.116) | copy-start | bytes 388
  22.8 12.2 %copy-start.72 = (pred[128]{0:T(512)(128)(4,1)}, pred[128]{0:T(512)(128)(4,1)S(1)}, u32[]{:S(2)}) copy-start(pred[128]{0:T(512)(128)(4,1)S(1)} %get-tuple-element.117) | copy-start | bytes 388
  22.8 12.2 %copy-start.109 = (pred[128]{0:T(512)(128)(4,1)}, pred[128]{0:T(512)(128)(4,1)S(1)}, u32[]{:S(2)}) copy-start(pred[128]{0:T(512)(128)(4,1)S(1)} %get-tuple-element.110) | copy-start | bytes 388
  22.8 12.2 %copy-start.111 = (pred[128]{0:T(512)(128)(4,1)}, pred[128]{0:T(512)(128)(4,1)S(1)}, u32[]{:S(2)}) copy-start(pred[128]{0:T(512)(128)(4,1)S(1)} %get-tuple-element.102) | copy-start | bytes 388
  22.9 8.4 %copy-start.97 = (s32[1024]{0:T(1024)}, s32[1024]{0:T(1024)S(1)}, u32[]{:S(2)}) copy-start(s32[1024]{0:T(1024)S(1)} %pad_clamp_fusion.7) | copy-start | bytes 12292
  22.9 12.1 %copy-start.92 = (pred[128]{0:T(512)(128)(4,1)}, pred[128]{0:T(512)(128)(4,1)S(1)}, u32[]{:S(2)}) copy-start(pred[128]{0:T(512)(128)(4,1)S(1)} %get-tuple-element.71) | copy-start | bytes 388
  22.9 12.1 %copy-start.74 = (pred[128]{0:T(512)(128)(4,1)}, pred[128]{0:T(512)(128)(4,1)S(1)}, u32[]{:S(2)}) copy-start(pred[128]{0:T(512)(128)(4,1)S(1)} %get-tuple-element.118) | copy-start | bytes 388
  23.0 12.1 %copy-start.77 = (pred[128]{0:T(512)(128)(4,1)}, pred[128]{0:T(512)(128)(4,1)S(1)}, u32[]{:S(2)}) copy-start(pred[128]{0:T(512)(128)(4,1)S(1)} %get-tuple-element.119) | copy-start | bytes 388
  23.0 12.1 %copy-start.80 = (pred[128]{0:T(512)(128)(4,1)}, pred[128]{0:T(512)(128)(4,1)S(1)}, u32[]{:S(2)}) copy-start(pred[128]{0:T(512)(128)(4,1)S(1)} %get-tuple-element.120) | copy-start | bytes 388
  23.0 12.1 %copy-start.83 = (pred[128]{0:T(512)(128)(4,1)}, pred[128]{0:T(512)(128)(4,1)S(1)}, u32[]{:S(2)}) copy-start(pred[128]{0:T(512)(128)(4,1)S(1)} %get-tuple-element.121) | copy-start | bytes 388
  23.0 12.1 %copy-start.86 = (pred[128]{0:T(512)(128)(4,1)}, pred[128]{0:T(512)(128)(4,1)S(1)}, u32[]{:S(2)}) copy-start(pred[128]{0:T(512)(128)(4,1)S(1)} %get-tuple-element.122) | copy-start | bytes 388
  23.0 12.1 %copy-start.89 = (pred[128]{0:T(512)(128)(4,1)}, pred[128]{0:T(512)(128)(4,1)S(1)}, u32[]{:S(2)}) copy-start(pred[128]{0:T(512)(128)(4,1)S(1)} %get-tuple-element.125) | copy-start | bytes 388
  23.0 12.1 %copy-start.113 = (pred[128]{0:T(512)(128)(4,1)}, pred[128]{0:T(512)(128)(4,1)S(1)}, u32[]{:S(2)}) copy-start(pred[128]{0:T(512)(128)(4,1)S(1)} %get-tuple-element.73) | copy-start | bytes 388
  23.0 12.1 %copy-start.115 = (pred[128]{0:T(512)(128)(4,1)}, pred[128]{0:T(512)(128)(4,1)S(1)}, u32[]{:S(2)}) copy-start(pred[128]{0:T(512)(128)(4,1)S(1)} %get-tuple-element.123) | copy-start | bytes 388
  23.1 10.1 %copy-start.98 = (s32[1024]{0:T(1024)}, s32[1024]{0:T(1024)S(1)}, u32[]{:S(2)}) copy-start(s32[1024]{0:T(1024)S(1)} %get-tuple-element.139) | copy-start | bytes 12292
  24.1 11.0 %copy-start.106 = (pred[128]{0:T(512)(128)(4,1)}, pred[128]{0:T(512)(128)(4,1)S(1)}, u32[]{:S(2)}) copy-start(pred[128]{0:T(512)(128)(4,1)S(1)} %compare_and_fusion.9) | copy-start | bytes 388
  24.3 10.8 %copy-start.38 = (f32[1536]{0:T(1024)}, f32[1536]{0:T(1024)S(1)}, u32[]{:S(2)}) copy-start(f32[1536]{0:T(1024)S(1)} %get-tuple-element.52) | copy-start | bytes 18436
  24.3 10.8 %copy-start.40 = (f32[1536]{0:T(1024)}, f32[1536]{0:T(1024)S(1)}, u32[]{:S(2)}) copy-start(f32[1536]{0:T(1024)S(1)} %get-tuple-element.53) | copy-start | bytes 18436
  24.3 10.8 %copy-start.42 = (f32[1536]{0:T(1024)}, f32[1536]{0:T(1024)S(1)}, u32[]{:S(2)}) copy-start(f32[1536]{0:T(1024)S(1)} %get-tuple-element.54) | copy-start | bytes 18436
  24.3 10.8 %copy-start.44 = (f32[1536]{0:T(1024)}, f32[1536]{0:T(1024)S(1)}, u32[]{:S(2)}) copy-start(f32[1536]{0:T(1024)S(1)} %get-tuple-element.55) | copy-start | bytes 18436
  24.3 10.8 %copy-start.46 = (f32[1536]{0:T(1024)}, f32[1536]{0:T(1024)S(1)}, u32[]{:S(2)}) copy-start(f32[1536]{0:T(1024)S(1)} %get-tuple-element.56) | copy-start | bytes 18436
  24.3 10.8 %copy-start.48 = (f32[1536]{0:T(1024)}, f32[1536]{0:T(1024)S(1)}, u32[]{:S(2)}) copy-start(f32[1536]{0:T(1024)S(1)} %get-tuple-element.57) | copy-start | bytes 18436
  24.4 10.8 %copy-start.50 = (f32[1536]{0:T(1024)}, f32[1536]{0:T(1024)S(1)}, u32[]{:S(2)}) copy-start(f32[1536]{0:T(1024)S(1)} %get-tuple-element.58) | copy-start | bytes 18436
  24.4 10.8 %copy-start.52 = (f32[1536]{0:T(1024)}, f32[1536]{0:T(1024)S(1)}, u32[]{:S(2)}) copy-start(f32[1536]{0:T(1024)S(1)} %get-tuple-element.59) | copy-start | bytes 18436
  24.4 10.8 %copy-start.54 = (f32[1536]{0:T(1024)}, f32[1536]{0:T(1024)S(1)}, u32[]{:S(2)}) copy-start(f32[1536]{0:T(1024)S(1)} %get-tuple-element.60) | copy-start | bytes 18436
  25.5 9.8 %copy-start.6 = (bf16[128,1536]{1,0:T(8,128)(2,1)}, bf16[128,1536]{1,0:T(8,128)(2,1)S(1)}, u32[]{:S(2)}) copy-start(bf16[128,1536]{1,0:T(8,128)(2,1)S(1)} %gather_fusion) | copy-start | bytes 1179652
  39.8 50.2 %copy-start.124 = (s32[48]{0:T(128)S(1)}, s32[48]{0:T(128)}, u32[]{:S(2)}) copy-start(s32[48]{0:T(128)} %param.14) | copy-start | bytes 580
  41.0 49.2 %all-to-all-start = ((bf16[128,3,16,96]{0,3,1,2:T(8,128)(2,1)}), bf16[128,3,16,96]{0,3,1,2:T(8,128)(2,1)S(1)}, u32[]{:S(2)}, u32[]{:S(2)}) async-start(bf16[128,3,16,96]{0,3,1,2:T(8,128)(2,1)} %copy.146), calls=%async_computation | async-start | bytes 2359296 | tf_op jit(solution)/shard_map/all_to_all | solution.py:109
  45.0 166.4 %all-gather.7.cloned.1.call-start = ((), (), s32[]{:S(2)}) async-start(), calls=%async_computation.7 | async-start | bytes 5013504 | tf_op jit(solution)/shard_map/all_gather | solution.py:193
  90.1 9.1 %copy-start.61 = (bf16[3,2048]{1,0:T(4,128)(2,1)}, bf16[3,2048]{1,0:T(4,128)(2,1)S(1)}, u32[]{:S(2)}) copy-start(bf16[3,2048]{1,0:T(4,128)(2,1)S(1)} %get-tuple-element.97) | copy-start | bytes 36868
  90.2 10.9 %copy-start.17 = (f32[3,2048]{1,0:T(4,128)}, f32[3,2048]{1,0:T(4,128)S(1)}, u32[]{:S(2)}) copy-start(f32[3,2048]{1,0:T(4,128)S(1)} %get-tuple-element.96) | copy-start | bytes 73732
  144.5 19.0 %all-to-all-start.2 = ((bf16[128,16,96]{0,2,1:T(8,128)(2,1)}), bf16[128,16,96]{0,2,1:T(8,128)(2,1)S(1)}, u32[]{:S(2)}, u32[]{:S(2)}) async-start(bf16[128,16,96]{0,2,1:T(8,128)(2,1)} %bitcast.34), calls=%async_computation.2 | async-start | bytes 786432 | tf_op jit(solution)/shard_map/all_to_all | solution.py:174
  164.3 38.7 %all-to-all-start.4 = ((bf16[128,16,96]{0,2,1:T(8,128)(2,1)}), bf16[128,16,96]{0,2,1:T(8,128)(2,1)}, u32[]{:S(2)}, u32[]{:S(2)}) async-start(bf16[128,16,96]{0,2,1:T(8,128)(2,1)} %copy.164), calls=%async_computation.4 | async-start | bytes 786432 | tf_op jit(solution)/shard_map/all_to_all | solution.py:181
  203.0 170.2 %all-to-all-start.3 = ((bf16[2048,3,1,96]{3,1,2,0:T(4,128)(2,1)}), bf16[2048,3,1,96]{3,1,2,0:T(4,128)(2,1)}, u32[]{:S(2)}, u32[]{:S(2)}) async-start(bf16[2048,3,1,96]{3,1,2,0:T(4,128)(2,1)} %copy.156), calls=%async_computation.3 | async-start | bytes 4194304 | tf_op jit(solution)/shard_map/all_to_all | solution.py:238
  209.3 162.1 %all-reduce.3.cloned.1.call-start = ((), (), s32[]{:S(2)}) async-start(), calls=%async_computation.6 | async-start | bytes 884736 | tf_op jit(solution)/shard_map/psum | solution.py:196
  379.1 12.7 %copy-start.21 = (bf16[65,1,1536]{0,2,1:T(8,128)(2,1)S(1)}, bf16[65,1,1536]{0,2,1:T(8,128)(2,1)}, u32[]{:S(2)}) copy-start(bf16[65,1,1536]{0,2,1:T(8,128)(2,1)} %get-tuple-element.87) | copy-start | bytes 599044
  380.6 14.7 %copy-start.58 = (f32[1536]{0:T(1024)S(1)}, f32[1536]{0:T(1024)}, u32[]{:S(2)}) copy-start(f32[1536]{0:T(1024)} %get-tuple-element.41) | copy-start | bytes 18436
  384.8 107.9 %collective-permute-start.3 = (bf16[65,1536]{1,0:T(8,128)(2,1)S(1)}, bf16[65,1536]{1,0:T(8,128)(2,1)S(1)}, u32[]{:S(2)}, u32[]{:S(2)}) collective-permute-start(bf16[65,1536]{1,0:T(8,128)(2,1)S(1)} %bitcast.347), channel_id=1, source_target_pairs={{1,0},{2,1},{3,2},{4,3},{5,4},{6,5},{7,6},{8,7},{9,8},{10,9},{11,1... | collective-permute-start | bytes 599048 | tf_op jit(solution)/shard_map/ppermute | solution.py:27
  392.1 100.6 %collective-permute-start.2 = (bf16[65,1536]{1,0:T(8,128)(2,1)S(1)}, bf16[65,1536]{1,0:T(8,128)(2,1)S(1)}, u32[]{:S(2)}, u32[]{:S(2)}) collective-permute-start(bf16[65,1536]{1,0:T(8,128)(2,1)S(1)} %bitcast.348), channel_id=1, source_target_pairs={{0,1},{1,2},{2,3},{3,4},{4,5},{5,6},{6,7},{7,8},{8,9},{9,10},{10,1... | collective-permute-start | bytes 599048 | tf_op jit(solution)/shard_map/ppermute | solution.py:26
  (88 other events, 373.2 us)
Sparse Core Ops, SparseCore 0:
  10.1 62.2 all-gather.4
  74.6 53.0 all-gather.6
  215.9 155.4 all-reduce.2
where the time goes:
time: 524 us; the launch traced here: 518 us
  blocking collectives  160 us (31%)
  waiting for transfers between devices  158 us (30%)
  local copies, waits for them, and re-layouts  67.4 us (13%)
  matrix products  46.9 us (9%)
  starting transfers between devices  40.1 us (8%)
  other arithmetic  28.9 us (6%)
  between operations  16.1 us (3%)
    psum x1, waiting for transfers between devices, local(): weight_sum = lax.psum(weight_local, 'dp') / pack_count  151 us
    psum x1, blocking collectives, local(): gain_sum, taps_sum = lax.psum((pack_gain, taps_grad), ('dp', 'seq'))  96.1 us
    all_gather x1, blocking collectives, local(): rows_all = lax.all_gather(rows_local, 'seq', axis=1, tiled=True)  44.2 us
    gather x18, local copies, waits for them, and re-layouts, neighbour(): jnp.take(padded, source, axis=0)  23.2 us
    all_to_all x1, blocking collectives, local(): lax.all_to_all(attention_heads, 'seq', split_axis=0, concat_axis=1, tiled...  19.7 us
    ppermute x2, starting transfers between devices, with_halo(): after = lax.ppermute(initial, axis, down)  15.8 us
    unnamed x258, local copies, waits for them, and re-layouts  12.1 us
  transfers between devices with their start and end apart: 11, of which 2 were waited for; matrix products, arithmetic and copies ran while one was open for 22% of the time, Pallas kernels for 0%

commit v1 on v0

v1 whole, which is shorter than its diff:
```python
import math

import jax
import jax.numpy as jnp
from jax import lax
from jax.experimental import pallas as pl
from jax.experimental.pallas import tpu as pltpu
from jax.sharding import PartitionSpec as P

HEAD = 32
FEAT = 256
LANES = 128
CHUNK = 256
WIDTHS = (16, 32, 48, 64)

feature_floor = 0.1
epsilon = 1e-06
scale = 1.0 / math.sqrt(HEAD)
bf16, f32 = jnp.bfloat16, jnp.float32


def dot(a, b):
    return lax.dot_general(a, b, (((1,), (0,)), ((), ())), preferred_element_type=f32)


def dot_nt(a, b):
    return lax.dot_general(a, b, (((1,), (1,)), ((), ())), preferred_element_type=f32)


def omega_of(seed, e, f):
    hashed = seed * -1640531535 + (e * FEAT + f)
    hashed = hashed ^ ((hashed >> 16) & 65535)
    hashed = hashed * -2048144789
    hashed = hashed ^ ((hashed >> 13) & 524287)
    hashed = hashed * -1028477387
    hashed = hashed ^ ((hashed >> 16) & 65535)
    uniform = ((hashed >> 8) & 16777215).astype(f32) * (1.0 / 16777216.0)
    return 1.7320508 * (2.0 * uniform - 1.0)


def omega_tall(seed_row, heads):
    shape = (FEAT, heads * HEAD)
    lane = lax.broadcasted_iota(jnp.int32, shape, 1)
    block = omega_of(seed_row, lane % HEAD, lax.broadcasted_iota(jnp.int32, shape, 0))
    return jnp.concatenate(
        [jnp.where(lane // HEAD == h, block, 0.0) for h in range(heads)], axis=0
    ).astype(bf16)


def omega_wide(seed_column, heads):
    shape = (heads * HEAD, FEAT)
    row = lax.broadcasted_iota(jnp.int32, shape, 0)
    block = omega_of(seed_column, row % HEAD, lax.broadcasted_iota(jnp.int32, shape, 1))
    return jnp.concatenate(
        [jnp.where(row // HEAD == h, block, 0.0) for h in range(heads)], axis=1
    ).astype(bf16)


def head_mask(heads):
    shape = (LANES, heads * FEAT)
    row = lax.broadcasted_iota(jnp.int32, shape, 0)
    column = lax.broadcasted_iota(jnp.int32, shape, 1) // FEAT
    width = heads * HEAD
    channel = (row < width) & (row // HEAD == column)
    total = (row >= width) & (row < width + 3 * heads) & ((row - width) % heads == column)
    return channel | total


def chunk_of(ref, part, width, j):
    rows = pl.ds(part * width, width)
    return jnp.concatenate([ref[2 * j, rows, :], ref[2 * j + 1, rows, :]], axis=1)


def part_of(ref, start, count):
    return jnp.concatenate(
        [ref[s, pl.ds(start, count), :] for s in range(ref.shape[0])], axis=1
    )


def by_head(rows, heads):
    return jnp.concatenate(
        [jnp.broadcast_to(rows[h : h + 1], (HEAD, rows.shape[1])) for h in range(heads)], axis=0
    )


def head_sums(values, heads):
    return [
        jnp.sum(values[h * HEAD : (h + 1) * HEAD], axis=0, keepdims=True) for h in range(heads)
    ]


def shifted(values, shift):
    return pltpu.roll(values, shift % values.shape[1], axis=1)


class Grid:
    def __init__(self, ref, start):
        packing = part_of(ref, start, 16).astype(f32)
        self.image, self.row, self.column, self.width, self.height = (
            packing[i : i + 1] for i in range(5)
        )
        self.left = self.column > 0.5
        self.right = self.column < self.width - 1.5
        self.above = self.row > 0.5
        self.below = self.row < self.height - 1.5

    def column_before(self, values):
        return jnp.where(self.left, shifted(values, 1), 0.0)

    def column_after(self, values):
        return jnp.where(self.right, shifted(values, -1), 0.0)

    def by_rows(self, values, inside, sign):
        half = values.shape[1] // 2
        moved = jnp.where(inside & (self.width == 16.0), shifted(values, sign * 16), 0.0)
        front, back = moved[:, :half], moved[:, half:]
        for width in WIDTHS[1:]:
            mask = inside[:, :half] & (self.width[:, :half] == float(width))
            front = front + jnp.where(mask, shifted(values[:, :half], sign * width), 0.0)
        return jnp.concatenate([front, back], axis=1)

    def row_above(self, values):
        return self.by_rows(values, self.above, 1)

    def row_below(self, values):
        return self.by_rows(values, self.below, -1)


def features(pre):
    return (jnp.maximum(pre, 0.0) + feature_floor).astype(bf16)


def split_images(rows, image, j, middle):
    zero = jnp.zeros((), rows.dtype)
    front = back = None
    if j < middle:
        front = jnp.concatenate(
            [jnp.where(image == 0.0, rows, zero), jnp.where(image == 1.0, rows, zero)], axis=0
        ).astype(bf16)
    if j >= middle - 1:
        back = jnp.where(image == 2.0, rows, zero).astype(bf16)
    return front, back


def add(total, term):
    return term if total is None else total + term


def pick_image(left, right, image, j, middle, rows):
    if j < middle - 1:
        both = dot(left[: 2 * LANES], right)
        return jnp.where(image == 0.0, both[:rows], both[LANES : LANES + rows])
    if j >= middle:
        return dot(left[2 * LANES :], right)[:rows]
    every = dot(left, right)
    front = jnp.where(image == 0.0, every[:rows], every[LANES : LANES + rows])
    return jnp.where(image == 2.0, every[2 * LANES : 2 * LANES + rows], front)


def ones_rows(width, columns, count):
    row = lax.broadcasted_iota(jnp.int32, (LANES - width, columns), 0)
    return jnp.where(row < count, 1.0, 0.0)


def forward_kernel(heads, x_ref, taps_ref, seed_row_ref, weight_ref,
                   numer_ref, denom_ref, states_ref, conv_ref, weight_out):
    width = heads * HEAD
    chunks = x_ref.shape[0] * LANES // CHUNK
    middle = chunks // 2
    weight_out[...] = weight_ref[...]
    grid = Grid(x_ref, 3 * width)
    values = part_of(x_ref, 2 * width, width).astype(f32)
    taps = taps_ref[...]
    trio = (grid.column_before(values), values, grid.column_after(values))

    def row_of_taps(r):
        return sum(taps[:, 3 * r + c : 3 * r + c + 1] * trio[c] for c in range(3))

    conv = row_of_taps(1) + grid.row_above(row_of_taps(0)) + grid.row_below(row_of_taps(2))
    conv_ref[...] = conv.astype(bf16)
    omega = omega_tall(seed_row_ref[...], heads)
    front = back = None
    for j in range(chunks):
        lanes = pl.ds(j * CHUNK, CHUNK)
        image = grid.image[:, j * CHUNK : (j + 1) * CHUNK]
        rows = jnp.concatenate(
            [conv_ref[:, lanes].astype(f32), ones_rows(width, CHUNK, 3 * heads)], axis=0
        )
        feat_key = features(dot(omega, chunk_of(x_ref, 1, width, j)) * scale)
        first, last = split_images(rows, image, j, middle)
        if first is not None:
            front = add(front, dot_nt(first, feat_key))
        if last is not None:
            back = add(back, dot_nt(last, feat_key))
    mask = head_mask(heads)
    states = jnp.concatenate(
        [
            jnp.where(mask, part, 0.0).astype(bf16)
            for part in (front[:LANES], front[LANES:], back)
        ],
        axis=0,
    )
    states_ref[...] = states
    for j in range(chunks):
        lanes = pl.ds(j * CHUNK, CHUNK)
        image = grid.image[:, j * CHUNK : (j + 1) * CHUNK]
        feat_query = features(dot(omega, chunk_of(x_ref, 0, width, j)) * scale)
        both = pick_image(states, feat_query, image, j, middle, width + 8)
        numer_ref[:, lanes] = both[:width]
        denom_ref[:, lanes] = both[width : width + 8]


def sums_kernel(heads, numer_ref, denom_ref, weight_ref, cotangent_ref, gain_ref,
                grad_normed_ref, sums_ref):
    chunks = numer_ref.shape[1] // CHUNK
    weight, gain = weight_ref[...], gain_ref[...]
    squares, inner = [], []
    for j in range(chunks):
        lanes = pl.ds(j * CHUNK, CHUNK)
        grad_normed = dot_nt(weight, cotangent_ref[pl.ds(j * CHUNK, CHUNK), :])
        grad_normed_ref[:, lanes] = grad_normed
        attention = (numer_ref[:, lanes] / by_head(denom_ref[:, lanes], heads)).astype(bf16)
        attention = attention.astype(f32)
        square = jnp.sum(attention * attention, axis=0, keepdims=True)
        product = jnp.sum(gain * grad_normed * attention, axis=0, keepdims=True)
        for part in range(CHUNK // LANES):
            here = slice(part * LANES, (part + 1) * LANES)
            squares.append(square[:, here])
            inner.append(product[:, here])
    both = jnp.concatenate(squares + inner, axis=0)
    for peer in range(sums_ref.shape[0]):
        sums_ref[peer] = both


def normed_kernel(heads, numer_ref, denom_ref, grad_normed_ref, sums_ref, gain_ref, cotangent_ref,
                  normed_ref, grad_ref, weight_ref, gain_out):
    chunks = numer_ref.shape[1] // CHUNK
    groups = sums_ref.shape[0]
    width = heads * HEAD
    gain = gain_ref[...]
    sums = jnp.sum(sums_ref[...], axis=0)
    inverse = lax.rsqrt(sums[:groups] * (1.0 / (width * groups)) + epsilon)
    inner = inverse * inverse * inverse * sums[groups:] * (1.0 / (width * groups))
    weight = gain_sum = None
    for j in range(chunks):
        lanes = pl.ds(j * CHUNK, CHUNK)

        def tokens(values):
            return jnp.concatenate([values[2 * j : 2 * j + 1], values[2 * j + 1 : 2 * j + 2]], axis=1)

        inv_rms, away = tokens(inverse), tokens(inner)
        grad_normed = grad_normed_ref[:, lanes]
        attention = (numer_ref[:, lanes] / by_head(denom_ref[:, lanes], heads)).astype(bf16)
        attention = attention.astype(f32)
        normed = (attention * gain * inv_rms).astype(bf16)
        grad_ref[:, lanes] = inv_rms * gain * grad_normed - attention * away
        gain_sum = add(gain_sum, grad_normed * attention * inv_rms)
        for part in range(CHUNK // LANES):
            normed_ref[2 * j + part] = normed[:, part * LANES : (part + 1) * LANES]
        weight = add(weight, dot(normed, cotangent_ref[pl.ds(j * CHUNK, CHUNK), :]))
    gain_out[...] = jnp.broadcast_to(jnp.sum(gain_sum, axis=1, keepdims=True), gain_out.shape)
    across = weight.shape[1] // LANES
    for r in range(width // 8):
        for c in range(across):
            weight_ref[pl.ds((r * across + c) * 8, 8), :] = weight[
                r * 8 : (r + 1) * 8, c * LANES : (c + 1) * LANES
            ]
    used = width * across
    weight_ref[used:, :] = jnp.zeros((weight_ref.shape[0] - used, LANES), f32)


def backward_kernel(heads, x_ref, taps_ref, seed_row_ref, seed_column_ref, numer_ref, denom_ref,
                    states_ref, conv_ref, normed_ref, grad_ref, gain_ref,
                    out_ref, small_ref, grad_conv_ref):
    width = heads * HEAD
    chunks = x_ref.shape[0] * LANES // CHUNK
    middle = chunks // 2
    grid = Grid(x_ref, 3 * width)
    omega = omega_tall(seed_row_ref[...], heads)
    omega_back = omega_wide(seed_column_ref[...], heads)
    states = jnp.transpose(states_ref[...].astype(f32)).astype(bf16)
    mask = head_mask(heads)
    front = back = None

    def put(part, j, values):
        for half in range(CHUNK // LANES):
            out_ref[2 * j + half, pl.ds(part * width, width), :] = values[
                :, half * LANES : (half + 1) * LANES
            ]

    def spread(table, first, last):
        total = None
        if first is not None:
            total = add(total, dot(table[:, : 2 * LANES], first))
        if last is not None:
            total = add(total, dot(table[:, 2 * LANES :], last))
        return total

    for j in range(chunks):
        lanes = pl.ds(j * CHUNK, CHUNK)
        image = grid.image[:, j * CHUNK : (j + 1) * CHUNK]
        pre = dot(omega, chunk_of(x_ref, 0, width, j)) * scale
        feat_query = features(pre)
        grad = grad_ref[:, lanes].astype(bf16).astype(f32)
        denom = denom_ref[:, lanes]
        grad_numer = (grad / by_head(denom, heads)).astype(bf16).astype(f32)
        dots = head_sums(grad * numer_ref[:, lanes], heads)
        row = lax.broadcasted_iota(jnp.int32, (LANES - width, CHUNK), 0)
        extra = jnp.zeros((LANES - width, CHUNK), f32)
        for h in range(heads):
            below = denom[h : h + 1]
            rest = -dots[h] / (below * below)
            for level in range(3):
                high = rest.astype(bf16).astype(f32)
                extra = jnp.where(row == level * heads + h, high, extra)
                rest = rest - high
        rows = jnp.concatenate([grad_numer, extra], axis=0)
        first, last = split_images(rows, image, j, middle)
        if first is not None:
            front = add(front, dot_nt(first, feat_query))
        if last is not None:
            back = add(back, dot_nt(last, feat_query))
        gate = jnp.where(pre > 0, spread(states, first, last), 0.0).astype(bf16)
        put(1, j, (dot(omega_back, gate) * scale).astype(bf16))
    parts = []
    for part in (front[:LANES], front[LANES:], back):
        part = jnp.where(mask, part, 0.0)
        total = jnp.sum(part[width:], axis=0, keepdims=True)
        row = lax.broadcasted_iota(jnp.int32, (LANES - width, heads * FEAT), 0)
        parts.append(part[:width])
        parts.append(jnp.where(row == 0, total, 0.0))
    grad_states = jnp.concatenate(parts, axis=0)
    table = jnp.transpose(grad_states).astype(bf16)
    grad_states = grad_states.astype(bf16)
    for j in range(chunks):
        lanes = pl.ds(j * CHUNK, CHUNK)
        image = grid.image[:, j * CHUNK : (j + 1) * CHUNK]
        pre = dot(omega, chunk_of(x_ref, 1, width, j)) * scale
        feat_key = features(pre)
        rows = jnp.concatenate(
            [conv_ref[:, lanes].astype(f32), ones_rows(width, CHUNK, 1)], axis=0
        )
        first, last = split_images(rows, image, j, middle)
        gate = jnp.where(pre > 0, spread(table, first, last), 0.0).astype(bf16)
        put(2, j, (dot(omega_back, gate) * scale).astype(bf16))
        grad_conv_ref[:, lanes] = (
            pick_image(grad_states, feat_key, image, j, middle, width).astype(bf16).astype(f32)
        )
    grad_conv = grad_conv_ref[...]
    values = part_of(x_ref, 2 * width, width).astype(f32)
    taps = taps_ref[...]
    trio = (grid.column_before(values), values, grid.column_after(values))
    moved = (grid.row_below(grad_conv), grad_conv, grid.row_above(grad_conv))
    lane = lax.broadcasted_iota(jnp.int32, (width, LANES), 1)
    small = jnp.where(lane == 9, gain_ref[...], 0.0)
    for r in range(3):
        for c in range(3):
            total = jnp.sum(moved[r] * trio[c], axis=1, keepdims=True)
            small = jnp.where(lane == 3 * r + c, total, small)

    def column_of_taps(c):
        return sum(taps[:, 3 * r + c : 3 * r + c + 1] * moved[r] for r in range(3))

    grad_values = (
        column_of_taps(1)
        + grid.column_after(column_of_taps(0))
        + grid.column_before(column_of_taps(2))
    ).astype(bf16)
    small = jnp.concatenate([small, jnp.zeros((LANES - width, LANES), f32)], axis=0)
    small_ref[...] = jnp.transpose(small)[: small_ref.shape[0]]
    for s in range(x_ref.shape[0]):
        out_ref[s, pl.ds(0, width), :] = normed_ref[s]
        out_ref[s, pl.ds(3 * width, width), :] = grad_values[:, s * LANES : (s + 1) * LANES]
        out_ref[s, pl.ds(4 * width, 16), :] = jnp.zeros((16, LANES), bf16)


def pack_sum_kernel(parts_ref, small_ref, out_ref):
    packs = parts_ref.shape[0]
    rows = parts_ref.shape[1]
    total = jnp.sum(parts_ref[...], axis=0) * (1.0 / packs)
    small = small_ref[...]
    for peer in range(packs):
        out_ref[peer, pl.ds(0, rows), :] = total
        out_ref[peer, pl.ds(rows, 16), :] = small


def unpack_kernel(gathered_ref, outgoing_ref, weight_ref, payload_ref):
    packs = gathered_ref.shape[0]
    rows = gathered_ref.shape[1] - 16
    width, features_out = weight_ref.shape
    across = features_out // LANES
    for r in range(width // 8):
        for c in range(across):
            start = (r * across + c) * 8
            weight_ref[pl.ds(r * 8, 8), pl.ds(c * LANES, LANES)] = gathered_ref[
                start // rows, pl.ds(start % rows, 8), :
            ]
    small = jnp.sum(gathered_ref[:, pl.ds(rows, 16), :], axis=0) * (1.0 / packs)
    for peer in range(payload_ref.shape[0]):
        payload_ref[peer] = small.astype(bf16)


def call(kernel, name, out_shapes, operands, scratch=(), **more):
    return pl.pallas_call(
        kernel,
        name=name,
        out_shape=[jax.ShapeDtypeStruct(shape, kind) for shape, kind in out_shapes],
        scratch_shapes=list(scratch),
        compiler_params=pltpu.CompilerParams(vmem_limit_bytes=56 * 1024 * 1024),
        **more,
    )(*operands)


def swap(blocks, axis):
    return lax.all_to_all(blocks, axis, split_axis=0, concat_axis=0, tiled=True)


def local(projected, cotangent, out_weight, norm_gain, conv_taps, feature_seeds, packing):
    groups = lax.axis_size("seq")
    member = lax.axis_index("seq")
    packs = lax.axis_size("dp")
    tokens, _, width_all = projected.shape[1:]
    features_out = cotangent.shape[2]
    width = width_all // groups
    heads = width // HEAD
    all_tokens = tokens * groups
    cotangent_all = lax.all_gather(cotangent[0], "seq", axis=0, tiled=True)
    by_peer = projected[0].transpose(1, 2, 0).reshape(3, groups, width, tokens)
    by_peer = by_peer.transpose(1, 0, 2, 3).reshape(groups, 3 * width, tokens)
    rows = jnp.pad(packing[0].astype(bf16), ((0, 11), (0, 0)))
    outgoing = jnp.concatenate(
        [by_peer, jnp.broadcast_to(rows[None], (groups, 16, tokens))], axis=1
    )
    seeds = jnp.repeat(lax.dynamic_slice_in_dim(feature_seeds, member * heads, heads, 0), HEAD)
    taps = jnp.pad(
        lax.dynamic_slice_in_dim(conv_taps, member * width, width, 1).T, ((0, 0), (0, 7))
    )
    gain = lax.dynamic_slice_in_dim(norm_gain, member * width, width, 0)[:, None]
    x = swap(outgoing, "seq")
    numer, denom, states, conv, weight_local = call(
        lambda *refs: forward_kernel(heads, *refs),
        "forward",
        [
            ((width, all_tokens), f32),
            ((8, all_tokens), f32),
            ((3 * LANES, heads * FEAT), bf16),
            ((width, all_tokens), bf16),
            ((width, features_out), bf16),
        ],
        (x, taps, seeds[None], out_weight),
    )
    weight_all = lax.all_gather(weight_local, "seq", axis=0, tiled=True)
    grad_normed, sums = call(
        lambda *refs: sums_kernel(heads, *refs),
        "sums",
        [((width, all_tokens), f32), ((groups, 2 * groups, LANES), f32)],
        (numer, denom, out_weight, cotangent_all, gain),
    )
    sums = swap(sums, "seq")
    normed, grad, weight_tiles, gain_part = call(
        lambda *refs: normed_kernel(heads, *refs),
        "normed",
        [
            ((groups, width, LANES), bf16),
            ((width, all_tokens), f32),
            ((1024, LANES), f32),
            ((width, LANES), f32),
        ],
        (numer, denom, grad_normed, sums, gain, cotangent_all),
    )
    weight_parts = swap(weight_tiles.reshape(packs, 1024 // packs, LANES), "dp")
    leaving, small = call(
        lambda *refs: backward_kernel(heads, *refs),
        "backward",
        [((groups, 4 * width + 16, LANES), bf16), ((16, LANES), f32)],
        (x, taps, seeds[None], seeds[:, None], numer, denom, states, conv, normed, grad, gain_part),
        scratch=[pltpu.VMEM((width, all_tokens), f32)],
    )
    shared = call(
        pack_sum_kernel,
        "pack_sum",
        [((packs, 1024 // packs + 16, LANES), f32)],
        (weight_parts, small),
    )[0]
    gathered = swap(shared, "dp")
    weight_grad, leaving = call(
        unpack_kernel,
        "unpack",
        [((width, features_out), f32), (leaving.shape, bf16)],
        (gathered, leaving),
        grid=(1,),
        in_specs=[
            pl.BlockSpec(gathered.shape, lambda i: (0, 0, 0)),
            pl.BlockSpec(memory_space=pl.ANY),
        ],
        out_specs=[
            pl.BlockSpec((width, features_out), lambda i: (0, 0)),
            pl.BlockSpec((groups, 16, LANES), lambda i: (0, 4 * width // 16, 0)),
        ],
        input_output_aliases={1: 1},
    )
    back = swap(leaving, "seq")
    normed_rows = back[:, :width].reshape(width_all, tokens)
    block_out = lax.dot_general(
        normed_rows, weight_all, (((0,), (0,)), ((), ())), preferred_element_type=f32
    ).astype(bf16)
    grads = back[:, width : 4 * width].reshape(groups, 3, width, tokens)
    grad_tokens = grads.transpose(3, 1, 0, 2).reshape(tokens, 3, width_all)
    small_all = back[:, 4 * width : 4 * width + 10, :width].astype(f32)
    small_all = small_all.transpose(1, 0, 2).reshape(10, width_all)
    return block_out[None], grad_tokens[None], weight_grad, small_all[9], small_all[:9]


def solution(mesh):
    in_specs = (
        P("dp", "seq", None, None),
        P("dp", "seq", None),
        P("seq", None),
        P(),
        P(),
        P(),
        P("dp", None, "seq"),
    )
    out_specs = (P("dp", "seq", None), P("dp", "seq", None, None), P("seq", None), P(), P())
    return jax.shard_map(local, mesh=mesh, in_specs=in_specs, out_specs=out_specs, check_vma=False)
```

time: 524 us -> 230 us (0.44); the launches traced: 518 us -> 229 us
  waiting for transfers between devices: 158 us -> 47.2 us
  blocking collectives: 160 us -> 92.6 us
  local copies, waits for them, and re-layouts: 67.4 us -> 11.2 us
  matrix products: 46.9 us -> 3.43 us
  Pallas kernels: 0 us -> 36.4 us
  other arithmetic: 28.9 us -> 1.16 us
  starting transfers between devices: 40.1 us -> 23.2 us
    psum x1 -> x0, waiting for transfers between devices: 151 us -> none  [local(): weight_sum = lax.psum(weight_local, 'dp') / pack_count]
    psum x1 -> x0, blocking collectives: 96.1 us -> none  [local(): gain_sum, taps_sum = lax.psum((pack_gain, taps_grad), ('dp', 'seq'))]
    all_to_all x1 -> x3, blocking collectives: 19.7 us -> 92.6 us  [swap(): return lax.all_to_all(blocks, axis, split_axis=0, concat_axis=0, tiled=True)]
    all_gather x1 -> x0, blocking collectives: 44.2 us -> none  [local(): rows_all = lax.all_gather(rows_local, 'seq', axis=1, tiled=True)]
    dot_general x16 -> x1, matrix products: 46.9 us -> 3.43 us  [local(): lax.dot_general(normed_rows, weight_all, (((0,), (0,)), ((), ())), prefer...]
    pallas_call x0 -> x6, Pallas kernels: none -> 36.4 us  [call(): pl.pallas_call(kernel, name=name, out_shape=[jax.ShapeDtypeStruct(shape,...]
    all_to_all x4 -> x2, waiting for transfers between devices: 6.15 us -> 40.7 us  [swap(): return lax.all_to_all(blocks, axis, split_axis=0, concat_axis=0, tiled=True)]
    gather x18 -> x0, local copies, waits for them, and re-layouts: 23.2 us -> none  [neighbour(): jnp.take(padded, source, axis=0)]
  transfers between devices with their start and end apart: 11 -> 4, of which waited for: 2 -> 3; matrix products, arithmetic and copies ran while one was open for 22% -> 4% of each run, Pallas kernels for 0% -> 16%
where the time goes in v1:
time: 230 us; the launch traced here: 229 us
  blocking collectives  92.6 us (40%)
  waiting for transfers between devices  47.2 us (21%)
  Pallas kernels  36.4 us (16%)
  starting transfers between devices  23.2 us (10%)
  between operations  14.2 us (6%)
  local copies, waits for them, and re-layouts  11.2 us (5%)
  matrix products  3.43 us (1%)
    all_to_all x3, blocking collectives, swap(): return lax.all_to_all(blocks, axis, split_axis=0, concat_axis=0, tiled=True)  92.6 us
    all_to_all x2, waiting for transfers between devices, swap(): return lax.all_to_all(blocks, axis, split_axis=0, concat_axis=0, tiled=True)  40.7 us
    pallas_call x6, Pallas kernels, call(): pl.pallas_call(kernel, name=name, out_shape=[jax.ShapeDtypeStruct(shape,...  36.4 us
    all_to_all x2, starting transfers between devices, swap(): return lax.all_to_all(blocks, axis, split_axis=0, concat_axis=0, tiled=True)  23.1 us
    all_gather x1, waiting for transfers between devices, local(): cotangent_all = lax.all_gather(cotangent[0], 'seq', axis=0, tiled=True)  5.79 us
    unnamed x14, local copies, waits for them, and re-layouts  5.77 us
  transfers between devices with their start and end apart: 4, of which 3 were waited for; matrix products, arithmetic and copies ran while one was open for 4% of the time, Pallas kernels for 16%

profile of v1, /device:TPU:1, one launch (start us, length us, event | category | flops | bytes accessed | tf_op | source)
XLA Modules:
  0.0 229.4 jit_solution(14173632607248448373)
XLA Ops:
  7.2 0.0 copy-start
  7.2 0.0 all-gather.6.cloned.1.call-start
  7.2 0.7 all-gather.6.cloned.1.call-update
  7.9 1.7 copy.19
  9.6 0.0 copy-start.3
  9.6 0.1 copy.20
  9.7 0.6 copy-done.3
  10.3 1.1 pad_maximum_fusion
  11.5 0.0 copy-start.4
  11.5 10.5 %all-to-all-start = ((bf16[16,304,128]{2,1,0:T(8,128)(2,1)}), bf16[16,304,128]{2,1,0:T(8,128)(2,1)S(1)}, u32[]{:S(2)}, u32[]{:S(2)}) async-start(bf16[16,304,128]{2,1,0:T(8,128)(2,1)} %pad_maximum_fusion), calls=%async_computation | async-start | bytes 2490368 | tf_op jit(solution)/shard_map/all_to_all | solution.py:415
  22.0 0.0 all-gather.4.cloned.1.call-start
  22.0 0.0 copy-done
  22.1 0.1 constant_dynamic-slice_fusion
  22.1 0.1 copy.29
  22.2 0.0 copy-done.4
  22.2 0.1 dynamic_slice.10
  22.3 0.1 broadcast_in_dim.16
  22.4 0.6 broadcast_in_dim_reshape.10.refs_2_
  23.0 0.6 pad.9.refs_1_
  23.6 39.0 %all-to-all-done.refs_0_ = bf16[16,304,128]{2,1,0:T(8,128)(2,1)S(1)} async-done(((bf16[16,304,128]{2,1,0:T(8,128)(2,1)}), bf16[16,304,128]{2,1,0:T(8,128)(2,1)S(1)}, u32[]{:S(2)}, u32[]{:S(2)}) %all-to-all-start) | async-done | bytes 1245216 | tf_op jit(solution)/shard_map/all_to_all | solution.py:415
  62.6 0.0 copy-start.1
  62.6 1.1 copy-done.1
  63.7 8.2 %forward.1 = (f32[96,2048]{1,0:T(8,128)}, f32[8,2048]{1,0:T(8,128)}, bf16[384,768]{1,0:T(8,128)(2,1)}, bf16[96,2048]{1,0:T(8,128)(2,1)}, bf16[96,1152]{1,0:T(8,128)(2,1)}) custom-call(bf16[16,304,128]{2,1,0:T(8,128)(2,1)} %copy-done.1, f32[96,16]{1,0:T(8,128)} %pad.9.refs_1_, s32[1,96]{1,0:T(1,128)} %broadcast_in_dim_reshape.10.refs_2_, bf16[96,1152]{1,0:T(8,128)(2,1)} %refs_2_.1), custom_call_target="tpu_custom_call" | custom-call | tf_op jit(solution)/shard_map/forward/pallas_call | solution.py:404
  71.9 0.0 all-gather.4.cloned.1.call-update
  71.9 0.8 dynamic-slice_bitcast_fusion
  72.7 0.7 copy.22.refs_4_
  73.4 5.8 %all-gather.6.cloned.1.call-done = bf16[1,2048,1152]{2,1,0:T(8,128)(2,1)} async-done(((bf16[1,128,1152]{2,1,0:T(8,128)(2,1)}), bf16[1,2048,1152]{2,1,0:T(8,128)(2,1)}) %all-gather.6.cloned.1.call-update) | async-done | bytes 4718608 | tf_op jit(solution)/shard_map/all_gather | solution.py:427
  79.2 5.1 %sums.1 = (f32[96,2048]{1,0:T(8,128)}, f32[16,32,128]{2,1,0:T(8,128)}) custom-call(f32[96,2048]{1,0:T(8,128)} %get-tuple-element.20.refs_0_.refs_4_, f32[8,2048]{1,0:T(8,128)} %get-tuple-element.21.refs_1_.refs_5_, bf16[96,1152]{1,0:T(8,128)(2,1)} %refs_2_.1, bf16[2048,1152]{1,0:T(8,128)(2,1)} %bitcast.28, f32[96,1]{1,0:T(8,128)} %copy.22.refs_4_), custom_call_target="tpu_custom_call" | custom-call | tf_op jit(solution)/shard_map/sums/pallas_call | solution.py:404
  84.4 16.5 %all_to_all.25.refs_3_ = f32[16,32,128]{2,1,0:T(8,128)} all-to-all(f32[16,32,128]{2,1,0:T(8,128)} %get-tuple-element.23), channel_id=1, replica_groups=mesh['dp'=32,'seq'=16] {'seq'}, dimensions={0} | all-to-all | bytes 524288 | tf_op jit(solution)/shard_map/all_to_all | solution.py:415
  100.9 4.9 %normed.1 = (bf16[16,96,128]{2,1,0:T(8,128)(2,1)}, f32[96,2048]{1,0:T(8,128)}, f32[1024,128]{1,0:T(8,128)}, f32[96,128]{1,0:T(8,128)}) custom-call(f32[96,2048]{1,0:T(8,128)} %get-tuple-element.20.refs_0_.refs_4_, f32[8,2048]{1,0:T(8,128)} %get-tuple-element.21.refs_1_.refs_5_, f32[96,2048]{1,0:T(8,128)} %get-tuple-element.22.refs_2_, ...), custom_call_target="tpu_custom_call" | custom-call | tf_op jit(solution)/shard_map/normed/pallas_call | solution.py:404
  105.8 12.6 %all-to-all-start.2 = ((f32[32,32,128]{2,1,0:T(8,128)}), f32[32,32,128]{2,1,0:T(8,128)S(1)}, u32[]{:S(2)}, u32[]{:S(2)}) async-start(f32[32,32,128]{2,1,0:T(8,128)} %bitcast.36), calls=%async_computation.2 | async-start | bytes 1048576 | tf_op jit(solution)/shard_map/all_to_all | solution.py:415
  118.4 0.7 broadcast_in_dim_reshape.13.refs_3_
  119.1 14.3 %backward.1 = (bf16[16,400,128]{2,1,0:T(8,128)(2,1)}, f32[16,128]{1,0:T(8,128)}) custom-call(bf16[16,304,128]{2,1,0:T(8,128)(2,1)} %copy-done.1, f32[96,16]{1,0:T(8,128)} %pad.9.refs_1_, s32[1,96]{1,0:T(1,128)} %broadcast_in_dim_reshape.10.refs_2_, s32[96,1]{1,0:T(8,128)} %broadcast_in_dim_reshape.13.refs_3_, f32[96,2048]{1,0:T(8,128)} %get-tuple-element.20.refs_0_.refs_4_, ...), custom_call_target="tpu_custom_call" | custom-call | tf_op jit(solution)/shard_map/backward/pallas_call | solution.py:404
  133.4 1.7 all-to-all-done.2.parts_ref
  135.1 0.0 copy-start.2
  135.1 0.8 copy-done.2
  135.9 2.0 pack_sum.1
  137.9 28.1 %all_to_all.26.gathered_ref = f32[32,48,128]{2,1,0:T(8,128)} all-to-all(f32[32,48,128]{2,1,0:T(8,128)} %pack_sum.1), channel_id=1, replica_groups=mesh['dp'=32,'seq'=16] {'dp'}, dimensions={0} | all-to-all | bytes 1572864 | tf_op jit(solution)/shard_map/all_to_all | solution.py:415
  166.0 2.0 unpack.1
  168.0 48.0 %all_to_all.27 = bf16[16,400,128]{2,1,0:T(8,128)(2,1)S(1)} all-to-all(bf16[16,400,128]{2,1,0:T(8,128)(2,1)} %get-tuple-element.32), channel_id=1, replica_groups=mesh['dp'=32,'seq'=16] {'seq'}, dimensions={0} | all-to-all | bytes 3276800 | tf_op jit(solution)/shard_map/all_to_all | solution.py:415
  216.0 0.1 slice.26
  216.1 0.1 copy.25
  216.2 1.4 copy.27
  217.6 0.7 slice.24
  218.4 0.7 squeeze.12
  219.1 0.0 all-gather.4.cloned.1.call-done
  219.1 3.4 %fusion = bf16[1,128,1152]{2,1,0:T(8,128)(2,1)} fusion(bf16[1536,128]{1,0:T(8,128)(2,1)S(1)} %bitcast.34, bf16[1536,1152]{1,0:T(8,128)(2,1)} %all-gather.4.cloned.1.call-done), kind=kOutput, calls=%fused_computation.1 | convolution fusion | flops 453132288 | bytes 4227072 | tf_op jit(solution)/shard_map/dot_general | solution.py:504
  (8 shorter events, 0.1 us)
Async XLA Ops:
  7.2 14.9 %copy-start = (f32[9,1536]{1,0:T(8,128)S(1)}, f32[9,1536]{1,0:T(8,128)}, u32[]{:S(2)}) copy-start(f32[9,1536]{1,0:T(8,128)} %param.11) | copy-start | bytes 165892
  7.2 72.0 %all-gather.6.cloned.1.call-start = ((), (), s32[]{:S(2)}) async-start(), calls=%async_computation.6 | async-start | bytes 5013504 | tf_op jit(solution)/shard_map/all_gather | solution.py:427
  9.6 0.7 copy-start.3
  11.5 10.7 %copy-start.4 = (s32[48]{0:T(128)S(1)}, s32[48]{0:T(128)}, u32[]{:S(2)}) copy-start(s32[48]{0:T(128)} %param.12) | copy-start | bytes 580
  11.5 51.1 %all-to-all-start = ((bf16[16,304,128]{2,1,0:T(8,128)(2,1)}), bf16[16,304,128]{2,1,0:T(8,128)(2,1)S(1)}, u32[]{:S(2)}, u32[]{:S(2)}) async-start(bf16[16,304,128]{2,1,0:T(8,128)(2,1)} %pad_maximum_fusion), calls=%async_computation | async-start | bytes 2490368 | tf_op jit(solution)/shard_map/all_to_all | solution.py:415
  22.0 197.1 %all-gather.4.cloned.1.call-start = ((), (), s32[]{:S(2)}) async-start(), calls=%async_computation.5 | async-start | bytes 3760128 | tf_op jit(solution)/shard_map/all_gather | solution.py:452
  62.6 1.1 copy-start.1
  105.8 29.4 %all-to-all-start.2 = ((f32[32,32,128]{2,1,0:T(8,128)}), f32[32,32,128]{2,1,0:T(8,128)S(1)}, u32[]{:S(2)}, u32[]{:S(2)}) async-start(f32[32,32,128]{2,1,0:T(8,128)} %bitcast.36), calls=%async_computation.2 | async-start | bytes 1048576 | tf_op jit(solution)/shard_map/all_to_all | solution.py:415
  135.1 0.8 copy-start.2
Sparse Core Ops, SparseCore 0:
  10.1 69.0 all-gather.5
  81.3 44.5 all-gather.3

commit v2 on v1

--- a/solution.py
+++ b/solution.py
@@ -11,6 +11,8 @@
 FEAT = 256
 LANES = 128
 CHUNK = 256
+VMEM = 24 * 1024 * 1024
+ALL_VMEM = 60 * 1024 * 1024
 WIDTHS = (16, 32, 48, 64)
 
 feature_floor = 0.1
@@ -162,8 +164,28 @@
     return jnp.where(row < count, 1.0, 0.0)
 
 
+def prepare_kernel(projected_ref, packing_ref, out_ref):
+    groups = out_ref.shape[0]
+    parts, tokens, width_all = projected_ref.shape
+    width = width_all // groups
+    for part in range(parts):
+        turned = jnp.transpose(projected_ref[part])
+        for g in range(groups):
+            out_ref[g, pl.ds(part * width, width), :] = turned[g * width : (g + 1) * width]
+    rows = packing_ref[...].astype(f32).astype(bf16)
+    for g in range(groups):
+        out_ref[g, pl.ds(parts * width, 16), :] = rows
+
+
+def finish_kernel(normed_ref, grad_ref, weight_ref, block_ref, grad_out):
+    groups, width, tokens = normed_ref.shape
+    grad_out[0] = jnp.transpose(grad_ref[...].reshape(groups * width, tokens))
+    normed = jnp.transpose(normed_ref[...].reshape(groups * width, tokens))
+    block_ref[...] = dot(normed, weight_ref[...]).astype(bf16)
+
+
 def forward_kernel(heads, x_ref, taps_ref, seed_row_ref, weight_ref,
-                   numer_ref, denom_ref, states_ref, conv_ref, weight_out):
+                   numer_ref, denom_ref, attention_ref, squares_ref, states_ref, conv_ref, weight_out):
     width = heads * HEAD
     chunks = x_ref.shape[0] * LANES // CHUNK
     middle = chunks // 2
@@ -201,6 +223,7 @@
         axis=0,
     )
     states_ref[...] = states
+    squares = []
     for j in range(chunks):
         lanes = pl.ds(j * CHUNK, CHUNK)
         image = grid.image[:, j * CHUNK : (j + 1) * CHUNK]
@@ -208,70 +231,85 @@
         both = pick_image(states, feat_query, image, j, middle, width + 8)
         numer_ref[:, lanes] = both[:width]
         denom_ref[:, lanes] = both[width : width + 8]
-
-
-def sums_kernel(heads, numer_ref, denom_ref, weight_ref, cotangent_ref, gain_ref,
-                grad_normed_ref, sums_ref):
-    chunks = numer_ref.shape[1] // CHUNK
+        attention = (both[:width] / by_head(both[width : width + 8], heads)).astype(bf16)
+        attention_ref[:, lanes] = attention
+        attention = attention.astype(f32)
+        squares.append(jnp.sum(attention * attention, axis=0, keepdims=True))
+    to_peers(squares, squares_ref)
+
+
+def to_peers(sums, out_ref):
+    rows = [
+        total[:, part * LANES : (part + 1) * LANES]
+        for total in sums
+        for part in range(CHUNK // LANES)
+    ]
+    rows = jnp.concatenate(rows, axis=0).astype(bf16)
+    for peer in range(out_ref.shape[0]):
+        out_ref[peer] = rows
+
+
+def tokens_of(values, j):
+    return jnp.concatenate([values[2 * j : 2 * j + 1], values[2 * j + 1 : 2 * j + 2]], axis=1)
+
+
+def inner_kernel(attention_ref, weight_ref, cotangent_ref, gain_ref, grad_normed_ref, inner_ref,
+                 rows_ref):
+    step = pl.program_id(0)
+    chunks = attention_ref.shape[1] // CHUNK
     weight, gain = weight_ref[...], gain_ref[...]
-    squares, inner = [], []
+    rows = []
     for j in range(chunks):
         lanes = pl.ds(j * CHUNK, CHUNK)
         grad_normed = dot_nt(weight, cotangent_ref[pl.ds(j * CHUNK, CHUNK), :])
         grad_normed_ref[:, lanes] = grad_normed
-        attention = (numer_ref[:, lanes] / by_head(denom_ref[:, lanes], heads)).astype(bf16)
-        attention = attention.astype(f32)
-        square = jnp.sum(attention * attention, axis=0, keepdims=True)
-        product = jnp.sum(gain * grad_normed * attention, axis=0, keepdims=True)
+        attention = attention_ref[:, lanes].astype(f32)
+        inner = jnp.sum(gain * grad_normed * attention, axis=0, keepdims=True)
         for part in range(CHUNK // LANES):
-            here = slice(part * LANES, (part + 1) * LANES)
-            squares.append(square[:, here])
-            inner.append(product[:, here])
-    both = jnp.concatenate(squares + inner, axis=0)
-    for peer in range(sums_ref.shape[0]):
-        sums_ref[peer] = both
-
-
-def normed_kernel(heads, numer_ref, denom_ref, grad_normed_ref, sums_ref, gain_ref, cotangent_ref,
-                  normed_ref, grad_ref, weight_ref, gain_out):
-    chunks = numer_ref.shape[1] // CHUNK
-    groups = sums_ref.shape[0]
-    width = heads * HEAD
+            rows.append(inner[:, part * LANES : (part + 1) * LANES])
+    rows_ref[pl.ds(pl.multiple_of(step * 8, 8), 8), :] = jnp.concatenate(rows, axis=0)
+
+    @pl.when(step == pl.num_programs(0) - 1)
+    def _():
+        rows = rows_ref[...].astype(bf16)
+        for peer in range(inner_ref.shape[0]):
+            inner_ref[peer] = rows
+
+
+def normed_kernel(attention_ref, grad_normed_ref, squares_ref, gain_ref, cotangent_ref,
+                  normed_ref, inverse_ref, weight_ref, gain_out):
+    width, tokens = attention_ref.shape
+    chunks = tokens // CHUNK
+    groups = squares_ref.shape[0]
     gain = gain_ref[...]
-    sums = jnp.sum(sums_ref[...], axis=0)
-    inverse = lax.rsqrt(sums[:groups] * (1.0 / (width * groups)) + epsilon)
-    inner = inverse * inverse * inverse * sums[groups:] * (1.0 / (width * groups))
+    squares = jnp.sum(squares_ref[...].astype(f32), axis=0)
+    inverse = lax.rsqrt(squares * (1.0 / (width * groups)) + epsilon)
+    inverse_ref[...] = inverse
     weight = gain_sum = None
     for j in range(chunks):
         lanes = pl.ds(j * CHUNK, CHUNK)
-
-        def tokens(values):
-            return jnp.concatenate([values[2 * j : 2 * j + 1], values[2 * j + 1 : 2 * j + 2]], axis=1)
-
-        inv_rms, away = tokens(inverse), tokens(inner)
-        grad_normed = grad_normed_ref[:, lanes]
-        attention = (numer_ref[:, lanes] / by_head(denom_ref[:, lanes], heads)).astype(bf16)
-        attention = attention.astype(f32)
+        inv_rms = tokens_of(inverse, j)
+        attention = attention_ref[:, lanes].astype(f32)
         normed = (attention * gain * inv_rms).astype(bf16)
-        grad_ref[:, lanes] = inv_rms * gain * grad_normed - attention * away
-        gain_sum = add(gain_sum, grad_normed * attention * inv_rms)
+        gain_sum = add(gain_sum, grad_normed_ref[:, lanes] * attention * inv_rms)
         for part in range(CHUNK // LANES):
             normed_ref[2 * j + part] = normed[:, part * LANES : (part + 1) * LANES]
         weight = add(weight, dot(normed, cotangent_ref[pl.ds(j * CHUNK, CHUNK), :]))
     gain_out[...] = jnp.broadcast_to(jnp.sum(gain_sum, axis=1, keepdims=True), gain_out.shape)
     across = weight.shape[1] // LANES
-    for r in range(width // 8):
+    weight = weight.astype(bf16)
+    for r in range(width // 16):
         for c in range(across):
-            weight_ref[pl.ds((r * across + c) * 8, 8), :] = weight[
-                r * 8 : (r + 1) * 8, c * LANES : (c + 1) * LANES
+            weight_ref[pl.ds((r * across + c) * 16, 16), :] = weight[
+                r * 16 : (r + 1) * 16, c * LANES : (c + 1) * LANES
             ]
     used = width * across
-    weight_ref[used:, :] = jnp.zeros((weight_ref.shape[0] - used, LANES), f32)
+    weight_ref[used:, :] = jnp.zeros((weight_ref.shape[0] - used, LANES), bf16)
 
 
 def backward_kernel(heads, x_ref, taps_ref, seed_row_ref, seed_column_ref, numer_ref, denom_ref,
-                    states_ref, conv_ref, normed_ref, grad_ref, gain_ref,
-                    out_ref, small_ref, grad_conv_ref):
+                    states_ref, conv_ref, normed_ref, attention_ref, grad_normed_ref,
+                    inverse_ref, inner_ref, norm_gain_ref, gain_ref, out_ref, small_ref, grad_conv_ref):
     width = heads * HEAD
     chunks = x_ref.shape[0] * LANES // CHUNK
     middle = chunks // 2
@@ -281,6 +319,10 @@
     states = jnp.transpose(states_ref[...].astype(f32)).astype(bf16)
     mask = head_mask(heads)
     front = back = None
+    norm_gain = norm_gain_ref[...]
+    inverse = inverse_ref[...]
+    away = jnp.sum(inner_ref[...].astype(f32), axis=0) * (1.0 / (width * x_ref.shape[0]))
+    away = inverse * inverse * inverse * away
 
     def put(part, j, values):
         for half in range(CHUNK // LANES):
@@ -301,7 +343,9 @@
         image = grid.image[:, j * CHUNK : (j + 1) * CHUNK]
         pre = dot(omega, chunk_of(x_ref, 0, width, j)) * scale
         feat_query = features(pre)
-        grad = grad_ref[:, lanes].astype(bf16).astype(f32)
+        grad = tokens_of(inverse, j) * norm_gain * grad_normed_ref[:, lanes]
+        grad = grad - attention_ref[:, lanes].astype(f32) * tokens_of(away, j)
+        grad = grad.astype(bf16).astype(f32)
         denom = denom_ref[:, lanes]
         grad_numer = (grad / by_head(denom, heads)).astype(bf16).astype(f32)
         dots = head_sums(grad * numer_ref[:, lanes], heads)
@@ -377,36 +421,39 @@
 def pack_sum_kernel(parts_ref, small_ref, out_ref):
     packs = parts_ref.shape[0]
     rows = parts_ref.shape[1]
-    total = jnp.sum(parts_ref[...], axis=0) * (1.0 / packs)
-    small = small_ref[...]
+    total = (jnp.sum(parts_ref[...].astype(f32), axis=0) * (1.0 / packs)).astype(bf16)
+    small = small_ref[...].astype(bf16)
     for peer in range(packs):
         out_ref[peer, pl.ds(0, rows), :] = total
         out_ref[peer, pl.ds(rows, 16), :] = small
 
 
-def unpack_kernel(gathered_ref, outgoing_ref, weight_ref, payload_ref):
+def small_kernel(gathered_ref, outgoing_ref, payload_ref):
     packs = gathered_ref.shape[0]
+    small = jnp.sum(gathered_ref[...].astype(f32), axis=0) * (1.0 / packs)
+    for peer in range(payload_ref.shape[0]):
+        payload_ref[peer] = small.astype(bf16)
+
+
+def unpack_kernel(gathered_ref, weight_ref):
     rows = gathered_ref.shape[1] - 16
     width, features_out = weight_ref.shape
     across = features_out // LANES
-    for r in range(width // 8):
+    for r in range(width // 16):
         for c in range(across):
-            start = (r * across + c) * 8
-            weight_ref[pl.ds(r * 8, 8), pl.ds(c * LANES, LANES)] = gathered_ref[
-                start // rows, pl.ds(start % rows, 8), :
-            ]
-    small = jnp.sum(gathered_ref[:, pl.ds(rows, 16), :], axis=0) * (1.0 / packs)
-    for peer in range(payload_ref.shape[0]):
-        payload_ref[peer] = small.astype(bf16)
-
-
-def call(kernel, name, out_shapes, operands, scratch=(), **more):
+            start = (r * across + c) * 16
+            weight_ref[pl.ds(r * 16, 16), pl.ds(c * LANES, LANES)] = gathered_ref[
+                start // rows, pl.ds(start % rows, 16), :
+            ].astype(f32)
+
+
+def call(kernel, name, out_shapes, operands, scratch=(), vmem=VMEM, **more):
     return pl.pallas_call(
         kernel,
         name=name,
         out_shape=[jax.ShapeDtypeStruct(shape, kind) for shape, kind in out_shapes],
         scratch_shapes=list(scratch),
-        compiler_params=pltpu.CompilerParams(vmem_limit_bytes=56 * 1024 * 1024),
+        compiler_params=pltpu.CompilerParams(vmem_limit_bytes=vmem),
         **more,
     )(*operands)
 
@@ -425,87 +472,117 @@
     heads = width // HEAD
     all_tokens = tokens * groups
     cotangent_all = lax.all_gather(cotangent[0], "seq", axis=0, tiled=True)
-    by_peer = projected[0].transpose(1, 2, 0).reshape(3, groups, width, tokens)
-    by_peer = by_peer.transpose(1, 0, 2, 3).reshape(groups, 3 * width, tokens)
-    rows = jnp.pad(packing[0].astype(bf16), ((0, 11), (0, 0)))
-    outgoing = jnp.concatenate(
-        [by_peer, jnp.broadcast_to(rows[None], (groups, 16, tokens))], axis=1
-    )
+    outgoing = call(
+        prepare_kernel,
+        "prepare",
+        [((groups, 3 * width + 16, tokens), bf16)],
+        (projected[0].transpose(1, 0, 2), jnp.pad(packing[0], ((0, 11), (0, 0)))),
+    )[0]
     seeds = jnp.repeat(lax.dynamic_slice_in_dim(feature_seeds, member * heads, heads, 0), HEAD)
     taps = jnp.pad(
         lax.dynamic_slice_in_dim(conv_taps, member * width, width, 1).T, ((0, 0), (0, 7))
     )
     gain = lax.dynamic_slice_in_dim(norm_gain, member * width, width, 0)[:, None]
     x = swap(outgoing, "seq")
-    numer, denom, states, conv, weight_local = call(
+    numer, denom, attention, squares, states, conv, weight_local = call(
         lambda *refs: forward_kernel(heads, *refs),
         "forward",
         [
             ((width, all_tokens), f32),
             ((8, all_tokens), f32),
+            ((width, all_tokens), bf16),
+            ((groups, groups, LANES), bf16),
             ((3 * LANES, heads * FEAT), bf16),
             ((width, all_tokens), bf16),
             ((width, features_out), bf16),
         ],
         (x, taps, seeds[None], out_weight),
     )
+    squares = swap(squares, "seq")
     weight_all = lax.all_gather(weight_local, "seq", axis=0, tiled=True)
-    grad_normed, sums = call(
-        lambda *refs: sums_kernel(heads, *refs),
-        "sums",
-        [((width, all_tokens), f32), ((groups, 2 * groups, LANES), f32)],
-        (numer, denom, out_weight, cotangent_all, gain),
-    )
-    sums = swap(sums, "seq")
-    normed, grad, weight_tiles, gain_part = call(
-        lambda *refs: normed_kernel(heads, *refs),
+    grad_normed, inner = call(
+        inner_kernel,
+        "inner",
+        [((width, all_tokens), f32), ((groups, groups, LANES), bf16)],
+        (attention, out_weight, cotangent_all, gain),
+        vmem=ALL_VMEM,
+        grid=(groups // 8,),
+        in_specs=[
+            pl.BlockSpec((width, 8 * LANES), lambda i: (0, i)),
+            pl.BlockSpec((width, features_out), lambda i: (0, 0)),
+            pl.BlockSpec((8 * LANES, features_out), lambda i: (i, 0)),
+            pl.BlockSpec((width, 1), lambda i: (0, 0)),
+        ],
+        out_specs=[
+            pl.BlockSpec((width, 8 * LANES), lambda i: (0, i)),
+            pl.BlockSpec((groups, groups, LANES), lambda i: (0, 0, 0)),
+        ],
+        scratch=[pltpu.VMEM((groups, LANES), f32)],
+    )
+    inner = swap(inner, "seq")
+    normed, inverse, weight_tiles, gain_part = call(
+        normed_kernel,
         "normed",
         [
             ((groups, width, LANES), bf16),
-            ((width, all_tokens), f32),
-            ((1024, LANES), f32),
+            ((groups, LANES), f32),
+            ((1024, LANES), bf16),
             ((width, LANES), f32),
         ],
-        (numer, denom, grad_normed, sums, gain, cotangent_all),
+        (attention, grad_normed, squares, gain, cotangent_all),
     )
     weight_parts = swap(weight_tiles.reshape(packs, 1024 // packs, LANES), "dp")
     leaving, small = call(
         lambda *refs: backward_kernel(heads, *refs),
         "backward",
         [((groups, 4 * width + 16, LANES), bf16), ((16, LANES), f32)],
-        (x, taps, seeds[None], seeds[:, None], numer, denom, states, conv, normed, grad, gain_part),
+        (x, taps, seeds[None], seeds[:, None], numer, denom, states, conv, normed, attention,
+         grad_normed, inverse, inner, gain, gain_part),
         scratch=[pltpu.VMEM((width, all_tokens), f32)],
     )
     shared = call(
         pack_sum_kernel,
         "pack_sum",
-        [((packs, 1024 // packs + 16, LANES), f32)],
+        [((packs, 1024 // packs + 16, LANES), bf16)],
         (weight_parts, small),
     )[0]
     gathered = swap(shared, "dp")
-    weight_grad, leaving = call(
-        unpack_kernel,
-        "unpack",
-        [((width, features_out), f32), (leaving.shape, bf16)],
+    leaving = call(
+        small_kernel,
+        "small",
+        [(leaving.shape, bf16)],
         (gathered, leaving),
         grid=(1,),
         in_specs=[
-            pl.BlockSpec(gathered.shape, lambda i: (0, 0, 0)),
+            pl.BlockSpec((packs, 16, LANES), lambda i: (0, 1024 // packs // 16, 0)),
             pl.BlockSpec(memory_space=pl.ANY),
         ],
+        out_specs=[pl.BlockSpec((groups, 16, LANES), lambda i: (0, 4 * width // 16, 0))],
+        input_output_aliases={1: 0},
+    )[0]
+    weight_grad = call(
+        unpack_kernel, "unpack", [((width, features_out), f32)], (gathered,)
+    )[0]
+    back = swap(leaving, "seq")
+    across = features_out // 3
+    block_out, grads = call(
+        finish_kernel,
+        "finish",
+        [((tokens, features_out), bf16), ((3, tokens, width_all), bf16)],
+        (back, back, weight_all),
+        vmem=ALL_VMEM,
+        grid=(3,),
+        in_specs=[
+            pl.BlockSpec((groups, width, tokens), lambda i: (0, 0, 0)),
+            pl.BlockSpec((groups, width, tokens), lambda i: (0, i + 1, 0)),
+            pl.BlockSpec((width_all, across), lambda i: (0, i)),
+        ],
         out_specs=[
-            pl.BlockSpec((width, features_out), lambda i: (0, 0)),
-            pl.BlockSpec((groups, 16, LANES), lambda i: (0, 4 * width // 16, 0)),
-        ],
-        input_output_aliases={1: 1},
-    )
-    back = swap(leaving, "seq")
-    normed_rows = back[:, :width].reshape(width_all, tokens)
-    block_out = lax.dot_general(
-        normed_rows, weight_all, (((0,), (0,)), ((), ())), preferred_element_type=f32
-    ).astype(bf16)
-    grads = back[:, width : 4 * width].reshape(groups, 3, width, tokens)
-    grad_tokens = grads.transpose(3, 1, 0, 2).reshape(tokens, 3, width_all)
+            pl.BlockSpec((tokens, across), lambda i: (0, i)),
+            pl.BlockSpec((1, tokens, width_all), lambda i: (i, 0, 0)),
+        ],
+    )
+    grad_tokens = grads.transpose(1, 0, 2)
     small_all = back[:, 4 * width : 4 * width + 10, :width].astype(f32)
     small_all = small_all.transpose(1, 0, 2).reshape(10, width_all)
     return block_out[None], grad_tokens[None], weight_grad, small_all[9], small_all[:9]

time: 230 us -> 214 us (0.930)
  blocking collectives: 92.6 us -> 20.6 us
  waiting for transfers between devices: 47.2 us -> 82.7 us
  starting transfers between devices: 23.2 us -> 43.5 us
  local copies, waits for them, and re-layouts: 11.2 us -> 20.4 us
  Pallas kernels: 36.4 us -> 31.6 us
  matrix products: 3.43 us -> 0 us
    all_to_all x3 -> x1, blocking collectives: 92.6 us -> 20.6 us  [swap(): return lax.all_to_all(blocks, axis, split_axis=0, concat_axis=0, tiled=True)]
    all_to_all x2 -> x5, waiting for transfers between devices: 40.7 us -> 81.3 us  [swap(): return lax.all_to_all(blocks, axis, split_axis=0, concat_axis=0, tiled=True)]
    all_to_all x2 -> x5, starting transfers between devices: 23.1 us -> 43.4 us  [swap(): return lax.all_to_all(blocks, axis, split_axis=0, concat_axis=0, tiled=True)]
    unnamed x14 -> x52, local copies, waits for them, and re-layouts: 5.77 us -> 16.2 us
    all_gather x1, waiting for transfers between devices: 5.79 us -> 0.72 us  [local(): cotangent_all = lax.all_gather(cotangent[0], 'seq', axis=0, tiled=True)]
    pallas_call x6 -> x9, Pallas kernels: 36.4 us -> 31.6 us  [call(): pl.pallas_call(kernel, name=name, out_shape=[jax.ShapeDtypeStruct(shape,...]
    dot_general x1 -> x0, matrix products: 3.43 us -> none  [local(): lax.dot_general(normed_rows, weight_all, (((0,), (0,)), ((), ())), prefer...]
  transfers between devices with their start and end apart: 4 -> 7, of which waited for: 3 -> 5; matrix products, arithmetic and copies ran while one was open for 4% -> 2% of each run, Pallas kernels for 16% -> 13%
where the time goes in v2:
time: 214 us; the launch traced here: 213 us
  waiting for transfers between devices  82.7 us (39%)
  starting transfers between devices  43.5 us (20%)
  Pallas kernels  31.6 us (15%)
  blocking collectives  20.6 us (10%)
  local copies, waits for them, and re-layouts  20.4 us (10%)
  between operations  14.2 us (7%)
    all_to_all x5, waiting for transfers between devices, swap(): return lax.all_to_all(blocks, axis, split_axis=0, concat_axis=0, tiled=True)  81.3 us
    all_to_all x5, starting transfers between devices, swap(): return lax.all_to_all(blocks, axis, split_axis=0, concat_axis=0, tiled=True)  43.4 us
    pallas_call x9, Pallas kernels, call(): pl.pallas_call(kernel, name=name, out_shape=[jax.ShapeDtypeStruct(shape,...  31.6 us
    all_to_all x1, blocking collectives, swap(): return lax.all_to_all(blocks, axis, split_axis=0, concat_axis=0, tiled=True)  20.6 us
    unnamed x52, local copies, waits for them, and re-layouts  16.2 us
  transfers between devices with their start and end apart: 7, of which 5 were waited for; matrix products, arithmetic and copies ran while one was open for 2% of the time, Pallas kernels for 13%

profile of v2, /device:TPU:1, one launch (start us, length us, event | category | flops | bytes accessed | tf_op | source)
XLA Modules:
  0.0 213.0 jit_solution(13091094098037626819)
XLA Ops:
  7.2 0.7 all-gather.6.cloned.1.call-update
  7.9 0.7 copy.27
  8.6 1.3 copy-done.6
  9.9 1.4 prepare.1
  11.3 10.5 %all-to-all-start = ((bf16[16,304,128]{2,1,0:T(8,128)(2,1)}), bf16[16,304,128]{2,1,0:T(8,128)(2,1)S(1)}, u32[]{:S(2)}, u32[]{:S(2)}) async-start(bf16[16,304,128]{2,1,0:T(8,128)(2,1)} %prepare.1), calls=%async_computation | async-start | bytes 2490368 | tf_op jit(solution)/shard_map/all_to_all | solution.py:462
  21.9 0.1 constant_dynamic-slice_fusion
  22.0 0.1 copy.25
  22.1 0.1 dynamic_slice.10
  22.1 0.1 broadcast_in_dim.12
  22.2 0.1 broadcast_in_dim_reshape.7.refs_2_
  22.3 39.9 %all-to-all-done.refs_0_ = bf16[16,304,128]{2,1,0:T(8,128)(2,1)S(1)} async-done(((bf16[16,304,128]{2,1,0:T(8,128)(2,1)}), bf16[16,304,128]{2,1,0:T(8,128)(2,1)S(1)}, u32[]{:S(2)}, u32[]{:S(2)}) %all-to-all-start) | async-done | bytes 1245216 | tf_op jit(solution)/shard_map/all_to_all | solution.py:462
  62.2 6.4 %forward.1 = (f32[96,2048]{1,0:T(8,128)S(1)}, f32[8,2048]{1,0:T(8,128)S(1)}, bf16[96,2048]{1,0:T(8,128)(2,1)S(1)}, bf16[16,16,128]{2,1,0:T(8,128)(2,1)}, bf16[38...) custom-call(bf16[16,304,128]{2,1,0:T(8,128)(2,1)S(1)} %all-to-all-done.refs_0_, ...), custom_call_target="tpu_custom_call" | custom-call | tf_op jit(solution)/shard_map/forward/pallas_call | solution.py:451
  68.6 0.7 copy-done.2
  69.3 0.9 copy-done.9
  70.3 0.6 copy-done.17
  70.9 5.9 %all-to-all-start.1 = ((bf16[16,16,128]{2,1,0:T(8,128)(2,1)}), bf16[16,16,128]{2,1,0:T(8,128)(2,1)S(1)}, u32[]{:S(2)}, u32[]{:S(2)}) async-start(bf16[16,16,128]{2,1,0:T(8,128)(2,1)} %get-tuple-element.24), calls=%async_computation.1 | async-start | bytes 131072 | tf_op jit(solution)/shard_map/all_to_all | solution.py:462
  76.8 0.8 dynamic-slice_bitcast_fusion
  77.6 0.7 copy.19.gain_ref.refs_13_
  78.3 0.7 all-gather.6.cloned.1.call-done
  79.0 4.4 %inner.1 = (f32[96,2048]{1,0:T(8,128)}, bf16[16,16,128]{2,1,0:T(8,128)(2,1)}) custom-call(bf16[96,2048]{1,0:T(8,128)(2,1)} %copy-done.2, bf16[96,1152]{1,0:T(8,128)(2,1)} %weight_ref.1, bf16[2048,1152]{1,0:T(8,128)(2,1)} %bitcast.18, f32[96,1]{1,0:T(8,128)} %copy.19.gain_ref.refs_13_), custom_call_target="tpu_custom_call" | custom-call | tf_op jit(solution)/shard_map/inner/pallas_call | solution.py:451
  83.4 1.2 all-to-all-done.1.squares_ref
  84.6 5.3 %all-to-all-start.3 = ((bf16[16,16,128]{2,1,0:T(8,128)(2,1)}), bf16[16,16,128]{2,1,0:T(8,128)(2,1)S(1)}, u32[]{:S(2)}, u32[]{:S(2)}) async-start(bf16[16,16,128]{2,1,0:T(8,128)(2,1)} %get-tuple-element.32), calls=%async_computation.3 | async-start | bytes 131072 | tf_op jit(solution)/shard_map/all_to_all | solution.py:462
  89.9 2.3 %copy-done.1 = bf16[1,2048,1152]{2,1,0:T(8,128)(2,1)S(1)} copy-done((bf16[1,2048,1152]{2,1,0:T(8,128)(2,1)S(1)}, bf16[1,2048,1152]{2,1,0:T(8,128)(2,1)}, u32[]{:S(2)}) %copy-start.1) | copy-done | bytes 4718616
  92.3 1.1 copy-done.4
  93.4 1.0 normed.1
  94.4 0.7 copy-done.13
  95.1 0.7 copy-done.15
  95.8 0.6 copy-done.19
  96.5 1.3 all-to-all-done.3.refs_12_
  97.7 12.8 %all-to-all-start.2 = ((bf16[32,32,128]{2,1,0:T(8,128)(2,1)}), bf16[32,32,128]{2,1,0:T(8,128)(2,1)S(1)}, u32[]{:S(2)}, u32[]{:S(2)}) async-start(bf16[32,32,128]{2,1,0:T(8,128)(2,1)} %bitcast.21), calls=%async_computation.2 | async-start | bytes 524288 | tf_op jit(solution)/shard_map/all_to_all | solution.py:462
  110.5 0.7 broadcast_in_dim_reshape.9.refs_3_
  111.3 1.2 copy-done.10
  112.4 1.0 copy-done.12
  113.4 1.0 copy-done.14
  114.4 0.8 copy-done.16
  115.2 0.8 copy-done.18
  116.1 0.8 copy-done.20
  116.9 0.7 copy-done.22
  117.5 12.1 %backward.1 = (bf16[16,400,128]{2,1,0:T(8,128)(2,1)}, f32[16,128]{1,0:T(8,128)S(1)}) custom-call(bf16[16,304,128]{2,1,0:T(8,128)(2,1)S(1)} %all-to-all-done.refs_0_, f32[96,16]{1,0:T(8,128)S(1)} %pad.9.refs_1_, s32[1,96]{1,0:T(1,128)S(1)} %copy-done.22, s32[96,1]{1,0:T(8,128)S(1)} %copy-done.16, f32[96,2048]{1,0:T(8,128)S(1)} %copy-done.10, ...), custom_call_target="tpu_custom_call" | custom-call | tf_op jit(solution)/shard_map/backward/pallas_call | solution.py:451
  129.7 0.1 pack_sum.1
  129.7 20.6 %all_to_all.30.gathered_ref = bf16[32,48,128]{2,1,0:T(8,128)(2,1)S(1)} all-to-all(bf16[32,48,128]{2,1,0:T(8,128)(2,1)S(1)} %pack_sum.1), channel_id=1, replica_groups=mesh['dp'=32,'seq'=16] {'dp'}, dimensions={0} | all-to-all | bytes 786432 | tf_op jit(solution)/shard_map/all_to_all | solution.py:462
  150.3 0.7 small.1
  151.0 8.9 %all-to-all-start.5 = ((bf16[16,400,128]{2,1,0:T(8,128)(2,1)}), bf16[16,400,128]{2,1,0:T(8,128)(2,1)S(1)}, u32[]{:S(2)}, u32[]{:S(2)}) async-start(bf16[16,400,128]{2,1,0:T(8,128)(2,1)} %small.1), calls=%async_computation.5 | async-start | bytes 3276800 | tf_op jit(solution)/shard_map/all_to_all | solution.py:462
  159.9 0.8 unpack.1
  160.7 39.0 %all-to-all-done.5.normed_ref.grad_ref = bf16[16,400,128]{2,1,0:T(8,128)(2,1)S(1)} async-done(((bf16[16,400,128]{2,1,0:T(8,128)(2,1)}), bf16[16,400,128]{2,1,0:T(8,128)(2,1)S(1)}, u32[]{:S(2)}, u32[]{:S(2)}) %all-to-all-start.5) | async-done | bytes 1638432 | tf_op jit(solution)/shard_map/all_to_all | solution.py:462
  199.7 0.9 slice.16
  200.6 0.7 squeeze.15
  201.3 4.8 %finish.1 = (bf16[128,1152]{1,0:T(8,128)(2,1)}, bf16[3,128,1536]{2,1,0:T(8,128)(2,1)}) custom-call(bf16[16,400,128]{2,1,0:T(8,128)(2,1)} %copy-done.23, bf16[16,400,128]{2,1,0:T(8,128)(2,1)} %copy-done.23, bf16[1536,1152]{1,0:T(8,128)(2,1)} %all-gather.4.cloned.1.call-done.weight_ref), custom_call_target="tpu_custom_call" | custom-call | tf_op jit(solution)/shard_map/finish/pallas_call | solution.py:451
  (44 shorter events, 0.2 us)
Async XLA Ops:
  7.2 14.7 %copy-start = (f32[9,1536]{1,0:T(8,128)S(1)}, f32[9,1536]{1,0:T(8,128)}, u32[]{:S(2)}) copy-start(f32[9,1536]{1,0:T(8,128)} %param.11) | copy-start | bytes 165892
  7.2 71.8 %all-gather.6.cloned.1.call-start = ((), (), s32[]{:S(2)}) async-start(), calls=%async_computation.7 | async-start | bytes 5013504 | tf_op jit(solution)/shard_map/all_gather | solution.py:474
  8.6 1.3 copy-start.6
  11.3 10.8 %copy-start.24 = (s32[48]{0:T(128)S(1)}, s32[48]{0:T(128)}, u32[]{:S(2)}) copy-start(s32[48]{0:T(128)} %param.12) | copy-start | bytes 580
  11.3 50.9 %copy-start.7 = (bf16[96,1152]{1,0:T(8,128)(2,1)S(1)}, bf16[96,1152]{1,0:T(8,128)(2,1)}, u32[]{:S(2)}) copy-start(bf16[96,1152]{1,0:T(8,128)(2,1)} %weight_ref.1) | copy-start | bytes 663556
  11.3 50.9 %all-to-all-start = ((bf16[16,304,128]{2,1,0:T(8,128)(2,1)}), bf16[16,304,128]{2,1,0:T(8,128)(2,1)S(1)}, u32[]{:S(2)}, u32[]{:S(2)}) async-start(bf16[16,304,128]{2,1,0:T(8,128)(2,1)} %prepare.1), calls=%async_computation | async-start | bytes 2490368 | tf_op jit(solution)/shard_map/all_to_all | solution.py:462
  21.8 179.5 %all-gather.4.cloned.1.call-start = ((), (), s32[]{:S(2)}) async-start(), calls=%async_computation.6 | async-start | bytes 3760128 | tf_op jit(solution)/shard_map/all_gather | solution.py:502
  22.3 61.1 %copy-start.21 = (s32[1,96]{1,0:T(1,128)}, s32[1,96]{1,0:T(1,128)S(1)}, u32[]{:S(2)}) copy-start(s32[1,96]{1,0:T(1,128)S(1)} %broadcast_in_dim_reshape.7.refs_2_) | copy-start | bytes 1156
  68.6 0.7 copy-start.2
  69.3 0.9 copy-start.9
  70.3 0.6 copy-start.17
  70.9 8.1 %copy-start.11 = (bf16[96,2048]{1,0:T(8,128)(2,1)}, bf16[96,2048]{1,0:T(8,128)(2,1)S(1)}, u32[]{:S(2)}) copy-start(bf16[96,2048]{1,0:T(8,128)(2,1)S(1)} %get-tuple-element.29.refs_7_) | copy-start | bytes 1179652
  70.9 13.7 %all-to-all-start.1 = ((bf16[16,16,128]{2,1,0:T(8,128)(2,1)}), bf16[16,16,128]{2,1,0:T(8,128)(2,1)S(1)}, u32[]{:S(2)}, u32[]{:S(2)}) async-start(bf16[16,16,128]{2,1,0:T(8,128)(2,1)} %get-tuple-element.24), calls=%async_computation.1 | async-start | bytes 131072 | tf_op jit(solution)/shard_map/all_to_all | solution.py:462
  79.0 10.9 %copy-start.3 = (bf16[96,2048]{1,0:T(8,128)(2,1)S(1)}, bf16[96,2048]{1,0:T(8,128)(2,1)}, u32[]{:S(2)}) copy-start(bf16[96,2048]{1,0:T(8,128)(2,1)} %copy-done.2) | copy-start | bytes 1179652
  79.0 10.9 %copy-start.8 = (f32[96,1]{1,0:T(8,128)S(1)}, f32[96,1]{1,0:T(8,128)}, u32[]{:S(2)}) copy-start(f32[96,1]{1,0:T(8,128)} %copy.19.gain_ref.refs_13_) | copy-start | bytes 1156
  84.6 13.1 %all-to-all-start.3 = ((bf16[16,16,128]{2,1,0:T(8,128)(2,1)}), bf16[16,16,128]{2,1,0:T(8,128)(2,1)S(1)}, u32[]{:S(2)}, u32[]{:S(2)}) async-start(bf16[16,16,128]{2,1,0:T(8,128)(2,1)} %get-tuple-element.32), calls=%async_computation.3 | async-start | bytes 131072 | tf_op jit(solution)/shard_map/all_to_all | solution.py:462
  89.9 2.3 %copy-start.1 = (bf16[1,2048,1152]{2,1,0:T(8,128)(2,1)S(1)}, bf16[1,2048,1152]{2,1,0:T(8,128)(2,1)}, u32[]{:S(2)}) copy-start(bf16[1,2048,1152]{2,1,0:T(8,128)(2,1)} %all-gather.6.cloned.1.call-done) | copy-start | bytes 14155780
  92.3 1.1 copy-start.4
  93.4 17.9 %copy-start.5 = (f32[96,2048]{1,0:T(8,128)S(1)}, f32[96,2048]{1,0:T(8,128)}, u32[]{:S(2)}) copy-start(f32[96,2048]{1,0:T(8,128)} %get-tuple-element.23.grad_normed_ref.refs_10_) | copy-start | bytes 2359300
  94.4 0.8 copy-start.13
  95.1 0.7 copy-start.15
  95.8 0.6 copy-start.19
  97.7 31.9 %all-to-all-start.2 = ((bf16[32,32,128]{2,1,0:T(8,128)(2,1)}), bf16[32,32,128]{2,1,0:T(8,128)(2,1)S(1)}, u32[]{:S(2)}, u32[]{:S(2)}) async-start(bf16[32,32,128]{2,1,0:T(8,128)(2,1)} %bitcast.21), calls=%async_computation.2 | async-start | bytes 524288 | tf_op jit(solution)/shard_map/all_to_all | solution.py:462
  111.3 1.2 copy-start.10
  112.4 1.0 copy-start.12
  113.4 1.0 copy-start.14
  114.4 0.8 copy-start.16
  115.2 0.8 copy-start.18
  116.1 0.8 copy-start.20
  116.9 0.7 copy-start.22
  151.0 48.7 %all-to-all-start.5 = ((bf16[16,400,128]{2,1,0:T(8,128)(2,1)}), bf16[16,400,128]{2,1,0:T(8,128)(2,1)S(1)}, u32[]{:S(2)}, u32[]{:S(2)}) async-start(bf16[16,400,128]{2,1,0:T(8,128)(2,1)} %small.1), calls=%async_computation.5 | async-start | bytes 3276800 | tf_op jit(solution)/shard_map/all_to_all | solution.py:462
  199.6 1.7 copy-start.23
Sparse Core Ops, SparseCore 0:
  10.1 68.8 all-gather.5
  81.1 44.1 all-gather.3

commit v3 on v2

--- a/solution.py
+++ b/solution.py
@@ -177,11 +177,15 @@
         out_ref[g, pl.ds(parts * width, 16), :] = rows
 
 
-def finish_kernel(normed_ref, grad_ref, weight_ref, block_ref, grad_out):
+def finish_kernel(normed_ref, grad_ref, weight_ref, block_ref, grad_out, turned_ref):
     groups, width, tokens = normed_ref.shape
+
+    @pl.when(pl.program_id(0) == 0)
+    def _():
+        turned_ref[...] = jnp.transpose(normed_ref[...].reshape(groups * width, tokens))
+
     grad_out[0] = jnp.transpose(grad_ref[...].reshape(groups * width, tokens))
-    normed = jnp.transpose(normed_ref[...].reshape(groups * width, tokens))
-    block_ref[...] = dot(normed, weight_ref[...]).astype(bf16)
+    block_ref[...] = dot(turned_ref[...], weight_ref[...]).astype(bf16)
 
 
 def forward_kernel(heads, x_ref, taps_ref, seed_row_ref, weight_ref,
@@ -415,36 +419,59 @@
     for s in range(x_ref.shape[0]):
         out_ref[s, pl.ds(0, width), :] = normed_ref[s]
         out_ref[s, pl.ds(3 * width, width), :] = grad_values[:, s * LANES : (s + 1) * LANES]
-        out_ref[s, pl.ds(4 * width, 16), :] = jnp.zeros((16, LANES), bf16)
+
+
+def split_small(small, out_ref, start):
+    high = small.astype(bf16)
+    out_ref[pl.ds(start, 16), :] = high
+    out_ref[pl.ds(start + 16, 16), :] = (small - high.astype(f32)).astype(bf16)
+
+
+def whole_small(ref, start):
+    return ref[pl.ds(start, 16), :].astype(f32) + ref[pl.ds(start + 16, 16), :].astype(f32)
 
 
 def pack_sum_kernel(parts_ref, small_ref, out_ref):
-    packs = parts_ref.shape[0]
-    rows = parts_ref.shape[1]
-    total = (jnp.sum(parts_ref[...].astype(f32), axis=0) * (1.0 / packs)).astype(bf16)
-    small = small_ref[...].astype(bf16)
-    for peer in range(packs):
-        out_ref[peer, pl.ds(0, rows), :] = total
-        out_ref[peer, pl.ds(rows, 16), :] = small
-
-
-def small_kernel(gathered_ref, outgoing_ref, payload_ref):
-    packs = gathered_ref.shape[0]
-    small = jnp.sum(gathered_ref[...].astype(f32), axis=0) * (1.0 / packs)
-    for peer in range(payload_ref.shape[0]):
-        payload_ref[peer] = small.astype(bf16)
-
-
-def unpack_kernel(gathered_ref, weight_ref):
-    rows = gathered_ref.shape[1] - 16
+    packs, rows, _ = parts_ref.shape
+    total = jnp.sum(parts_ref[...].astype(f32), axis=0) * (1.0 / packs)
+    out_ref[pl.ds(0, rows), :] = total.astype(bf16)
+    split_small(small_ref[...] * (1.0 / packs), out_ref, rows)
+
+
+def join_kernel(own_ref, got_ref, out_ref):
+    rows = own_ref.shape[0] - 32
+    out_ref[pl.ds(0, rows), :] = own_ref[pl.ds(0, rows), :]
+    out_ref[pl.ds(rows, rows), :] = got_ref[pl.ds(0, rows), :]
+    split_small(whole_small(own_ref, rows) + whole_small(got_ref, rows), out_ref, 2 * rows)
+
+
+def unpack_kernel(packs, pack_ref, gathered_ref, weight_ref):
+    total = gathered_ref.shape[0] - 32
+    rows = total // packs
     width, features_out = weight_ref.shape
     across = features_out // LANES
     for r in range(width // 16):
         for c in range(across):
-            start = (r * across + c) * 16
+            block, row = divmod((r * across + c) * 16, rows)
+            place = pl.multiple_of((pack_ref[0] ^ block) * rows + row, 16)
             weight_ref[pl.ds(r * 16, 16), pl.ds(c * LANES, LANES)] = gathered_ref[
-                start // rows, pl.ds(start % rows, 16), :
+                pl.ds(place, 16), :
             ].astype(f32)
+
+
+def spread_kernel(gathered_ref, _, small_ref):
+    small = whole_small(gathered_ref, gathered_ref.shape[0] - 32)
+    for peer in range(small_ref.shape[0]):
+        small_ref[peer] = small
+
+
+def small_kernel(small_ref, taps_ref, gain_ref):
+    groups = small_ref.shape[0]
+    width = taps_ref.shape[1] // groups
+    for g in range(groups):
+        here = pl.ds(g * width, width)
+        taps_ref[:, here] = small_ref[g, pl.ds(0, 9), pl.ds(0, width)]
+        gain_ref[:, here] = small_ref[g, pl.ds(9, 1), pl.ds(0, width)]
 
 
 def call(kernel, name, out_shapes, operands, scratch=(), vmem=VMEM, **more):
@@ -530,40 +557,49 @@
             ((width, LANES), f32),
         ],
         (attention, grad_normed, squares, gain, cotangent_all),
+        vmem=ALL_VMEM,
     )
     weight_parts = swap(weight_tiles.reshape(packs, 1024 // packs, LANES), "dp")
     leaving, small = call(
         lambda *refs: backward_kernel(heads, *refs),
         "backward",
-        [((groups, 4 * width + 16, LANES), bf16), ((16, LANES), f32)],
+        [((groups, 4 * width, LANES), bf16), ((16, LANES), f32)],
         (x, taps, seeds[None], seeds[:, None], numer, denom, states, conv, normed, attention,
          grad_normed, inverse, inner, gain, gain_part),
+        vmem=ALL_VMEM,
         scratch=[pltpu.VMEM((width, all_tokens), f32)],
     )
-    shared = call(
+    back = swap(leaving, "seq")
+    joined = call(
         pack_sum_kernel,
         "pack_sum",
-        [((packs, 1024 // packs + 16, LANES), bf16)],
+        [((1024 // packs + 32, LANES), bf16)],
         (weight_parts, small),
     )[0]
-    gathered = swap(shared, "dp")
-    leaving = call(
-        small_kernel,
-        "small",
-        [(leaving.shape, bf16)],
-        (gathered, leaving),
-        grid=(1,),
-        in_specs=[
-            pl.BlockSpec((packs, 16, LANES), lambda i: (0, 1024 // packs // 16, 0)),
-            pl.BlockSpec(memory_space=pl.ANY),
-        ],
-        out_specs=[pl.BlockSpec((groups, 16, LANES), lambda i: (0, 4 * width // 16, 0))],
-        input_output_aliases={1: 0},
+    distance = 1
+    while distance < packs:
+        got = lax.ppermute(joined, "dp", [(i, i ^ distance) for i in range(packs)])
+        rows = joined.shape[0] - 32
+        joined = call(
+            join_kernel, "join", [((2 * rows + 32, LANES), bf16)], (joined, got)
+        )[0]
+        distance *= 2
+    vmem = pl.BlockSpec(memory_space=pltpu.VMEM)
+    weight_grad = call(
+        lambda *refs: unpack_kernel(packs, *refs),
+        "unpack",
+        [((width, features_out), f32)],
+        (lax.axis_index("dp").astype(jnp.int32)[None], joined),
+        in_specs=[pl.BlockSpec(memory_space=pltpu.SMEM), vmem],
     )[0]
-    weight_grad = call(
-        unpack_kernel, "unpack", [((width, features_out), f32)], (gathered,)
+    small = call(
+        spread_kernel,
+        "spread",
+        [((groups, 16, LANES), f32)],
+        (joined, back),
+        in_specs=[vmem, pl.BlockSpec(memory_space=pl.ANY)],
     )[0]
-    back = swap(leaving, "seq")
+    small = swap(small, "seq")
     across = features_out // 3
     block_out, grads = call(
         finish_kernel,
@@ -581,11 +617,13 @@
             pl.BlockSpec((tokens, across), lambda i: (0, i)),
             pl.BlockSpec((1, tokens, width_all), lambda i: (i, 0, 0)),
         ],
+        scratch=[pltpu.VMEM((tokens, width_all), bf16)],
     )
     grad_tokens = grads.transpose(1, 0, 2)
-    small_all = back[:, 4 * width : 4 * width + 10, :width].astype(f32)
-    small_all = small_all.transpose(1, 0, 2).reshape(10, width_all)
-    return block_out[None], grad_tokens[None], weight_grad, small_all[9], small_all[:9]
+    taps_grad, gain_grad = call(
+        small_kernel, "small", [((9, width_all), f32), ((1, width_all), f32)], (small,)
+    )
+    return block_out[None], grad_tokens[None], weight_grad, gain_grad.reshape(-1), taps_grad
 
 
 def solution(mesh):

time: 214 us -> 194 us (0.907)
  starting transfers between devices: 43.5 us -> 66.6 us
  blocking collectives: 20.6 us -> 0 us
  waiting for transfers between devices: 82.7 us -> 65.1 us
  local copies, waits for them, and re-layouts: 20.4 us -> 8.5 us
  Pallas kernels: 31.6 us -> 38.5 us
    all_to_all x5 -> x6, waiting for transfers between devices: 81.3 us -> 54.6 us  [swap(): return lax.all_to_all(blocks, axis, split_axis=0, concat_axis=0, tiled=True)]
    ppermute x0 -> x5, starting transfers between devices: none -> 22.6 us  [local(): got = lax.ppermute(joined, 'dp', [(i, i ^ distance) for i in range(packs)])]
    all_to_all x1 -> x0, blocking collectives: 20.6 us -> none  [swap(): return lax.all_to_all(blocks, axis, split_axis=0, concat_axis=0, tiled=True)]
    unnamed x52 -> x34, local copies, waits for them, and re-layouts: 16.2 us -> 5.95 us
    ppermute x0 -> x5, waiting for transfers between devices: none -> 9.76 us  [local(): got = lax.ppermute(joined, 'dp', [(i, i ^ distance) for i in range(packs)])]
    pallas_call x9 -> x15, Pallas kernels: 31.6 us -> 38.5 us  [call(): pl.pallas_call(kernel, name=name, out_shape=[jax.ShapeDtypeStruct(shape,...]
    all_to_all x5 -> x6, starting transfers between devices: 43.4 us -> 44 us  [swap(): return lax.all_to_all(blocks, axis, split_axis=0, concat_axis=0, tiled=True)]
  transfers between devices with their start and end apart: 7 -> 13, of which waited for: 5 -> 10; matrix products, arithmetic and copies ran while one was open for 2% -> 2% of each run, Pallas kernels for 13% -> 20%
where the time goes in v3:
time: 194 us
  starting transfers between devices  66.6 us (34%)
  waiting for transfers between devices  65.1 us (34%)
  Pallas kernels  38.5 us (20%)
  between operations  14.2 us (7%)
  local copies, waits for them, and re-layouts  8.5 us (4%)
    all_to_all x6, waiting for transfers between devices, swap(): return lax.all_to_all(blocks, axis, split_axis=0, concat_axis=0, tiled=True)  54.6 us
    all_to_all x6, starting transfers between devices, swap(): return lax.all_to_all(blocks, axis, split_axis=0, concat_axis=0, tiled=True)  44 us
    pallas_call x15, Pallas kernels, call(): pl.pallas_call(kernel, name=name, out_shape=[jax.ShapeDtypeStruct(shape,...  38.5 us
    ppermute x5, starting transfers between devices, local(): got = lax.ppermute(joined, 'dp', [(i, i ^ distance) for i in range(packs)])  22.6 us
    ppermute x5, waiting for transfers between devices, local(): got = lax.ppermute(joined, 'dp', [(i, i ^ distance) for i in range(packs)])  9.76 us
    unnamed x34, local copies, waits for them, and re-layouts  5.95 us
  transfers between devices with their start and end apart: 13, of which 10 were waited for; matrix products, arithmetic and copies ran while one was open for 2% of the time, Pallas kernels for 20%

profile of v3, /device:TPU:1, one launch (start us, length us, event | category | flops | bytes accessed | tf_op | source)
XLA Modules:
  0.0 193.5 jit_solution(9464970105073338300)
XLA Ops:
  7.2 0.0 all-gather.6.cloned.1.call-start
  7.2 0.7 all-gather.6.cloned.1.call-update
  7.9 0.7 copy.20
  8.6 1.3 copy-done.4
  9.9 1.4 prepare.1
  11.3 10.5 %all-to-all-start = ((bf16[16,304,128]{2,1,0:T(8,128)(2,1)}), bf16[16,304,128]{2,1,0:T(8,128)(2,1)S(1)}, u32[]{:S(2)}, u32[]{:S(2)}) async-start(bf16[16,304,128]{2,1,0:T(8,128)(2,1)} %prepare.1), calls=%async_computation | async-start | bytes 2490368 | tf_op jit(solution)/shard_map/all_to_all | solution.py:489
  21.9 0.1 constant_dynamic-slice_fusion
  22.0 0.1 copy.18
  22.1 0.1 dynamic_slice.10
  22.2 0.1 broadcast_in_dim.15
  22.2 0.1 broadcast_in_dim_reshape.7.refs_2_
  22.3 39.8 %all-to-all-done.refs_0_ = bf16[16,304,128]{2,1,0:T(8,128)(2,1)S(1)} async-done(((bf16[16,304,128]{2,1,0:T(8,128)(2,1)}), bf16[16,304,128]{2,1,0:T(8,128)(2,1)S(1)}, u32[]{:S(2)}, u32[]{:S(2)}) %all-to-all-start) | async-done | bytes 1245216 | tf_op jit(solution)/shard_map/all_to_all | solution.py:489
  62.2 6.4 %forward.1 = (f32[96,2048]{1,0:T(8,128)S(1)}, f32[8,2048]{1,0:T(8,128)S(1)}, bf16[96,2048]{1,0:T(8,128)(2,1)S(1)}, bf16[16,16,128]{2,1,0:T(8,128)(2,1)}, bf16[38...) custom-call(bf16[16,304,128]{2,1,0:T(8,128)(2,1)S(1)} %all-to-all-done.refs_0_, ...), custom_call_target="tpu_custom_call" | custom-call | tf_op jit(solution)/shard_map/forward/pallas_call | solution.py:478
  68.6 0.8 copy-done.3
  69.3 0.9 copy-done.6
  70.2 0.8 copy-done.7
  71.1 0.7 copy-done.9
  71.8 0.6 copy-done.10
  72.5 5.9 %all-to-all-start.1 = ((bf16[16,16,128]{2,1,0:T(8,128)(2,1)}), bf16[16,16,128]{2,1,0:T(8,128)(2,1)S(1)}, u32[]{:S(2)}, u32[]{:S(2)}) async-start(bf16[16,16,128]{2,1,0:T(8,128)(2,1)} %get-tuple-element.30), calls=%async_computation.1 | async-start | bytes 131072 | tf_op jit(solution)/shard_map/all_to_all | solution.py:489
  78.3 0.8 dynamic-slice_bitcast_fusion
  79.1 0.7 copy.13.gain_ref.refs_13_
  79.8 4.3 %inner.1 = (f32[96,2048]{1,0:T(8,128)}, bf16[16,16,128]{2,1,0:T(8,128)(2,1)}) custom-call(bf16[96,2048]{1,0:T(8,128)(2,1)} %copy-done.3, bf16[96,1152]{1,0:T(8,128)(2,1)} %weight_ref.1, bf16[2048,1152]{1,0:T(8,128)(2,1)} %bitcast.17, f32[96,1]{1,0:T(8,128)} %copy.13.gain_ref.refs_13_), custom_call_target="tpu_custom_call" | custom-call | tf_op jit(solution)/shard_map/inner/pallas_call | solution.py:478
  84.2 2.0 %all-to-all-done.1.squares_ref = bf16[16,16,128]{2,1,0:T(8,128)(2,1)S(1)} async-done(((bf16[16,16,128]{2,1,0:T(8,128)(2,1)}), bf16[16,16,128]{2,1,0:T(8,128)(2,1)S(1)}, u32[]{:S(2)}, u32[]{:S(2)}) %all-to-all-start.1) | async-done | bytes 65568 | tf_op jit(solution)/shard_map/all_to_all | solution.py:489
  86.2 5.3 %all-to-all-start.2 = ((bf16[16,16,128]{2,1,0:T(8,128)(2,1)}), bf16[16,16,128]{2,1,0:T(8,128)(2,1)S(1)}, u32[]{:S(2)}, u32[]{:S(2)}) async-start(bf16[16,16,128]{2,1,0:T(8,128)(2,1)} %get-tuple-element.33), calls=%async_computation.2 | async-start | bytes 131072 | tf_op jit(solution)/shard_map/all_to_all | solution.py:489
  91.5 4.4 %normed.1 = (bf16[16,96,128]{2,1,0:T(8,128)(2,1)}, f32[16,128]{1,0:T(8,128)}, bf16[1024,128]{1,0:T(8,128)(2,1)}, f32[96,128]{1,0:T(8,128)}) custom-call(bf16[96,2048]{1,0:T(8,128)(2,1)} %copy-done.3, f32[96,2048]{1,0:T(8,128)} %get-tuple-element.29.grad_normed_ref.refs_10_, bf16[16,16,128]{2,1,0:T(8,128)(2,1)} %copy-done.14, ...), custom_call_target="tpu_custom_call" | custom-call | tf_op jit(solution)/shard_map/normed/pallas_call | solution.py:478
  95.9 3.4 %all-to-all-done.2.refs_12_ = bf16[16,16,128]{2,1,0:T(8,128)(2,1)S(1)} async-done(((bf16[16,16,128]{2,1,0:T(8,128)(2,1)}), bf16[16,16,128]{2,1,0:T(8,128)(2,1)S(1)}, u32[]{:S(2)}, u32[]{:S(2)}) %all-to-all-start.2) | async-done | bytes 65568 | tf_op jit(solution)/shard_map/all_to_all | solution.py:489
  99.3 12.9 %all-to-all-start.4 = ((bf16[32,32,128]{2,1,0:T(8,128)(2,1)}), bf16[32,32,128]{2,1,0:T(8,128)(2,1)S(1)}, u32[]{:S(2)}, u32[]{:S(2)}) async-start(bf16[32,32,128]{2,1,0:T(8,128)(2,1)} %bitcast.19), calls=%async_computation.4 | async-start | bytes 524288 | tf_op jit(solution)/shard_map/all_to_all | solution.py:489
  112.2 0.7 broadcast_in_dim_reshape.9.refs_3_
  112.9 14.6 %backward.1 = (bf16[16,384,128]{2,1,0:T(8,128)(2,1)}, f32[16,128]{1,0:T(8,128)}) custom-call(bf16[16,304,128]{2,1,0:T(8,128)(2,1)} %copy-done.2, f32[96,16]{1,0:T(8,128)} %copy-done.8, s32[1,96]{1,0:T(1,128)} %copy-done.12, s32[96,1]{1,0:T(8,128)} %broadcast_in_dim_reshape.9.refs_3_, f32[96,2048]{1,0:T(8,128)} %copy-done.6, f32[8,2048]{1,0:T(8,128)} %copy-done.10, ...), custom_call_target="tpu_custom_call" | custom-call | tf_op jit(solution)/shard_map/backward/pallas_call | solution.py:478
  127.5 3.7 %all-to-all-start.3 = ((bf16[16,384,128]{2,1,0:T(8,128)(2,1)}), bf16[16,384,128]{2,1,0:T(8,128)(2,1)S(1)}, u32[]{:S(2)}, u32[]{:S(2)}) async-start(bf16[16,384,128]{2,1,0:T(8,128)(2,1)} %get-tuple-element.35), calls=%async_computation.3 | async-start | bytes 3145728 | tf_op jit(solution)/shard_map/all_to_all | solution.py:489
  131.3 3.2 %collective-permute-start = (bf16[64,128]{1,0:T(8,128)(2,1)S(1)}, bf16[64,128]{1,0:T(8,128)(2,1)S(1)}, u32[]{:S(2)}, u32[]{:S(2)}) collective-permute-start(bf16[64,128]{1,0:T(8,128)(2,1)S(1)} %pack_sum.1.own_ref), channel_id=1, source_target_pairs={{0,16},{16,0},{32,48},{48,32},{64,80},{80,64},{96,112},{112,96},{1... | collective-permute-start | bytes 49160 | tf_op jit(solution)/shard_map/ppermute | solution.py:581
  134.6 1.2 collective-permute-done.got_ref
  135.8 4.2 %collective-permute-start.1 = (bf16[96,128]{1,0:T(8,128)(2,1)S(1)}, bf16[96,128]{1,0:T(8,128)(2,1)S(1)}, u32[]{:S(2)}, u32[]{:S(2)}) collective-permute-start(bf16[96,128]{1,0:T(8,128)(2,1)S(1)} %join.5.own_ref), channel_id=1, source_target_pairs={{0,32},{16,48},{32,0},{48,16},{64,96},{80,112},{96,64},{112,80},{1... | collective-permute-start | bytes 73736 | tf_op jit(solution)/shard_map/ppermute | solution.py:581
  140.0 1.6 collective-permute-done.1.got_ref
  141.6 7.4 %collective-permute-start.2 = (bf16[160,128]{1,0:T(8,128)(2,1)S(1)}, bf16[160,128]{1,0:T(8,128)(2,1)S(1)}, u32[]{:S(2)}, u32[]{:S(2)}) collective-permute-start(bf16[160,128]{1,0:T(8,128)(2,1)S(1)} %join.6.own_ref), channel_id=1, source_target_pairs={{0,64},{16,80},{32,96},{48,112},{64,0},{80,16},{96,32},{112,48},{1... | collective-permute-start | bytes 122888 | tf_op jit(solution)/shard_map/ppermute | solution.py:581
  149.0 1.7 collective-permute-done.2.got_ref
  150.7 3.1 %collective-permute-start.3 = (bf16[288,128]{1,0:T(8,128)(2,1)S(1)}, bf16[288,128]{1,0:T(8,128)(2,1)S(1)}, u32[]{:S(2)}, u32[]{:S(2)}) collective-permute-start(bf16[288,128]{1,0:T(8,128)(2,1)S(1)} %join.7.own_ref), channel_id=1, source_target_pairs={{0,128},{16,144},{32,160},{48,176},{64,192},{80,208},{96,224},{112... | collective-permute-start | bytes 221192 | tf_op jit(solution)/shard_map/ppermute | solution.py:581
  153.8 2.3 %collective-permute-done.3.got_ref = bf16[288,128]{1,0:T(8,128)(2,1)S(1)} collective-permute-done((bf16[288,128]{1,0:T(8,128)(2,1)S(1)}, bf16[288,128]{1,0:T(8,128)(2,1)S(1)}, u32[]{:S(2)}, u32[]{:S(2)}) %collective-permute-start.3) | collective-permute-done | bytes 73760 | tf_op jit(solution)/shard_map/ppermute | solution.py:581
  156.1 4.6 %collective-permute-start.4 = (bf16[544,128]{1,0:T(8,128)(2,1)S(1)}, bf16[544,128]{1,0:T(8,128)(2,1)S(1)}, u32[]{:S(2)}, u32[]{:S(2)}) collective-permute-start(bf16[544,128]{1,0:T(8,128)(2,1)S(1)} %join.8.own_ref), channel_id=1, source_target_pairs={{0,256},{16,272},{32,288},{48,304},{64,320},{80,336},{96,352},{112... | collective-permute-start | bytes 417800 | tf_op jit(solution)/shard_map/ppermute | solution.py:581
  160.7 3.0 %collective-permute-done.4.got_ref = bf16[544,128]{1,0:T(8,128)(2,1)S(1)} collective-permute-done((bf16[544,128]{1,0:T(8,128)(2,1)S(1)}, bf16[544,128]{1,0:T(8,128)(2,1)S(1)}, u32[]{:S(2)}, u32[]{:S(2)}) %collective-permute-start.4) | collective-permute-done | bytes 139296 | tf_op jit(solution)/shard_map/ppermute | solution.py:581
  163.7 6.0 %all-to-all-done.3.normed_ref.grad_ref._ = bf16[16,384,128]{2,1,0:T(8,128)(2,1)S(1)} async-done(((bf16[16,384,128]{2,1,0:T(8,128)(2,1)}), bf16[16,384,128]{2,1,0:T(8,128)(2,1)S(1)}, u32[]{:S(2)}, u32[]{:S(2)}) %all-to-all-start.3) | async-done | bytes 1572896 | tf_op jit(solution)/shard_map/all_to_all | solution.py:489
  169.7 0.7 spread.1
  170.4 5.7 %all-to-all-start.5 = ((f32[16,16,128]{2,1,0:T(8,128)}), f32[16,16,128]{2,1,0:T(8,128)S(1)}, u32[]{:S(2)}, u32[]{:S(2)}) async-start(f32[16,16,128]{2,1,0:T(8,128)} %spread.1), calls=%async_computation.5 | async-start | bytes 262144 | tf_op jit(solution)/shard_map/all_to_all | solution.py:489
  176.1 0.8 unpack.1
  177.0 4.9 %finish.1 = (bf16[128,1152]{1,0:T(8,128)(2,1)}, bf16[3,128,1536]{2,1,0:T(8,128)(2,1)}) custom-call(bf16[16,384,128]{2,1,0:T(8,128)(2,1)} %copy-done.1, bf16[16,384,128]{2,1,0:T(8,128)(2,1)} %copy-done.1, bf16[1536,1152]{1,0:T(8,128)(2,1)} %all-gather.4.cloned.1.call-done.weight_ref), custom_call_target="tpu_custom_call" | custom-call | tf_op jit(solution)/shard_map/finish/pallas_call | solution.py:478
  181.8 3.5 %all-to-all-done.5.small_ref = f32[16,16,128]{2,1,0:T(8,128)S(1)} async-done(((f32[16,16,128]{2,1,0:T(8,128)}), f32[16,16,128]{2,1,0:T(8,128)S(1)}, u32[]{:S(2)}, u32[]{:S(2)}) %all-to-all-start.5) | async-done | bytes 131104 | tf_op jit(solution)/shard_map/all_to_all | solution.py:489
  185.3 0.7 small.1
  186.1 0.6 reduce
  (39 shorter events, 0.3 us)
Async XLA Ops:
  7.2 14.7 %copy-start = (f32[9,1536]{1,0:T(8,128)S(1)}, f32[9,1536]{1,0:T(8,128)}, u32[]{:S(2)}) copy-start(f32[9,1536]{1,0:T(8,128)} %param.11) | copy-start | bytes 165892
  7.2 72.7 %all-gather.6.cloned.1.call-start = ((), (), s32[]{:S(2)}) async-start(), calls=%async_computation.7 | async-start | bytes 5013504 | tf_op jit(solution)/shard_map/all_gather | solution.py:501
  8.6 1.3 copy-start.4
  11.3 10.8 %copy-start.15 = (s32[48]{0:T(128)S(1)}, s32[48]{0:T(128)}, u32[]{:S(2)}) copy-start(s32[48]{0:T(128)} %param.12) | copy-start | bytes 580
  11.3 50.9 %copy-start.5 = (bf16[96,1152]{1,0:T(8,128)(2,1)S(1)}, bf16[96,1152]{1,0:T(8,128)(2,1)}, u32[]{:S(2)}) copy-start(bf16[96,1152]{1,0:T(8,128)(2,1)} %weight_ref.1) | copy-start | bytes 663556
  11.3 50.9 %all-to-all-start = ((bf16[16,304,128]{2,1,0:T(8,128)(2,1)}), bf16[16,304,128]{2,1,0:T(8,128)(2,1)S(1)}, u32[]{:S(2)}, u32[]{:S(2)}) async-start(bf16[16,304,128]{2,1,0:T(8,128)(2,1)} %prepare.1), calls=%async_computation | async-start | bytes 2490368 | tf_op jit(solution)/shard_map/all_to_all | solution.py:489
  21.8 155.2 %all-gather.4.cloned.1.call-start = ((), (), s32[]{:S(2)}) async-start(), calls=%async_computation.6 | async-start | bytes 3760128 | tf_op jit(solution)/shard_map/all_gather | solution.py:529
  22.3 61.9 %copy-start.12 = (s32[1,96]{1,0:T(1,128)}, s32[1,96]{1,0:T(1,128)S(1)}, u32[]{:S(2)}) copy-start(s32[1,96]{1,0:T(1,128)S(1)} %broadcast_in_dim_reshape.7.refs_2_) | copy-start | bytes 1156
  22.3 61.8 %copy-start.8 = (f32[96,16]{1,0:T(8,128)}, f32[96,16]{1,0:T(8,128)S(1)}, u32[]{:S(2)}) copy-start(f32[96,16]{1,0:T(8,128)S(1)} %pad.9.refs_1_) | copy-start | bytes 18436
  62.2 22.0 %copy-start.2 = (bf16[16,304,128]{2,1,0:T(8,128)(2,1)}, bf16[16,304,128]{2,1,0:T(8,128)(2,1)S(1)}, u32[]{:S(2)}) copy-start(bf16[16,304,128]{2,1,0:T(8,128)(2,1)S(1)} %all-to-all-done.refs_0_) | copy-start | bytes 3735556
  68.6 0.8 copy-start.3
  69.3 0.9 copy-start.6
  70.2 0.8 copy-start.7
  71.1 0.7 copy-start.9
  71.8 0.6 copy-start.10
  72.5 13.7 %all-to-all-start.1 = ((bf16[16,16,128]{2,1,0:T(8,128)(2,1)}), bf16[16,16,128]{2,1,0:T(8,128)(2,1)S(1)}, u32[]{:S(2)}, u32[]{:S(2)}) async-start(bf16[16,16,128]{2,1,0:T(8,128)(2,1)} %get-tuple-element.30), calls=%async_computation.1 | async-start | bytes 131072 | tf_op jit(solution)/shard_map/all_to_all | solution.py:489
  86.2 5.3 %copy-start.14 = (bf16[16,16,128]{2,1,0:T(8,128)(2,1)}, bf16[16,16,128]{2,1,0:T(8,128)(2,1)S(1)}, u32[]{:S(2)}) copy-start(bf16[16,16,128]{2,1,0:T(8,128)(2,1)S(1)} %all-to-all-done.1.squares_ref) | copy-start | bytes 196612
  86.2 13.1 %all-to-all-start.2 = ((bf16[16,16,128]{2,1,0:T(8,128)(2,1)}), bf16[16,16,128]{2,1,0:T(8,128)(2,1)S(1)}, u32[]{:S(2)}, u32[]{:S(2)}) async-start(bf16[16,16,128]{2,1,0:T(8,128)(2,1)} %get-tuple-element.33), calls=%async_computation.2 | async-start | bytes 131072 | tf_op jit(solution)/shard_map/all_to_all | solution.py:489
  99.3 13.6 %copy-start.13 = (bf16[16,16,128]{2,1,0:T(8,128)(2,1)}, bf16[16,16,128]{2,1,0:T(8,128)(2,1)S(1)}, u32[]{:S(2)}) copy-start(bf16[16,16,128]{2,1,0:T(8,128)(2,1)S(1)} %all-to-all-done.2.refs_12_) | copy-start | bytes 196612
  99.3 28.3 %all-to-all-start.4 = ((bf16[32,32,128]{2,1,0:T(8,128)(2,1)}), bf16[32,32,128]{2,1,0:T(8,128)(2,1)S(1)}, u32[]{:S(2)}, u32[]{:S(2)}) async-start(bf16[32,32,128]{2,1,0:T(8,128)(2,1)} %bitcast.19), calls=%async_computation.4 | async-start | bytes 524288 | tf_op jit(solution)/shard_map/all_to_all | solution.py:489
  127.5 3.7 %copy-start.11 = (f32[16,128]{1,0:T(8,128)S(1)}, f32[16,128]{1,0:T(8,128)}, u32[]{:S(2)}) copy-start(f32[16,128]{1,0:T(8,128)} %get-tuple-element.40.small_ref) | copy-start | bytes 24580
  127.5 42.2 %all-to-all-start.3 = ((bf16[16,384,128]{2,1,0:T(8,128)(2,1)}), bf16[16,384,128]{2,1,0:T(8,128)(2,1)S(1)}, u32[]{:S(2)}, u32[]{:S(2)}) async-start(bf16[16,384,128]{2,1,0:T(8,128)(2,1)} %get-tuple-element.35), calls=%async_computation.3 | async-start | bytes 3145728 | tf_op jit(solution)/shard_map/all_to_all | solution.py:489
  131.3 4.5 %collective-permute-start = (bf16[64,128]{1,0:T(8,128)(2,1)S(1)}, bf16[64,128]{1,0:T(8,128)(2,1)S(1)}, u32[]{:S(2)}, u32[]{:S(2)}) collective-permute-start(bf16[64,128]{1,0:T(8,128)(2,1)S(1)} %pack_sum.1.own_ref), channel_id=1, source_target_pairs={{0,16},{16,0},{32,48},{48,32},{64,80},{80,64},{96,112},{112,96},{1... | collective-permute-start | bytes 49160 | tf_op jit(solution)/shard_map/ppermute | solution.py:581
  135.8 5.8 %collective-permute-start.1 = (bf16[96,128]{1,0:T(8,128)(2,1)S(1)}, bf16[96,128]{1,0:T(8,128)(2,1)S(1)}, u32[]{:S(2)}, u32[]{:S(2)}) collective-permute-start(bf16[96,128]{1,0:T(8,128)(2,1)S(1)} %join.5.own_ref), channel_id=1, source_target_pairs={{0,32},{16,48},{32,0},{48,16},{64,96},{80,112},{96,64},{112,80},{1... | collective-permute-start | bytes 73736 | tf_op jit(solution)/shard_map/ppermute | solution.py:581
  141.6 9.1 %collective-permute-start.2 = (bf16[160,128]{1,0:T(8,128)(2,1)S(1)}, bf16[160,128]{1,0:T(8,128)(2,1)S(1)}, u32[]{:S(2)}, u32[]{:S(2)}) collective-permute-start(bf16[160,128]{1,0:T(8,128)(2,1)S(1)} %join.6.own_ref), channel_id=1, source_target_pairs={{0,64},{16,80},{32,96},{48,112},{64,0},{80,16},{96,32},{112,48},{1... | collective-permute-start | bytes 122888 | tf_op jit(solution)/shard_map/ppermute | solution.py:581
  150.7 5.4 %collective-permute-start.3 = (bf16[288,128]{1,0:T(8,128)(2,1)S(1)}, bf16[288,128]{1,0:T(8,128)(2,1)S(1)}, u32[]{:S(2)}, u32[]{:S(2)}) collective-permute-start(bf16[288,128]{1,0:T(8,128)(2,1)S(1)} %join.7.own_ref), channel_id=1, source_target_pairs={{0,128},{16,144},{32,160},{48,176},{64,192},{80,208},{96,224},{112... | collective-permute-start | bytes 221192 | tf_op jit(solution)/shard_map/ppermute | solution.py:581
  156.1 7.6 %collective-permute-start.4 = (bf16[544,128]{1,0:T(8,128)(2,1)S(1)}, bf16[544,128]{1,0:T(8,128)(2,1)S(1)}, u32[]{:S(2)}, u32[]{:S(2)}) collective-permute-start(bf16[544,128]{1,0:T(8,128)(2,1)S(1)} %join.8.own_ref), channel_id=1, source_target_pairs={{0,256},{16,272},{32,288},{48,304},{64,320},{80,336},{96,352},{112... | collective-permute-start | bytes 417800 | tf_op jit(solution)/shard_map/ppermute | solution.py:581
  169.7 7.3 %copy-start.1 = (bf16[16,384,128]{2,1,0:T(8,128)(2,1)}, bf16[16,384,128]{2,1,0:T(8,128)(2,1)S(1)}, u32[]{:S(2)}) copy-start(bf16[16,384,128]{2,1,0:T(8,128)(2,1)S(1)} %all-to-all-done.3.normed_ref.grad_ref._) | copy-start | bytes 4718596
  170.4 14.9 %all-to-all-start.5 = ((f32[16,16,128]{2,1,0:T(8,128)}), f32[16,16,128]{2,1,0:T(8,128)S(1)}, u32[]{:S(2)}, u32[]{:S(2)}) async-start(f32[16,16,128]{2,1,0:T(8,128)} %spread.1), calls=%async_computation.5 | async-start | bytes 262144 | tf_op jit(solution)/shard_map/all_to_all | solution.py:489
Sparse Core Ops, SparseCore 0:
  10.1 68.8 all-gather.5
  81.1 44.1 all-gather.3

commit v4 on v3

--- a/solution.py
+++ b/solution.py
@@ -166,15 +166,17 @@
 
 def prepare_kernel(projected_ref, packing_ref, out_ref):
     groups = out_ref.shape[0]
-    parts, tokens, width_all = projected_ref.shape
-    width = width_all // groups
-    for part in range(parts):
-        turned = jnp.transpose(projected_ref[part])
+    width = projected_ref.shape[2] // groups
+    turned = jnp.transpose(projected_ref[0])
+    here = pl.ds(pl.multiple_of(pl.program_id(0) * width, 16), width)
+    for g in range(groups):
+        out_ref[g, here, :] = turned[g * width : (g + 1) * width]
+
+    @pl.when(pl.program_id(0) == 0)
+    def _():
+        rows = packing_ref[...].astype(f32).astype(bf16)
         for g in range(groups):
-            out_ref[g, pl.ds(part * width, width), :] = turned[g * width : (g + 1) * width]
-    rows = packing_ref[...].astype(f32).astype(bf16)
-    for g in range(groups):
-        out_ref[g, pl.ds(parts * width, 16), :] = rows
+            out_ref[g, pl.ds(out_ref.shape[1] - 16, 16), :] = rows
 
 
 def finish_kernel(normed_ref, grad_ref, weight_ref, block_ref, grad_out, turned_ref):
@@ -188,8 +190,8 @@
     block_ref[...] = dot(turned_ref[...], weight_ref[...]).astype(bf16)
 
 
-def forward_kernel(heads, x_ref, taps_ref, seed_row_ref, weight_ref,
-                   numer_ref, denom_ref, attention_ref, squares_ref, states_ref, conv_ref, weight_out):
+def forward_kernel(heads, x_ref, taps_ref, seed_row_ref, weight_ref, _, __,
+                   ratio_ref, half_ref, squares_ref, states_ref, weight_out):
     width = heads * HEAD
     chunks = x_ref.shape[0] * LANES // CHUNK
     middle = chunks // 2
@@ -203,14 +205,15 @@
         return sum(taps[:, 3 * r + c : 3 * r + c + 1] * trio[c] for c in range(3))
 
     conv = row_of_taps(1) + grid.row_above(row_of_taps(0)) + grid.row_below(row_of_taps(2))
-    conv_ref[...] = conv.astype(bf16)
+    half_ref[pl.ds(width, width), :] = conv.astype(bf16)
     omega = omega_tall(seed_row_ref[...], heads)
     front = back = None
     for j in range(chunks):
         lanes = pl.ds(j * CHUNK, CHUNK)
         image = grid.image[:, j * CHUNK : (j + 1) * CHUNK]
         rows = jnp.concatenate(
-            [conv_ref[:, lanes].astype(f32), ones_rows(width, CHUNK, 3 * heads)], axis=0
+            [half_ref[pl.ds(width, width), lanes].astype(f32), ones_rows(width, CHUNK, 3 * heads)],
+            axis=0,
         )
         feat_key = features(dot(omega, chunk_of(x_ref, 1, width, j)) * scale)
         first, last = split_images(rows, image, j, middle)
@@ -233,10 +236,9 @@
         image = grid.image[:, j * CHUNK : (j + 1) * CHUNK]
         feat_query = features(dot(omega, chunk_of(x_ref, 0, width, j)) * scale)
         both = pick_image(states, feat_query, image, j, middle, width + 8)
-        numer_ref[:, lanes] = both[:width]
-        denom_ref[:, lanes] = both[width : width + 8]
-        attention = (both[:width] / by_head(both[width : width + 8], heads)).astype(bf16)
-        attention_ref[:, lanes] = attention
+        ratio_ref[:, lanes] = both
+        attention = (both[:width] * by_head(1.0 / both[width:], heads)).astype(bf16)
+        half_ref[pl.ds(0, width), lanes] = attention
         attention = attention.astype(f32)
         squares.append(jnp.sum(attention * attention, axis=0, keepdims=True))
     to_peers(squares, squares_ref)
@@ -257,8 +259,8 @@
     return jnp.concatenate([values[2 * j : 2 * j + 1], values[2 * j + 1 : 2 * j + 2]], axis=1)
 
 
-def inner_kernel(attention_ref, weight_ref, cotangent_ref, gain_ref, grad_normed_ref, inner_ref,
-                 rows_ref):
+def inner_kernel(attention_ref, weight_ref, cotangent_ref, gain_ref,
+                 grad_normed_ref, inner_ref, rows_ref):
     step = pl.program_id(0)
     chunks = attention_ref.shape[1] // CHUNK
     weight, gain = weight_ref[...], gain_ref[...]
@@ -271,49 +273,67 @@
         inner = jnp.sum(gain * grad_normed * attention, axis=0, keepdims=True)
         for part in range(CHUNK // LANES):
             rows.append(inner[:, part * LANES : (part + 1) * LANES])
-    rows_ref[pl.ds(pl.multiple_of(step * 8, 8), 8), :] = jnp.concatenate(rows, axis=0)
+    for i, row in enumerate(rows):
+        rows_ref[step * len(rows) + i] = row
 
     @pl.when(step == pl.num_programs(0) - 1)
     def _():
-        rows = rows_ref[...].astype(bf16)
+        rows = [rows_ref[i] for i in range(rows_ref.shape[0])]
+        rows = jnp.concatenate(rows, axis=0).astype(bf16)
         for peer in range(inner_ref.shape[0]):
             inner_ref[peer] = rows
 
 
 def normed_kernel(attention_ref, grad_normed_ref, squares_ref, gain_ref, cotangent_ref,
-                  normed_ref, inverse_ref, weight_ref, gain_out):
+                  normed_ref, inverse_ref, weight_ref, gain_out, rows_ref, total_ref, gain_sum_ref):
+    step = pl.program_id(0)
     width, tokens = attention_ref.shape
     chunks = tokens // CHUNK
     groups = squares_ref.shape[0]
     gain = gain_ref[...]
-    squares = jnp.sum(squares_ref[...].astype(f32), axis=0)
-    inverse = lax.rsqrt(squares * (1.0 / (width * groups)) + epsilon)
-    inverse_ref[...] = inverse
-    weight = gain_sum = None
+
+    @pl.when(step == 0)
+    def _():
+        squares = jnp.sum(squares_ref[...].astype(f32), axis=0)
+        inverse = lax.rsqrt(squares * (1.0 / (width * groups)) + epsilon)
+        inverse_ref[...] = inverse
+        for i in range(groups):
+            rows_ref[i] = inverse[i : i + 1]
+        total_ref[...] = jnp.zeros_like(total_ref)
+        gain_sum_ref[...] = jnp.zeros_like(gain_sum_ref)
+
+    weight, gain_sum = total_ref[...], gain_sum_ref[...]
     for j in range(chunks):
         lanes = pl.ds(j * CHUNK, CHUNK)
-        inv_rms = tokens_of(inverse, j)
+        first = (step * chunks + j) * 2
+        inv_rms = jnp.concatenate([rows_ref[first], rows_ref[first + 1]], axis=1)
         attention = attention_ref[:, lanes].astype(f32)
         normed = (attention * gain * inv_rms).astype(bf16)
-        gain_sum = add(gain_sum, grad_normed_ref[:, lanes] * attention * inv_rms)
+        gain_sum = gain_sum + grad_normed_ref[:, lanes] * attention * inv_rms
         for part in range(CHUNK // LANES):
             normed_ref[2 * j + part] = normed[:, part * LANES : (part + 1) * LANES]
-        weight = add(weight, dot(normed, cotangent_ref[pl.ds(j * CHUNK, CHUNK), :]))
-    gain_out[...] = jnp.broadcast_to(jnp.sum(gain_sum, axis=1, keepdims=True), gain_out.shape)
-    across = weight.shape[1] // LANES
-    weight = weight.astype(bf16)
-    for r in range(width // 16):
-        for c in range(across):
-            weight_ref[pl.ds((r * across + c) * 16, 16), :] = weight[
-                r * 16 : (r + 1) * 16, c * LANES : (c + 1) * LANES
-            ]
-    used = width * across
-    weight_ref[used:, :] = jnp.zeros((weight_ref.shape[0] - used, LANES), bf16)
-
-
-def backward_kernel(heads, x_ref, taps_ref, seed_row_ref, seed_column_ref, numer_ref, denom_ref,
-                    states_ref, conv_ref, normed_ref, attention_ref, grad_normed_ref,
-                    inverse_ref, inner_ref, norm_gain_ref, gain_ref, out_ref, small_ref, grad_conv_ref):
+        weight = weight + dot(normed, cotangent_ref[pl.ds(j * CHUNK, CHUNK), :])
+    total_ref[...] = weight
+    gain_sum_ref[...] = gain_sum
+
+    @pl.when(step == pl.num_programs(0) - 1)
+    def _():
+        total = jnp.sum(gain_sum_ref[...], axis=1, keepdims=True)
+        gain_out[...] = jnp.broadcast_to(total, gain_out.shape)
+        across = total_ref.shape[1] // LANES
+        for r in range(width // 16):
+            for c in range(across):
+                weight_ref[pl.ds((r * across + c) * 16, 16), :] = total_ref[
+                    pl.ds(r * 16, 16), pl.ds(c * LANES, LANES)
+                ].astype(bf16)
+        used = width * across
+        weight_ref[used:, :] = jnp.zeros((weight_ref.shape[0] - used, LANES), bf16)
+
+
+def backward_kernel(heads, x_ref, taps_ref, seed_row_ref, seed_column_ref, ratio_ref, half_ref,
+                    states_ref, normed_ref, grad_normed_ref,
+                    inverse_ref, inner_ref, norm_gain_ref, gain_ref, out_ref, small_ref,
+                    grad_conv_ref):
     width = heads * HEAD
     chunks = x_ref.shape[0] * LANES // CHUNK
     middle = chunks // 2
@@ -348,16 +368,15 @@
         pre = dot(omega, chunk_of(x_ref, 0, width, j)) * scale
         feat_query = features(pre)
         grad = tokens_of(inverse, j) * norm_gain * grad_normed_ref[:, lanes]
-        grad = grad - attention_ref[:, lanes].astype(f32) * tokens_of(away, j)
+        grad = grad - half_ref[pl.ds(0, width), lanes].astype(f32) * tokens_of(away, j)
         grad = grad.astype(bf16).astype(f32)
-        denom = denom_ref[:, lanes]
-        grad_numer = (grad / by_head(denom, heads)).astype(bf16).astype(f32)
-        dots = head_sums(grad * numer_ref[:, lanes], heads)
+        below = 1.0 / ratio_ref[pl.ds(width, 8), lanes]
+        grad_numer = (grad * by_head(below, heads)).astype(bf16).astype(f32)
+        dots = head_sums(grad * ratio_ref[pl.ds(0, width), lanes], heads)
         row = lax.broadcasted_iota(jnp.int32, (LANES - width, CHUNK), 0)
         extra = jnp.zeros((LANES - width, CHUNK), f32)
         for h in range(heads):
-            below = denom[h : h + 1]
-            rest = -dots[h] / (below * below)
+            rest = -dots[h] * (below[h : h + 1] * below[h : h + 1])
             for level in range(3):
                 high = rest.astype(bf16).astype(f32)
                 extra = jnp.where(row == level * heads + h, high, extra)
@@ -386,7 +405,7 @@
         pre = dot(omega, chunk_of(x_ref, 1, width, j)) * scale
         feat_key = features(pre)
         rows = jnp.concatenate(
-            [conv_ref[:, lanes].astype(f32), ones_rows(width, CHUNK, 1)], axis=0
+            [half_ref[pl.ds(width, width), lanes].astype(f32), ones_rows(width, CHUNK, 1)], axis=0
         )
         first, last = split_images(rows, image, j, middle)
         gate = jnp.where(pre > 0, spread(table, first, last), 0.0).astype(bf16)
@@ -504,6 +523,13 @@
         "prepare",
         [((groups, 3 * width + 16, tokens), bf16)],
         (projected[0].transpose(1, 0, 2), jnp.pad(packing[0], ((0, 11), (0, 0)))),
+        vmem=ALL_VMEM,
+        grid=(3,),
+        in_specs=[
+            pl.BlockSpec((1, tokens, width_all), lambda i: (i, 0, 0)),
+            pl.BlockSpec((16, tokens), lambda i: (0, 0)),
+        ],
+        out_specs=[pl.BlockSpec((groups, 3 * width + 16, tokens), lambda i: (0, 0, 0))],
     )[0]
     seeds = jnp.repeat(lax.dynamic_slice_in_dim(feature_seeds, member * heads, heads, 0), HEAD)
     taps = jnp.pad(
@@ -511,40 +537,47 @@
     )
     gain = lax.dynamic_slice_in_dim(norm_gain, member * width, width, 0)[:, None]
     x = swap(outgoing, "seq")
-    numer, denom, attention, squares, states, conv, weight_local = call(
+    anywhere = pl.BlockSpec(memory_space=pl.ANY)
+    vmem = pl.BlockSpec(memory_space=pltpu.VMEM)
+    seed_column = seeds[:, None]
+    ratio, half, squares, states, weight_local = call(
         lambda *refs: forward_kernel(heads, *refs),
         "forward",
         [
-            ((width, all_tokens), f32),
-            ((8, all_tokens), f32),
-            ((width, all_tokens), bf16),
+            ((width + 8, all_tokens), f32),
+            ((2 * width, all_tokens), bf16),
             ((groups, groups, LANES), bf16),
             ((3 * LANES, heads * FEAT), bf16),
-            ((width, all_tokens), bf16),
             ((width, features_out), bf16),
         ],
-        (x, taps, seeds[None], out_weight),
+        (x, taps, seeds[None], out_weight, seed_column, gain),
+        in_specs=[vmem, vmem, vmem, vmem, anywhere, anywhere],
     )
     squares = swap(squares, "seq")
     weight_all = lax.all_gather(weight_local, "seq", axis=0, tiled=True)
+    steps = groups // 4
+    block = 4 * LANES
     grad_normed, inner = call(
         inner_kernel,
         "inner",
-        [((width, all_tokens), f32), ((groups, groups, LANES), bf16)],
-        (attention, out_weight, cotangent_all, gain),
+        [
+            ((width, all_tokens), f32),
+            ((groups, groups, LANES), bf16),
+        ],
+        (half, out_weight, cotangent_all, gain),
         vmem=ALL_VMEM,
-        grid=(groups // 8,),
+        grid=(steps,),
         in_specs=[
-            pl.BlockSpec((width, 8 * LANES), lambda i: (0, i)),
+            pl.BlockSpec((width, block), lambda i: (0, i)),
             pl.BlockSpec((width, features_out), lambda i: (0, 0)),
-            pl.BlockSpec((8 * LANES, features_out), lambda i: (i, 0)),
+            pl.BlockSpec((block, features_out), lambda i: (i, 0)),
             pl.BlockSpec((width, 1), lambda i: (0, 0)),
         ],
         out_specs=[
-            pl.BlockSpec((width, 8 * LANES), lambda i: (0, i)),
+            pl.BlockSpec((width, block), lambda i: (0, i)),
             pl.BlockSpec((groups, groups, LANES), lambda i: (0, 0, 0)),
         ],
-        scratch=[pltpu.VMEM((groups, LANES), f32)],
+        scratch=[pltpu.VMEM((groups, 1, LANES), f32)],
     )
     inner = swap(inner, "seq")
     normed, inverse, weight_tiles, gain_part = call(
@@ -556,15 +589,34 @@
             ((1024, LANES), bf16),
             ((width, LANES), f32),
         ],
-        (attention, grad_normed, squares, gain, cotangent_all),
+        (half, grad_normed, squares, gain, cotangent_all),
         vmem=ALL_VMEM,
+        grid=(steps,),
+        in_specs=[
+            pl.BlockSpec((width, block), lambda i: (0, i)),
+            pl.BlockSpec((width, block), lambda i: (0, i)),
+            pl.BlockSpec((groups, groups, LANES), lambda i: (0, 0, 0)),
+            pl.BlockSpec((width, 1), lambda i: (0, 0)),
+            pl.BlockSpec((block, features_out), lambda i: (i, 0)),
+        ],
+        out_specs=[
+            pl.BlockSpec((groups // steps, width, LANES), lambda i: (i, 0, 0)),
+            pl.BlockSpec((groups, LANES), lambda i: (0, 0)),
+            pl.BlockSpec((1024, LANES), lambda i: (0, 0)),
+            pl.BlockSpec((width, LANES), lambda i: (0, 0)),
+        ],
+        scratch=[
+            pltpu.VMEM((groups, 1, LANES), f32),
+            pltpu.VMEM((width, features_out), f32),
+            pltpu.VMEM((width, CHUNK), f32),
+        ],
     )
     weight_parts = swap(weight_tiles.reshape(packs, 1024 // packs, LANES), "dp")
     leaving, small = call(
         lambda *refs: backward_kernel(heads, *refs),
         "backward",
         [((groups, 4 * width, LANES), bf16), ((16, LANES), f32)],
-        (x, taps, seeds[None], seeds[:, None], numer, denom, states, conv, normed, attention,
+        (x, taps, seeds[None], seed_column, ratio, half, states, normed,
          grad_normed, inverse, inner, gain, gain_part),
         vmem=ALL_VMEM,
         scratch=[pltpu.VMEM((width, all_tokens), f32)],
@@ -584,7 +636,6 @@
             join_kernel, "join", [((2 * rows + 32, LANES), bf16)], (joined, got)
         )[0]
         distance *= 2
-    vmem = pl.BlockSpec(memory_space=pltpu.VMEM)
     weight_grad = call(
         lambda *refs: unpack_kernel(packs, *refs),
         "unpack",
@@ -597,7 +648,7 @@
         "spread",
         [((groups, 16, LANES), f32)],
         (joined, back),
-        in_specs=[vmem, pl.BlockSpec(memory_space=pl.ANY)],
+        in_specs=[vmem, anywhere],
     )[0]
     small = swap(small, "seq")
     across = features_out // 3

time: 194 us -> 195 us (level)
  Pallas kernels: 38.5 us -> 42.1 us
  local copies, waits for them, and re-layouts: 8.5 us -> 5.39 us
    pallas_call x15, Pallas kernels: 38.5 us -> 42.1 us  [call(): pl.pallas_call(kernel, name=name, out_shape=[jax.ShapeDtypeStruct(shape,...]
    unnamed x34 -> x32, local copies, waits for them, and re-layouts: 5.95 us -> 3.48 us
    all_to_all x6, waiting for transfers between devices: 54.6 us -> 52.2 us  [swap(): return lax.all_to_all(blocks, axis, split_axis=0, concat_axis=0, tiled=True)]
  transfers between devices with their start and end apart: 13 -> 13, of which waited for: 10 -> 11; matrix products, arithmetic and copies ran while one was open for 2% -> 1% of each run, Pallas kernels for 20% -> 21%
where the time goes in v4:
time: 195 us; the launch traced here: 193 us
  starting transfers between devices  67 us (34%)
  waiting for transfers between devices  64.2 us (33%)
  Pallas kernels  42.1 us (22%)
  between operations  14.2 us (7%)
  local copies, waits for them, and re-layouts  5.39 us (3%)
    all_to_all x6, waiting for transfers between devices, swap(): return lax.all_to_all(blocks, axis, split_axis=0, concat_axis=0, tiled=True)  52.2 us
    all_to_all x6, starting transfers between devices, swap(): return lax.all_to_all(blocks, axis, split_axis=0, concat_axis=0, tiled=True)  44.3 us
    pallas_call x15, Pallas kernels, call(): pl.pallas_call(kernel, name=name, out_shape=[jax.ShapeDtypeStruct(shape,...  42.1 us
    ppermute x5, starting transfers between devices, local(): got = lax.ppermute(joined, 'dp', [(i, i ^ distance) for i in range(packs)])  22.5 us
    ppermute x5, waiting for transfers between devices, local(): got = lax.ppermute(joined, 'dp', [(i, i ^ distance) for i in range(packs)])  9.75 us
  transfers between devices with their start and end apart: 13, of which 11 were waited for; matrix products, arithmetic and copies ran while one was open for 1% of the time, Pallas kernels for 21%

profile of v4, /device:TPU:1, one launch (start us, length us, event | category | flops | bytes accessed | tf_op | source)
XLA Modules:
  0.0 193.5 jit_solution(11873572682475908989)
XLA Ops:
  7.2 0.0 all-gather.6.cloned.1.call-start
  7.2 0.7 all-gather.6.cloned.1.call-update
  7.9 0.7 copy.22
  8.6 0.6 pad.8.packing_ref
  9.2 3.4 %prepare.1 = bf16[16,304,128]{2,1,0:T(8,128)(2,1)} custom-call(bf16[3,128,1536]{2,1,0:T(8,128)(2,1)} %bitcast.18, s32[16,128]{1,0:T(8,128)} %pad.8.packing_ref), custom_call_target="tpu_custom_call" | custom-call | tf_op jit(solution)/shard_map/prepare/pallas_call | solution.py:497
  12.6 10.5 %all-to-all-start = ((bf16[16,304,128]{2,1,0:T(8,128)(2,1)}), bf16[16,304,128]{2,1,0:T(8,128)(2,1)S(1)}, u32[]{:S(2)}, u32[]{:S(2)}) async-start(bf16[16,304,128]{2,1,0:T(8,128)(2,1)} %prepare.1), calls=%async_computation | async-start | bytes 2490368 | tf_op jit(solution)/shard_map/all_to_all | solution.py:508
  23.1 0.0 all-gather.4.cloned.1.call-start
  23.2 0.1 dynamic_slice.10
  23.2 0.1 broadcast_in_dim.15
  23.3 0.1 broadcast_in_dim_reshape.9.refs_4_.refs_3_
  23.4 0.1 broadcast_in_dim_reshape.7.refs_2_
  23.5 0.8 dynamic-slice_bitcast_fusion
  24.3 0.1 copy.14.refs_5_.gain_ref.refs_11_
  24.4 0.1 constant_dynamic-slice_fusion
  24.5 0.1 copy.20
  24.6 39.2 %all-to-all-done.refs_0_ = bf16[16,304,128]{2,1,0:T(8,128)(2,1)S(1)} async-done(((bf16[16,304,128]{2,1,0:T(8,128)(2,1)}), bf16[16,304,128]{2,1,0:T(8,128)(2,1)S(1)}, u32[]{:S(2)}, u32[]{:S(2)}) %all-to-all-start) | async-done | bytes 1245216 | tf_op jit(solution)/shard_map/all_to_all | solution.py:508
  63.8 6.4 %forward.1 = (f32[104,2048]{1,0:T(8,128)S(1)}, bf16[192,2048]{1,0:T(8,128)(2,1)S(1)}, bf16[16,16,128]{2,1,0:T(8,128)(2,1)}, bf16[384,768]{1,0:T(8,128)(2,1)S(1)}, bf16[96,1152]{1,0:T(8,128)(2,1)}) custom-call(bf16[16,304,128]{2,1,0:T(8,128)(2,1)S(1)} %all-to-all-done.refs_0_, f32[96,16]{1,0:T(8,128)S(1)} %pad.9.refs_1_, ...), custom_call_target="tpu_custom_call" | custom-call | tf_op jit(solution)/shard_map/forward/pallas_call | solution.py:497
  70.2 0.9 copy-done.3
  71.1 0.9 copy-done.6
  72.0 0.8 copy-done.7
  72.9 5.8 %all-to-all-start.1 = ((bf16[16,16,128]{2,1,0:T(8,128)(2,1)}), bf16[16,16,128]{2,1,0:T(8,128)(2,1)S(1)}, u32[]{:S(2)}, u32[]{:S(2)}) async-start(bf16[16,16,128]{2,1,0:T(8,128)(2,1)} %get-tuple-element.26), calls=%async_computation.1 | async-start | bytes 131072 | tf_op jit(solution)/shard_map/all_to_all | solution.py:508
  78.7 1.6 all-gather.6.cloned.1.call-done
  80.3 5.2 %inner.1 = (f32[96,2048]{1,0:T(8,128)}, bf16[16,16,128]{2,1,0:T(8,128)(2,1)}) custom-call(bf16[192,2048]{1,0:T(8,128)(2,1)} %copy-done.3, bf16[96,1152]{1,0:T(8,128)(2,1)} %weight_ref.1, bf16[2048,1152]{1,0:T(8,128)(2,1)} %bitcast.16, f32[96,1]{1,0:T(8,128)} %copy-done.4), custom_call_target="tpu_custom_call" | custom-call | tf_op jit(solution)/shard_map/inner/pallas_call | solution.py:497
  85.5 1.0 all-to-all-done.1.squares_ref
  86.5 4.8 %all-to-all-start.2 = ((bf16[16,16,128]{2,1,0:T(8,128)(2,1)}), bf16[16,16,128]{2,1,0:T(8,128)(2,1)S(1)}, u32[]{:S(2)}, u32[]{:S(2)}) async-start(bf16[16,16,128]{2,1,0:T(8,128)(2,1)} %get-tuple-element.29), calls=%async_computation.2 | async-start | bytes 131072 | tf_op jit(solution)/shard_map/all_to_all | solution.py:508
  91.3 5.2 %normed.1 = (bf16[16,96,128]{2,1,0:T(8,128)(2,1)}, f32[16,128]{1,0:T(8,128)}, bf16[1024,128]{1,0:T(8,128)(2,1)}, f32[96,128]{1,0:T(8,128)}) custom-call(bf16[192,2048]{1,0:T(8,128)(2,1)} %copy-done.3, f32[96,2048]{1,0:T(8,128)} %get-tuple-element.25.grad_normed_ref.refs_8_, bf16[16,16,128]{2,1,0:T(8,128)(2,1)} %copy-done.13, f32[96,1]{1,0:T(8,128)} %copy-done.4, ...), custom_call_target="tpu_custom_call" | custom-call | tf_op jit(solution)/shard_map/normed/pallas_call | solution.py:497
  96.5 2.6 %all-to-all-done.2.refs_10_ = bf16[16,16,128]{2,1,0:T(8,128)(2,1)S(1)} async-done(((bf16[16,16,128]{2,1,0:T(8,128)(2,1)}), bf16[16,16,128]{2,1,0:T(8,128)(2,1)S(1)}, u32[]{:S(2)}, u32[]{:S(2)}) %all-to-all-start.2) | async-done | bytes 65568 | tf_op jit(solution)/shard_map/all_to_all | solution.py:508
  99.1 13.2 %all-to-all-start.4 = ((bf16[32,32,128]{2,1,0:T(8,128)(2,1)}), bf16[32,32,128]{2,1,0:T(8,128)(2,1)S(1)}, u32[]{:S(2)}, u32[]{:S(2)}) async-start(bf16[32,32,128]{2,1,0:T(8,128)(2,1)} %bitcast.19), calls=%async_computation.4 | async-start | bytes 524288 | tf_op jit(solution)/shard_map/all_to_all | solution.py:508
  112.3 14.6 %backward.1 = (bf16[16,384,128]{2,1,0:T(8,128)(2,1)}, f32[16,128]{1,0:T(8,128)}) custom-call(bf16[16,304,128]{2,1,0:T(8,128)(2,1)} %copy-done.2, f32[96,16]{1,0:T(8,128)} %copy-done.9, s32[1,96]{1,0:T(1,128)} %copy-done.11, s32[96,1]{1,0:T(8,128)} %copy-done.8, f32[104,2048]{1,0:T(8,128)} %copy-done.6, bf16[192,2048]{1,0:T(8,128)(2,1)} %copy-done.3, ...), custom_call_target="tpu_custom_call" | custom-call | tf_op jit(solution)/shard_map/backward/pallas_call | solution.py:497
  126.9 4.4 %all-to-all-start.3 = ((bf16[16,384,128]{2,1,0:T(8,128)(2,1)}), bf16[16,384,128]{2,1,0:T(8,128)(2,1)S(1)}, u32[]{:S(2)}, u32[]{:S(2)}) async-start(bf16[16,384,128]{2,1,0:T(8,128)(2,1)} %get-tuple-element.31), calls=%async_computation.3 | async-start | bytes 3145728 | tf_op jit(solution)/shard_map/all_to_all | solution.py:508
  131.3 3.3 %collective-permute-start = (bf16[64,128]{1,0:T(8,128)(2,1)S(1)}, bf16[64,128]{1,0:T(8,128)(2,1)S(1)}, u32[]{:S(2)}, u32[]{:S(2)}) collective-permute-start(bf16[64,128]{1,0:T(8,128)(2,1)S(1)} %pack_sum.1.own_ref), channel_id=1, source_target_pairs={{0,16},{16,0},{32,48},{48,32},{64,80},{80,64},{96,112},{112,96},{1... | collective-permute-start | bytes 49160 | tf_op jit(solution)/shard_map/ppermute | solution.py:633
  134.6 1.2 collective-permute-done.got_ref
  135.8 4.1 %collective-permute-start.1 = (bf16[96,128]{1,0:T(8,128)(2,1)S(1)}, bf16[96,128]{1,0:T(8,128)(2,1)S(1)}, u32[]{:S(2)}, u32[]{:S(2)}) collective-permute-start(bf16[96,128]{1,0:T(8,128)(2,1)S(1)} %join.5.own_ref), channel_id=1, source_target_pairs={{0,32},{16,48},{32,0},{48,16},{64,96},{80,112},{96,64},{112,80},{1... | collective-permute-start | bytes 73736 | tf_op jit(solution)/shard_map/ppermute | solution.py:633
  140.0 1.6 collective-permute-done.1.got_ref
  141.6 7.4 %collective-permute-start.2 = (bf16[160,128]{1,0:T(8,128)(2,1)S(1)}, bf16[160,128]{1,0:T(8,128)(2,1)S(1)}, u32[]{:S(2)}, u32[]{:S(2)}) collective-permute-start(bf16[160,128]{1,0:T(8,128)(2,1)S(1)} %join.6.own_ref), channel_id=1, source_target_pairs={{0,64},{16,80},{32,96},{48,112},{64,0},{80,16},{96,32},{112,48},{1... | collective-permute-start | bytes 122888 | tf_op jit(solution)/shard_map/ppermute | solution.py:633
  149.0 1.7 collective-permute-done.2.got_ref
  150.7 3.1 %collective-permute-start.3 = (bf16[288,128]{1,0:T(8,128)(2,1)S(1)}, bf16[288,128]{1,0:T(8,128)(2,1)S(1)}, u32[]{:S(2)}, u32[]{:S(2)}) collective-permute-start(bf16[288,128]{1,0:T(8,128)(2,1)S(1)} %join.7.own_ref), channel_id=1, source_target_pairs={{0,128},{16,144},{32,160},{48,176},{64,192},{80,208},{96,224},{112... | collective-permute-start | bytes 221192 | tf_op jit(solution)/shard_map/ppermute | solution.py:633
  153.8 2.3 %collective-permute-done.3.got_ref = bf16[288,128]{1,0:T(8,128)(2,1)S(1)} collective-permute-done((bf16[288,128]{1,0:T(8,128)(2,1)S(1)}, bf16[288,128]{1,0:T(8,128)(2,1)S(1)}, u32[]{:S(2)}, u32[]{:S(2)}) %collective-permute-start.3) | collective-permute-done | bytes 73760 | tf_op jit(solution)/shard_map/ppermute | solution.py:633
  156.1 4.6 %collective-permute-start.4 = (bf16[544,128]{1,0:T(8,128)(2,1)S(1)}, bf16[544,128]{1,0:T(8,128)(2,1)S(1)}, u32[]{:S(2)}, u32[]{:S(2)}) collective-permute-start(bf16[544,128]{1,0:T(8,128)(2,1)S(1)} %join.8.own_ref), channel_id=1, source_target_pairs={{0,256},{16,272},{32,288},{48,304},{64,320},{80,336},{96,352},{112... | collective-permute-start | bytes 417800 | tf_op jit(solution)/shard_map/ppermute | solution.py:633
  160.7 3.0 %collective-permute-done.4.got_ref = bf16[544,128]{1,0:T(8,128)(2,1)S(1)} collective-permute-done((bf16[544,128]{1,0:T(8,128)(2,1)S(1)}, bf16[544,128]{1,0:T(8,128)(2,1)S(1)}, u32[]{:S(2)}, u32[]{:S(2)}) %collective-permute-start.4) | collective-permute-done | bytes 139296 | tf_op jit(solution)/shard_map/ppermute | solution.py:633
  163.7 6.0 %all-to-all-done.3.normed_ref.grad_ref._ = bf16[16,384,128]{2,1,0:T(8,128)(2,1)S(1)} async-done(((bf16[16,384,128]{2,1,0:T(8,128)(2,1)}), bf16[16,384,128]{2,1,0:T(8,128)(2,1)S(1)}, u32[]{:S(2)}, u32[]{:S(2)}) %all-to-all-start.3) | async-done | bytes 1572896 | tf_op jit(solution)/shard_map/all_to_all | solution.py:508
  169.7 0.7 spread.1
  170.4 5.7 %all-to-all-start.5 = ((f32[16,16,128]{2,1,0:T(8,128)}), f32[16,16,128]{2,1,0:T(8,128)S(1)}, u32[]{:S(2)}, u32[]{:S(2)}) async-start(f32[16,16,128]{2,1,0:T(8,128)} %spread.1), calls=%async_computation.5 | async-start | bytes 262144 | tf_op jit(solution)/shard_map/all_to_all | solution.py:508
  176.1 0.8 unpack.1
  177.0 4.9 %finish.1 = (bf16[128,1152]{1,0:T(8,128)(2,1)}, bf16[3,128,1536]{2,1,0:T(8,128)(2,1)}) custom-call(bf16[16,384,128]{2,1,0:T(8,128)(2,1)} %copy-done.1, bf16[16,384,128]{2,1,0:T(8,128)(2,1)} %copy-done.1, bf16[1536,1152]{1,0:T(8,128)(2,1)} %all-gather.4.cloned.1.call-done.weight_ref), custom_call_target="tpu_custom_call" | custom-call | tf_op jit(solution)/shard_map/finish/pallas_call | solution.py:497
  181.8 3.5 %all-to-all-done.5.small_ref = f32[16,16,128]{2,1,0:T(8,128)S(1)} async-done(((f32[16,16,128]{2,1,0:T(8,128)}), f32[16,16,128]{2,1,0:T(8,128)S(1)}, u32[]{:S(2)}, u32[]{:S(2)}) %all-to-all-start.5) | async-done | bytes 131104 | tf_op jit(solution)/shard_map/all_to_all | solution.py:508
  185.3 0.7 small.1
  186.0 0.6 reduce
  (37 shorter events, 0.2 us)
Async XLA Ops:
  7.2 17.2 %copy-start = (f32[9,1536]{1,0:T(8,128)S(1)}, f32[9,1536]{1,0:T(8,128)}, u32[]{:S(2)}) copy-start(f32[9,1536]{1,0:T(8,128)} %param.11) | copy-start | bytes 165892
  7.2 73.1 %all-gather.6.cloned.1.call-start = ((), (), s32[]{:S(2)}) async-start(), calls=%async_computation.7 | async-start | bytes 5013504 | tf_op jit(solution)/shard_map/all_gather | solution.py:520
  12.6 10.6 %copy-start.14 = (s32[48]{0:T(128)S(1)}, s32[48]{0:T(128)}, u32[]{:S(2)}) copy-start(s32[48]{0:T(128)} %param.12) | copy-start | bytes 580
  12.6 51.2 %copy-start.5 = (bf16[96,1152]{1,0:T(8,128)(2,1)S(1)}, bf16[96,1152]{1,0:T(8,128)(2,1)}, u32[]{:S(2)}) copy-start(bf16[96,1152]{1,0:T(8,128)(2,1)} %weight_ref.1) | copy-start | bytes 663556
  12.6 51.2 %all-to-all-start = ((bf16[16,304,128]{2,1,0:T(8,128)(2,1)}), bf16[16,304,128]{2,1,0:T(8,128)(2,1)S(1)}, u32[]{:S(2)}, u32[]{:S(2)}) async-start(bf16[16,304,128]{2,1,0:T(8,128)(2,1)} %prepare.1), calls=%async_computation | async-start | bytes 2490368 | tf_op jit(solution)/shard_map/all_to_all | solution.py:508
  23.1 153.8 %all-gather.4.cloned.1.call-start = ((), (), s32[]{:S(2)}) async-start(), calls=%async_computation.6 | async-start | bytes 3760128 | tf_op jit(solution)/shard_map/all_gather | solution.py:557
  23.4 62.1 %copy-start.8 = (s32[96,1]{1,0:T(8,128)}, s32[96,1]{1,0:T(8,128)S(1)}, u32[]{:S(2)}) copy-start(s32[96,1]{1,0:T(8,128)S(1)} %broadcast_in_dim_reshape.9.refs_4_.refs_3_) | copy-start | bytes 1156
  23.5 62.0 %copy-start.11 = (s32[1,96]{1,0:T(1,128)}, s32[1,96]{1,0:T(1,128)S(1)}, u32[]{:S(2)}) copy-start(s32[1,96]{1,0:T(1,128)S(1)} %broadcast_in_dim_reshape.7.refs_2_) | copy-start | bytes 1156
  24.4 55.9 %copy-start.4 = (f32[96,1]{1,0:T(8,128)}, f32[96,1]{1,0:T(8,128)S(1)}, u32[]{:S(2)}) copy-start(f32[96,1]{1,0:T(8,128)S(1)} %copy.14.refs_5_.gain_ref.refs_11_) | copy-start | bytes 1156
  24.6 60.9 %copy-start.9 = (f32[96,16]{1,0:T(8,128)}, f32[96,16]{1,0:T(8,128)S(1)}, u32[]{:S(2)}) copy-start(f32[96,16]{1,0:T(8,128)S(1)} %pad.9.refs_1_) | copy-start | bytes 18436
  63.8 21.7 %copy-start.2 = (bf16[16,304,128]{2,1,0:T(8,128)(2,1)}, bf16[16,304,128]{2,1,0:T(8,128)(2,1)S(1)}, u32[]{:S(2)}) copy-start(bf16[16,304,128]{2,1,0:T(8,128)(2,1)S(1)} %all-to-all-done.refs_0_) | copy-start | bytes 3735556
  70.2 0.9 copy-start.3
  71.1 0.9 copy-start.6
  72.0 0.8 copy-start.7
  72.9 13.6 %all-to-all-start.1 = ((bf16[16,16,128]{2,1,0:T(8,128)(2,1)}), bf16[16,16,128]{2,1,0:T(8,128)(2,1)S(1)}, u32[]{:S(2)}, u32[]{:S(2)}) async-start(bf16[16,16,128]{2,1,0:T(8,128)(2,1)} %get-tuple-element.26), calls=%async_computation.1 | async-start | bytes 131072 | tf_op jit(solution)/shard_map/all_to_all | solution.py:508
  86.5 4.8 %copy-start.13 = (bf16[16,16,128]{2,1,0:T(8,128)(2,1)}, bf16[16,16,128]{2,1,0:T(8,128)(2,1)S(1)}, u32[]{:S(2)}) copy-start(bf16[16,16,128]{2,1,0:T(8,128)(2,1)S(1)} %all-to-all-done.1.squares_ref) | copy-start | bytes 196612
  86.5 12.6 %all-to-all-start.2 = ((bf16[16,16,128]{2,1,0:T(8,128)(2,1)}), bf16[16,16,128]{2,1,0:T(8,128)(2,1)S(1)}, u32[]{:S(2)}, u32[]{:S(2)}) async-start(bf16[16,16,128]{2,1,0:T(8,128)(2,1)} %get-tuple-element.29), calls=%async_computation.2 | async-start | bytes 131072 | tf_op jit(solution)/shard_map/all_to_all | solution.py:508
  99.1 13.2 %copy-start.12 = (bf16[16,16,128]{2,1,0:T(8,128)(2,1)}, bf16[16,16,128]{2,1,0:T(8,128)(2,1)S(1)}, u32[]{:S(2)}) copy-start(bf16[16,16,128]{2,1,0:T(8,128)(2,1)S(1)} %all-to-all-done.2.refs_10_) | copy-start | bytes 196612
  99.1 27.8 %all-to-all-start.4 = ((bf16[32,32,128]{2,1,0:T(8,128)(2,1)}), bf16[32,32,128]{2,1,0:T(8,128)(2,1)S(1)}, u32[]{:S(2)}, u32[]{:S(2)}) async-start(bf16[32,32,128]{2,1,0:T(8,128)(2,1)} %bitcast.19), calls=%async_computation.4 | async-start | bytes 524288 | tf_op jit(solution)/shard_map/all_to_all | solution.py:508
  126.9 4.4 %copy-start.10 = (f32[16,128]{1,0:T(8,128)S(1)}, f32[16,128]{1,0:T(8,128)}, u32[]{:S(2)}) copy-start(f32[16,128]{1,0:T(8,128)} %get-tuple-element.36.small_ref) | copy-start | bytes 24580
  126.9 42.8 %all-to-all-start.3 = ((bf16[16,384,128]{2,1,0:T(8,128)(2,1)}), bf16[16,384,128]{2,1,0:T(8,128)(2,1)S(1)}, u32[]{:S(2)}, u32[]{:S(2)}) async-start(bf16[16,384,128]{2,1,0:T(8,128)(2,1)} %get-tuple-element.31), calls=%async_computation.3 | async-start | bytes 3145728 | tf_op jit(solution)/shard_map/all_to_all | solution.py:508
  131.3 4.5 %collective-permute-start = (bf16[64,128]{1,0:T(8,128)(2,1)S(1)}, bf16[64,128]{1,0:T(8,128)(2,1)S(1)}, u32[]{:S(2)}, u32[]{:S(2)}) collective-permute-start(bf16[64,128]{1,0:T(8,128)(2,1)S(1)} %pack_sum.1.own_ref), channel_id=1, source_target_pairs={{0,16},{16,0},{32,48},{48,32},{64,80},{80,64},{96,112},{112,96},{1... | collective-permute-start | bytes 49160 | tf_op jit(solution)/shard_map/ppermute | solution.py:633
  135.8 5.8 %collective-permute-start.1 = (bf16[96,128]{1,0:T(8,128)(2,1)S(1)}, bf16[96,128]{1,0:T(8,128)(2,1)S(1)}, u32[]{:S(2)}, u32[]{:S(2)}) collective-permute-start(bf16[96,128]{1,0:T(8,128)(2,1)S(1)} %join.5.own_ref), channel_id=1, source_target_pairs={{0,32},{16,48},{32,0},{48,16},{64,96},{80,112},{96,64},{112,80},{1... | collective-permute-start | bytes 73736 | tf_op jit(solution)/shard_map/ppermute | solution.py:633
  141.6 9.1 %collective-permute-start.2 = (bf16[160,128]{1,0:T(8,128)(2,1)S(1)}, bf16[160,128]{1,0:T(8,128)(2,1)S(1)}, u32[]{:S(2)}, u32[]{:S(2)}) collective-permute-start(bf16[160,128]{1,0:T(8,128)(2,1)S(1)} %join.6.own_ref), channel_id=1, source_target_pairs={{0,64},{16,80},{32,96},{48,112},{64,0},{80,16},{96,32},{112,48},{1... | collective-permute-start | bytes 122888 | tf_op jit(solution)/shard_map/ppermute | solution.py:633
  150.7 5.4 %collective-permute-start.3 = (bf16[288,128]{1,0:T(8,128)(2,1)S(1)}, bf16[288,128]{1,0:T(8,128)(2,1)S(1)}, u32[]{:S(2)}, u32[]{:S(2)}) collective-permute-start(bf16[288,128]{1,0:T(8,128)(2,1)S(1)} %join.7.own_ref), channel_id=1, source_target_pairs={{0,128},{16,144},{32,160},{48,176},{64,192},{80,208},{96,224},{112... | collective-permute-start | bytes 221192 | tf_op jit(solution)/shard_map/ppermute | solution.py:633
  156.1 7.6 %collective-permute-start.4 = (bf16[544,128]{1,0:T(8,128)(2,1)S(1)}, bf16[544,128]{1,0:T(8,128)(2,1)S(1)}, u32[]{:S(2)}, u32[]{:S(2)}) collective-permute-start(bf16[544,128]{1,0:T(8,128)(2,1)S(1)} %join.8.own_ref), channel_id=1, source_target_pairs={{0,256},{16,272},{32,288},{48,304},{64,320},{80,336},{96,352},{112... | collective-permute-start | bytes 417800 | tf_op jit(solution)/shard_map/ppermute | solution.py:633
  169.7 7.3 %copy-start.1 = (bf16[16,384,128]{2,1,0:T(8,128)(2,1)}, bf16[16,384,128]{2,1,0:T(8,128)(2,1)S(1)}, u32[]{:S(2)}) copy-start(bf16[16,384,128]{2,1,0:T(8,128)(2,1)S(1)} %all-to-all-done.3.normed_ref.grad_ref._) | copy-start | bytes 4718596
  170.4 14.9 %all-to-all-start.5 = ((f32[16,16,128]{2,1,0:T(8,128)}), f32[16,16,128]{2,1,0:T(8,128)S(1)}, u32[]{:S(2)}, u32[]{:S(2)}) async-start(f32[16,16,128]{2,1,0:T(8,128)} %spread.1), calls=%async_computation.5 | async-start | bytes 262144 | tf_op jit(solution)/shard_map/all_to_all | solution.py:508
Sparse Core Ops, SparseCore 0:
  10.1 70.0 all-gather.5
  82.4 44.2 all-gather.3

commit v5 on v4

--- a/solution.py
+++ b/solution.py
@@ -166,17 +166,15 @@
 
 def prepare_kernel(projected_ref, packing_ref, out_ref):
     groups = out_ref.shape[0]
-    width = projected_ref.shape[2] // groups
-    turned = jnp.transpose(projected_ref[0])
-    here = pl.ds(pl.multiple_of(pl.program_id(0) * width, 16), width)
+    parts, tokens, width_all = projected_ref.shape
+    width = width_all // groups
+    for part in range(parts):
+        turned = jnp.transpose(projected_ref[part])
+        for g in range(groups):
+            out_ref[g, pl.ds(part * width, width), :] = turned[g * width : (g + 1) * width]
+    rows = packing_ref[...].astype(f32).astype(bf16)
     for g in range(groups):
-        out_ref[g, here, :] = turned[g * width : (g + 1) * width]
-
-    @pl.when(pl.program_id(0) == 0)
-    def _():
-        rows = packing_ref[...].astype(f32).astype(bf16)
-        for g in range(groups):
-            out_ref[g, pl.ds(out_ref.shape[1] - 16, 16), :] = rows
+        out_ref[g, pl.ds(parts * width, 16), :] = rows
 
 
 def finish_kernel(normed_ref, grad_ref, weight_ref, block_ref, grad_out, turned_ref):
@@ -285,49 +283,34 @@
 
 
 def normed_kernel(attention_ref, grad_normed_ref, squares_ref, gain_ref, cotangent_ref,
-                  normed_ref, inverse_ref, weight_ref, gain_out, rows_ref, total_ref, gain_sum_ref):
-    step = pl.program_id(0)
+                  normed_ref, inverse_ref, weight_ref, gain_out):
     width, tokens = attention_ref.shape
     chunks = tokens // CHUNK
     groups = squares_ref.shape[0]
     gain = gain_ref[...]
-
-    @pl.when(step == 0)
-    def _():
-        squares = jnp.sum(squares_ref[...].astype(f32), axis=0)
-        inverse = lax.rsqrt(squares * (1.0 / (width * groups)) + epsilon)
-        inverse_ref[...] = inverse
-        for i in range(groups):
-            rows_ref[i] = inverse[i : i + 1]
-        total_ref[...] = jnp.zeros_like(total_ref)
-        gain_sum_ref[...] = jnp.zeros_like(gain_sum_ref)
-
-    weight, gain_sum = total_ref[...], gain_sum_ref[...]
+    squares = jnp.sum(squares_ref[...].astype(f32), axis=0)
+    inverse = lax.rsqrt(squares * (1.0 / (width * groups)) + epsilon)
+    inverse_ref[...] = inverse
+    weight = gain_sum = None
     for j in range(chunks):
         lanes = pl.ds(j * CHUNK, CHUNK)
-        first = (step * chunks + j) * 2
-        inv_rms = jnp.concatenate([rows_ref[first], rows_ref[first + 1]], axis=1)
+        inv_rms = tokens_of(inverse, j)
         attention = attention_ref[:, lanes].astype(f32)
         normed = (attention * gain * inv_rms).astype(bf16)
-        gain_sum = gain_sum + grad_normed_ref[:, lanes] * attention * inv_rms
+        gain_sum = add(gain_sum, grad_normed_ref[:, lanes] * attention * inv_rms)
         for part in range(CHUNK // LANES):
             normed_ref[2 * j + part] = normed[:, part * LANES : (part + 1) * LANES]
-        weight = weight + dot(normed, cotangent_ref[pl.ds(j * CHUNK, CHUNK), :])
-    total_ref[...] = weight
-    gain_sum_ref[...] = gain_sum
-
-    @pl.when(step == pl.num_programs(0) - 1)
-    def _():
-        total = jnp.sum(gain_sum_ref[...], axis=1, keepdims=True)
-        gain_out[...] = jnp.broadcast_to(total, gain_out.shape)
-        across = total_ref.shape[1] // LANES
-        for r in range(width // 16):
-            for c in range(across):
-                weight_ref[pl.ds((r * across + c) * 16, 16), :] = total_ref[
-                    pl.ds(r * 16, 16), pl.ds(c * LANES, LANES)
-                ].astype(bf16)
-        used = width * across
-        weight_ref[used:, :] = jnp.zeros((weight_ref.shape[0] - used, LANES), bf16)
+        weight = add(weight, dot(normed, cotangent_ref[pl.ds(j * CHUNK, CHUNK), :]))
+    gain_out[...] = jnp.broadcast_to(jnp.sum(gain_sum, axis=1, keepdims=True), gain_out.shape)
+    across = weight.shape[1] // LANES
+    weight = weight.astype(bf16)
+    for r in range(width // 16):
+        for c in range(across):
+            weight_ref[pl.ds((r * across + c) * 16, 16), :] = weight[
+                r * 16 : (r + 1) * 16, c * LANES : (c + 1) * LANES
+            ]
+    used = width * across
+    weight_ref[used:, :] = jnp.zeros((weight_ref.shape[0] - used, LANES), bf16)
 
 
 def backward_kernel(heads, x_ref, taps_ref, seed_row_ref, seed_column_ref, ratio_ref, half_ref,
@@ -464,33 +447,38 @@
     split_small(whole_small(own_ref, rows) + whole_small(got_ref, rows), out_ref, 2 * rows)
 
 
-def unpack_kernel(packs, pack_ref, gathered_ref, weight_ref):
-    total = gathered_ref.shape[0] - 32
-    rows = total // packs
+def unpack_kernel(packs, pack_ref, own_ref, got_ref, weight_ref, small_ref, blocks_ref):
+    half = own_ref.shape[0] - 32
+    rows = 2 * half // packs
+    blocks_ref[pl.ds(0, half), :] = own_ref[pl.ds(0, half), :]
+    blocks_ref[pl.ds(half, half), :] = got_ref[pl.ds(0, half), :]
     width, features_out = weight_ref.shape
     across = features_out // LANES
     for r in range(width // 16):
         for c in range(across):
             block, row = divmod((r * across + c) * 16, rows)
             place = pl.multiple_of((pack_ref[0] ^ block) * rows + row, 16)
-            weight_ref[pl.ds(r * 16, 16), pl.ds(c * LANES, LANES)] = gathered_ref[
+            weight_ref[pl.ds(r * 16, 16), pl.ds(c * LANES, LANES)] = blocks_ref[
                 pl.ds(place, 16), :
             ].astype(f32)
-
-
-def spread_kernel(gathered_ref, _, small_ref):
-    small = whole_small(gathered_ref, gathered_ref.shape[0] - 32)
+    small_ref[...] = whole_small(own_ref, half) + whole_small(got_ref, half)
+
+
+def spread_kernel(total_ref, _, small_ref):
+    small = total_ref[...]
     for peer in range(small_ref.shape[0]):
         small_ref[peer] = small
 
 
-def small_kernel(small_ref, taps_ref, gain_ref):
+def small_kernel(small_ref, taps_ref, gain_out, gain_ref):
     groups = small_ref.shape[0]
     width = taps_ref.shape[1] // groups
     for g in range(groups):
         here = pl.ds(g * width, width)
         taps_ref[:, here] = small_ref[g, pl.ds(0, 9), pl.ds(0, width)]
         gain_ref[:, here] = small_ref[g, pl.ds(9, 1), pl.ds(0, width)]
+    for r in range(gain_out.shape[0]):
+        gain_out[pl.ds(r, 1), :] = gain_ref[:, pl.ds(r * LANES, LANES)]
 
 
 def call(kernel, name, out_shapes, operands, scratch=(), vmem=VMEM, **more):
@@ -523,13 +511,6 @@
         "prepare",
         [((groups, 3 * width + 16, tokens), bf16)],
         (projected[0].transpose(1, 0, 2), jnp.pad(packing[0], ((0, 11), (0, 0)))),
-        vmem=ALL_VMEM,
-        grid=(3,),
-        in_specs=[
-            pl.BlockSpec((1, tokens, width_all), lambda i: (i, 0, 0)),
-            pl.BlockSpec((16, tokens), lambda i: (0, 0)),
-        ],
-        out_specs=[pl.BlockSpec((groups, 3 * width + 16, tokens), lambda i: (0, 0, 0))],
     )[0]
     seeds = jnp.repeat(lax.dynamic_slice_in_dim(feature_seeds, member * heads, heads, 0), HEAD)
     taps = jnp.pad(
@@ -555,8 +536,8 @@
     )
     squares = swap(squares, "seq")
     weight_all = lax.all_gather(weight_local, "seq", axis=0, tiled=True)
-    steps = groups // 4
-    block = 4 * LANES
+    steps = groups // 8
+    block = 8 * LANES
     grad_normed, inner = call(
         inner_kernel,
         "inner",
@@ -591,24 +572,19 @@
         ],
         (half, grad_normed, squares, gain, cotangent_all),
         vmem=ALL_VMEM,
-        grid=(steps,),
+        grid=(1,),
         in_specs=[
-            pl.BlockSpec((width, block), lambda i: (0, i)),
-            pl.BlockSpec((width, block), lambda i: (0, i)),
+            pl.BlockSpec((width, all_tokens), lambda i: (0, 0)),
+            pl.BlockSpec((width, all_tokens), lambda i: (0, 0)),
             pl.BlockSpec((groups, groups, LANES), lambda i: (0, 0, 0)),
             pl.BlockSpec((width, 1), lambda i: (0, 0)),
-            pl.BlockSpec((block, features_out), lambda i: (i, 0)),
+            pl.BlockSpec((all_tokens, features_out), lambda i: (0, 0)),
         ],
         out_specs=[
-            pl.BlockSpec((groups // steps, width, LANES), lambda i: (i, 0, 0)),
+            pl.BlockSpec((groups, width, LANES), lambda i: (0, 0, 0)),
             pl.BlockSpec((groups, LANES), lambda i: (0, 0)),
             pl.BlockSpec((1024, LANES), lambda i: (0, 0)),
             pl.BlockSpec((width, LANES), lambda i: (0, 0)),
-        ],
-        scratch=[
-            pltpu.VMEM((groups, 1, LANES), f32),
-            pltpu.VMEM((width, features_out), f32),
-            pltpu.VMEM((width, CHUNK), f32),
         ],
     )
     weight_parts = swap(weight_tiles.reshape(packs, 1024 // packs, LANES), "dp")
@@ -629,25 +605,28 @@
         (weight_parts, small),
     )[0]
     distance = 1
-    while distance < packs:
+    while True:
         got = lax.ppermute(joined, "dp", [(i, i ^ distance) for i in range(packs)])
+        distance *= 2
+        if distance == packs:
+            break
         rows = joined.shape[0] - 32
         joined = call(
             join_kernel, "join", [((2 * rows + 32, LANES), bf16)], (joined, got)
         )[0]
-        distance *= 2
-    weight_grad = call(
+    weight_grad, total = call(
         lambda *refs: unpack_kernel(packs, *refs),
         "unpack",
-        [((width, features_out), f32)],
-        (lax.axis_index("dp").astype(jnp.int32)[None], joined),
-        in_specs=[pl.BlockSpec(memory_space=pltpu.SMEM), vmem],
-    )[0]
+        [((width, features_out), f32), ((16, LANES), f32)],
+        (lax.axis_index("dp").astype(jnp.int32)[None], joined, got),
+        in_specs=[pl.BlockSpec(memory_space=pltpu.SMEM), vmem, vmem],
+        scratch=[pltpu.VMEM((1024, LANES), bf16)],
+    )
     small = call(
         spread_kernel,
         "spread",
         [((groups, 16, LANES), f32)],
-        (joined, back),
+        (total, back),
         in_specs=[vmem, anywhere],
     )[0]
     small = swap(small, "seq")
@@ -672,7 +651,11 @@
     )
     grad_tokens = grads.transpose(1, 0, 2)
     taps_grad, gain_grad = call(
-        small_kernel, "small", [((9, width_all), f32), ((1, width_all), f32)], (small,)
+        small_kernel,
+        "small",
+        [((9, width_all), f32), ((width_all // LANES, LANES), f32)],
+        (small,),
+        scratch=[pltpu.VMEM((1, width_all), f32)],
     )
     return block_out[None], grad_tokens[None], weight_grad, gain_grad.reshape(-1), taps_grad
 

time: 195 us -> 191 us (0.979)
  Pallas kernels: 42.1 us -> 38.5 us
    pallas_call x15 -> x14, Pallas kernels: 42.1 us -> 38.5 us  [call(): pl.pallas_call(kernel, name=name, out_shape=[jax.ShapeDtypeStruct(shape,...]
    unnamed x32 -> x34, local copies, waits for them, and re-layouts: 3.48 us -> 4.73 us
  transfers between devices with their start and end apart: 13 -> 13, of which waited for: 11 -> 11; matrix products, arithmetic and copies ran while one was open for 1% -> 1% of each run, Pallas kernels for 21% -> 20%
where the time goes in v5:
time: 191 us; the launch traced here: 190 us
  starting transfers between devices  65.9 us (35%)
  waiting for transfers between devices  65.5 us (34%)
  Pallas kernels  38.5 us (20%)
  between operations  14.2 us (7%)
  local copies, waits for them, and re-layouts  6.04 us (3%)
    all_to_all x6, waiting for transfers between devices, swap(): return lax.all_to_all(blocks, axis, split_axis=0, concat_axis=0, tiled=True)  53.1 us
    all_to_all x6, starting transfers between devices, swap(): return lax.all_to_all(blocks, axis, split_axis=0, concat_axis=0, tiled=True)  43.2 us
    pallas_call x14, Pallas kernels, call(): pl.pallas_call(kernel, name=name, out_shape=[jax.ShapeDtypeStruct(shape,...  38.5 us
    ppermute x5, starting transfers between devices, local(): got = lax.ppermute(joined, 'dp', [(i, i ^ distance) for i in range(packs)])  22.6 us
    ppermute x5, waiting for transfers between devices, local(): got = lax.ppermute(joined, 'dp', [(i, i ^ distance) for i in range(packs)])  9.77 us
    unnamed x34, local copies, waits for them, and re-layouts  4.73 us
  transfers between devices with their start and end apart: 13, of which 11 were waited for; matrix products, arithmetic and copies ran while one was open for 1% of the time, Pallas kernels for 20%

profile of v5, /device:TPU:1, one launch (start us, length us, event | category | flops | bytes accessed | tf_op | source)
XLA Modules:
  0.0 190.1 jit_solution(927374233028196806)
XLA Ops:
  7.2 0.0 all-gather.6.cloned.1.call-start
  7.2 0.7 all-gather.6.cloned.1.call-update
  7.9 0.7 copy.22
  8.6 1.3 copy-done.5
  9.9 1.4 prepare.1
  11.3 10.5 %all-to-all-start = ((bf16[16,304,128]{2,1,0:T(8,128)(2,1)}), bf16[16,304,128]{2,1,0:T(8,128)(2,1)S(1)}, u32[]{:S(2)}, u32[]{:S(2)}) async-start(bf16[16,304,128]{2,1,0:T(8,128)(2,1)} %prepare.1), calls=%async_computation | async-start | bytes 2490368 | tf_op jit(solution)/shard_map/all_to_all | solution.py:496
  21.8 0.0 all-gather.4.cloned.1.call-start
  21.9 0.1 dynamic_slice.10
  22.0 0.1 broadcast_in_dim.15
  22.0 0.1 broadcast_in_dim_reshape.9.refs_4_.refs_3_
  22.2 0.1 broadcast_in_dim_reshape.7.refs_2_
  22.2 0.8 dynamic-slice_bitcast_fusion
  23.0 0.1 copy.14.refs_5_.gain_ref.refs_11_
  23.1 0.1 constant_dynamic-slice_fusion
  23.2 0.1 copy.20
  23.3 38.8 %all-to-all-done.refs_0_ = bf16[16,304,128]{2,1,0:T(8,128)(2,1)S(1)} async-done(((bf16[16,304,128]{2,1,0:T(8,128)(2,1)}), bf16[16,304,128]{2,1,0:T(8,128)(2,1)S(1)}, u32[]{:S(2)}, u32[]{:S(2)}) %all-to-all-start) | async-done | bytes 1245216 | tf_op jit(solution)/shard_map/all_to_all | solution.py:496
  62.2 6.4 %forward.1 = (f32[104,2048]{1,0:T(8,128)S(1)}, bf16[192,2048]{1,0:T(8,128)(2,1)S(1)}, bf16[16,16,128]{2,1,0:T(8,128)(2,1)}, bf16[384,768]{1,0:T(8,128)(2,1)S(1)}, bf16[96,1152]{1,0:T(8,128)(2,1)}) custom-call(bf16[16,304,128]{2,1,0:T(8,128)(2,1)S(1)} %all-to-all-done.refs_0_, f32[96,16]{1,0:T(8,128)S(1)} %pad.9.refs_1_, ...), custom_call_target="tpu_custom_call" | custom-call | tf_op jit(solution)/shard_map/forward/pallas_call | solution.py:485
  68.6 0.9 copy-done.3
  69.5 0.9 copy-done.7
  70.4 0.8 copy-done.8
  71.2 0.0 all-gather.4.cloned.1.call-update
  71.2 5.9 %all-to-all-start.1 = ((bf16[16,16,128]{2,1,0:T(8,128)(2,1)}), bf16[16,16,128]{2,1,0:T(8,128)(2,1)S(1)}, u32[]{:S(2)}, u32[]{:S(2)}) async-start(bf16[16,16,128]{2,1,0:T(8,128)(2,1)} %get-tuple-element.28), calls=%async_computation.1 | async-start | bytes 131072 | tf_op jit(solution)/shard_map/all_to_all | solution.py:496
  77.1 1.9 all-gather.6.cloned.1.call-done
  79.0 4.3 %inner.1 = (f32[96,2048]{1,0:T(8,128)}, bf16[16,16,128]{2,1,0:T(8,128)(2,1)}) custom-call(bf16[192,2048]{1,0:T(8,128)(2,1)} %copy-done.3, bf16[96,1152]{1,0:T(8,128)(2,1)} %weight_ref.1, bf16[2048,1152]{1,0:T(8,128)(2,1)} %bitcast.18, f32[96,1]{1,0:T(8,128)} %copy-done.4), custom_call_target="tpu_custom_call" | custom-call | tf_op jit(solution)/shard_map/inner/pallas_call | solution.py:485
  83.4 1.5 all-to-all-done.1.squares_ref
  84.9 3.9 %all-to-all-start.2 = ((bf16[16,16,128]{2,1,0:T(8,128)(2,1)}), bf16[16,16,128]{2,1,0:T(8,128)(2,1)S(1)}, u32[]{:S(2)}, u32[]{:S(2)}) async-start(bf16[16,16,128]{2,1,0:T(8,128)(2,1)} %get-tuple-element.31), calls=%async_computation.2 | async-start | bytes 131072 | tf_op jit(solution)/shard_map/all_to_all | solution.py:496
  88.8 4.4 %normed.1 = (bf16[16,96,128]{2,1,0:T(8,128)(2,1)}, f32[16,128]{1,0:T(8,128)}, bf16[1024,128]{1,0:T(8,128)(2,1)}, f32[96,128]{1,0:T(8,128)}) custom-call(bf16[192,2048]{1,0:T(8,128)(2,1)} %copy-done.3, f32[96,2048]{1,0:T(8,128)} %get-tuple-element.27.grad_normed_ref.refs_8_, bf16[16,16,128]{2,1,0:T(8,128)(2,1)} %copy-done.14, f32[96,1]{1,0:T(8,128)} %copy-done.4, ...), custom_call_target="tpu_custom_call" | custom-call | tf_op jit(solution)/shard_map/normed/pallas_call | solution.py:485
  93.2 3.4 %all-to-all-done.2.refs_10_ = bf16[16,16,128]{2,1,0:T(8,128)(2,1)S(1)} async-done(((bf16[16,16,128]{2,1,0:T(8,128)(2,1)}), bf16[16,16,128]{2,1,0:T(8,128)(2,1)S(1)}, u32[]{:S(2)}, u32[]{:S(2)}) %all-to-all-start.2) | async-done | bytes 65568 | tf_op jit(solution)/shard_map/all_to_all | solution.py:496
  96.6 12.2 %all-to-all-start.4 = ((bf16[32,32,128]{2,1,0:T(8,128)(2,1)}), bf16[32,32,128]{2,1,0:T(8,128)(2,1)S(1)}, u32[]{:S(2)}, u32[]{:S(2)}) async-start(bf16[32,32,128]{2,1,0:T(8,128)(2,1)} %bitcast.20), calls=%async_computation.4 | async-start | bytes 524288 | tf_op jit(solution)/shard_map/all_to_all | solution.py:496
  108.8 14.6 %backward.1 = (bf16[16,384,128]{2,1,0:T(8,128)(2,1)}, f32[16,128]{1,0:T(8,128)}) custom-call(bf16[16,304,128]{2,1,0:T(8,128)(2,1)} %copy-done.2, f32[96,16]{1,0:T(8,128)} %copy-done.10, s32[1,96]{1,0:T(1,128)} %copy-done.12, s32[96,1]{1,0:T(8,128)} %copy-done.9, f32[104,2048]{1,0:T(8,128)} %copy-done.7, bf16[192,2048]{1,0:T(8,128)(2,1)} %copy-done.3, ...), custom_call_target="tpu_custom_call" | custom-call | tf_op jit(solution)/shard_map/backward/pallas_call | solution.py:485
  123.5 4.2 %all-to-all-start.3 = ((bf16[16,384,128]{2,1,0:T(8,128)(2,1)}), bf16[16,384,128]{2,1,0:T(8,128)(2,1)S(1)}, u32[]{:S(2)}, u32[]{:S(2)}) async-start(bf16[16,384,128]{2,1,0:T(8,128)(2,1)} %get-tuple-element.33), calls=%async_computation.3 | async-start | bytes 3145728 | tf_op jit(solution)/shard_map/all_to_all | solution.py:496
  127.8 3.3 %collective-permute-start = (bf16[64,128]{1,0:T(8,128)(2,1)S(1)}, bf16[64,128]{1,0:T(8,128)(2,1)S(1)}, u32[]{:S(2)}, u32[]{:S(2)}) collective-permute-start(bf16[64,128]{1,0:T(8,128)(2,1)S(1)} %pack_sum.1.own_ref), channel_id=1, source_target_pairs={{0,16},{16,0},{32,48},{48,32},{64,80},{80,64},{96,112},{112,96},{1... | collective-permute-start | bytes 49160 | tf_op jit(solution)/shard_map/ppermute | solution.py:609
  131.1 1.2 collective-permute-done.got_ref
  132.3 4.2 %collective-permute-start.1 = (bf16[96,128]{1,0:T(8,128)(2,1)S(1)}, bf16[96,128]{1,0:T(8,128)(2,1)S(1)}, u32[]{:S(2)}, u32[]{:S(2)}) collective-permute-start(bf16[96,128]{1,0:T(8,128)(2,1)S(1)} %join.4.own_ref), channel_id=1, source_target_pairs={{0,32},{16,48},{32,0},{48,16},{64,96},{80,112},{96,64},{112,80},{1... | collective-permute-start | bytes 73736 | tf_op jit(solution)/shard_map/ppermute | solution.py:609
  136.5 1.6 collective-permute-done.1.got_ref
  138.1 7.4 %collective-permute-start.2 = (bf16[160,128]{1,0:T(8,128)(2,1)S(1)}, bf16[160,128]{1,0:T(8,128)(2,1)S(1)}, u32[]{:S(2)}, u32[]{:S(2)}) collective-permute-start(bf16[160,128]{1,0:T(8,128)(2,1)S(1)} %join.5.own_ref), channel_id=1, source_target_pairs={{0,64},{16,80},{32,96},{48,112},{64,0},{80,16},{96,32},{112,48},{1... | collective-permute-start | bytes 122888 | tf_op jit(solution)/shard_map/ppermute | solution.py:609
  145.5 1.7 collective-permute-done.2.got_ref
  147.2 3.1 %collective-permute-start.3 = (bf16[288,128]{1,0:T(8,128)(2,1)S(1)}, bf16[288,128]{1,0:T(8,128)(2,1)S(1)}, u32[]{:S(2)}, u32[]{:S(2)}) collective-permute-start(bf16[288,128]{1,0:T(8,128)(2,1)S(1)} %join.6.own_ref), channel_id=1, source_target_pairs={{0,128},{16,144},{32,160},{48,176},{64,192},{80,208},{96,224},{112... | collective-permute-start | bytes 221192 | tf_op jit(solution)/shard_map/ppermute | solution.py:609
  150.3 2.3 %collective-permute-done.3.got_ref = bf16[288,128]{1,0:T(8,128)(2,1)S(1)} collective-permute-done((bf16[288,128]{1,0:T(8,128)(2,1)S(1)}, bf16[288,128]{1,0:T(8,128)(2,1)S(1)}, u32[]{:S(2)}, u32[]{:S(2)}) %collective-permute-start.3) | collective-permute-done | bytes 73760 | tf_op jit(solution)/shard_map/ppermute | solution.py:609
  152.6 4.6 %collective-permute-start.4 = (bf16[544,128]{1,0:T(8,128)(2,1)S(1)}, bf16[544,128]{1,0:T(8,128)(2,1)S(1)}, u32[]{:S(2)}, u32[]{:S(2)}) collective-permute-start(bf16[544,128]{1,0:T(8,128)(2,1)S(1)} %join.7.refs_1_), channel_id=1, source_target_pairs={{0,256},{16,272},{32,288},{48,304},{64,320},{80,336},{96,352},{112... | collective-permute-start | bytes 417800 | tf_op jit(solution)/shard_map/ppermute | solution.py:609
  157.3 3.0 %collective-permute-done.4.refs_2_ = bf16[544,128]{1,0:T(8,128)(2,1)S(1)} collective-permute-done((bf16[544,128]{1,0:T(8,128)(2,1)S(1)}, bf16[544,128]{1,0:T(8,128)(2,1)S(1)}, u32[]{:S(2)}, u32[]{:S(2)}) %collective-permute-start.4) | collective-permute-done | bytes 139296 | tf_op jit(solution)/shard_map/ppermute | solution.py:609
  160.2 0.8 unpack.1
  161.1 5.1 %all-to-all-done.3.normed_ref.grad_ref._ = bf16[16,384,128]{2,1,0:T(8,128)(2,1)S(1)} async-done(((bf16[16,384,128]{2,1,0:T(8,128)(2,1)}), bf16[16,384,128]{2,1,0:T(8,128)(2,1)S(1)}, u32[]{:S(2)}, u32[]{:S(2)}) %all-to-all-start.3) | async-done | bytes 1572896 | tf_op jit(solution)/shard_map/all_to_all | solution.py:496
  166.2 0.7 spread.1
  166.9 6.5 %all-to-all-start.5 = ((f32[16,16,128]{2,1,0:T(8,128)}), f32[16,16,128]{2,1,0:T(8,128)S(1)}, u32[]{:S(2)}, u32[]{:S(2)}) async-start(f32[16,16,128]{2,1,0:T(8,128)} %spread.1), calls=%async_computation.5 | async-start | bytes 262144 | tf_op jit(solution)/shard_map/all_to_all | solution.py:496
  173.4 4.9 %finish.1 = (bf16[128,1152]{1,0:T(8,128)(2,1)}, bf16[3,128,1536]{2,1,0:T(8,128)(2,1)}) custom-call(bf16[16,384,128]{2,1,0:T(8,128)(2,1)} %copy-done.1, bf16[16,384,128]{2,1,0:T(8,128)(2,1)} %copy-done.1, bf16[1536,1152]{1,0:T(8,128)(2,1)} %all-gather.4.cloned.1.call-done.weight_ref), custom_call_target="tpu_custom_call" | custom-call | tf_op jit(solution)/shard_map/finish/pallas_call | solution.py:485
  178.3 4.3 %all-to-all-done.5.small_ref = f32[16,16,128]{2,1,0:T(8,128)S(1)} async-done(((f32[16,16,128]{2,1,0:T(8,128)}), f32[16,16,128]{2,1,0:T(8,128)S(1)}, u32[]{:S(2)}, u32[]{:S(2)}) %all-to-all-start.5) | async-done | bytes 131104 | tf_op jit(solution)/shard_map/all_to_all | solution.py:496
  182.6 0.8 small.1
  (37 shorter events, 0.2 us)
Async XLA Ops:
  7.2 16.0 %copy-start = (f32[9,1536]{1,0:T(8,128)S(1)}, f32[9,1536]{1,0:T(8,128)}, u32[]{:S(2)}) copy-start(f32[9,1536]{1,0:T(8,128)} %param.11) | copy-start | bytes 165892
  7.2 71.8 %all-gather.6.cloned.1.call-start = ((), (), s32[]{:S(2)}) async-start(), calls=%async_computation.7 | async-start | bytes 5013504 | tf_op jit(solution)/shard_map/all_gather | solution.py:508
  8.6 1.3 copy-start.5
  11.3 10.6 %copy-start.15 = (s32[48]{0:T(128)S(1)}, s32[48]{0:T(128)}, u32[]{:S(2)}) copy-start(s32[48]{0:T(128)} %param.12) | copy-start | bytes 580
  11.3 50.9 %copy-start.6 = (bf16[96,1152]{1,0:T(8,128)(2,1)S(1)}, bf16[96,1152]{1,0:T(8,128)(2,1)}, u32[]{:S(2)}) copy-start(bf16[96,1152]{1,0:T(8,128)(2,1)} %weight_ref.1) | copy-start | bytes 663556
  11.3 50.8 %all-to-all-start = ((bf16[16,304,128]{2,1,0:T(8,128)(2,1)}), bf16[16,304,128]{2,1,0:T(8,128)(2,1)S(1)}, u32[]{:S(2)}, u32[]{:S(2)}) async-start(bf16[16,304,128]{2,1,0:T(8,128)(2,1)} %prepare.1), calls=%async_computation | async-start | bytes 2490368 | tf_op jit(solution)/shard_map/all_to_all | solution.py:496
  21.8 151.6 %all-gather.4.cloned.1.call-start = ((), (), s32[]{:S(2)}) async-start(), calls=%async_computation.6 | async-start | bytes 3760128 | tf_op jit(solution)/shard_map/all_gather | solution.py:538
  22.1 61.2 %copy-start.9 = (s32[96,1]{1,0:T(8,128)}, s32[96,1]{1,0:T(8,128)S(1)}, u32[]{:S(2)}) copy-start(s32[96,1]{1,0:T(8,128)S(1)} %broadcast_in_dim_reshape.9.refs_4_.refs_3_) | copy-start | bytes 1156
  22.2 61.1 %copy-start.12 = (s32[1,96]{1,0:T(1,128)}, s32[1,96]{1,0:T(1,128)S(1)}, u32[]{:S(2)}) copy-start(s32[1,96]{1,0:T(1,128)S(1)} %broadcast_in_dim_reshape.7.refs_2_) | copy-start | bytes 1156
  23.1 55.9 %copy-start.4 = (f32[96,1]{1,0:T(8,128)}, f32[96,1]{1,0:T(8,128)S(1)}, u32[]{:S(2)}) copy-start(f32[96,1]{1,0:T(8,128)S(1)} %copy.14.refs_5_.gain_ref.refs_11_) | copy-start | bytes 1156
  23.3 60.0 %copy-start.10 = (f32[96,16]{1,0:T(8,128)}, f32[96,16]{1,0:T(8,128)S(1)}, u32[]{:S(2)}) copy-start(f32[96,16]{1,0:T(8,128)S(1)} %pad.9.refs_1_) | copy-start | bytes 18436
  62.2 21.2 %copy-start.2 = (bf16[16,304,128]{2,1,0:T(8,128)(2,1)}, bf16[16,304,128]{2,1,0:T(8,128)(2,1)S(1)}, u32[]{:S(2)}) copy-start(bf16[16,304,128]{2,1,0:T(8,128)(2,1)S(1)} %all-to-all-done.refs_0_) | copy-start | bytes 3735556
  68.6 0.9 copy-start.3
  69.5 0.9 copy-start.7
  70.4 0.8 copy-start.8
  71.2 13.7 %all-to-all-start.1 = ((bf16[16,16,128]{2,1,0:T(8,128)(2,1)}), bf16[16,16,128]{2,1,0:T(8,128)(2,1)S(1)}, u32[]{:S(2)}, u32[]{:S(2)}) async-start(bf16[16,16,128]{2,1,0:T(8,128)(2,1)} %get-tuple-element.28), calls=%async_computation.1 | async-start | bytes 131072 | tf_op jit(solution)/shard_map/all_to_all | solution.py:496
  84.9 3.9 %copy-start.14 = (bf16[16,16,128]{2,1,0:T(8,128)(2,1)}, bf16[16,16,128]{2,1,0:T(8,128)(2,1)S(1)}, u32[]{:S(2)}) copy-start(bf16[16,16,128]{2,1,0:T(8,128)(2,1)S(1)} %all-to-all-done.1.squares_ref) | copy-start | bytes 196612
  84.9 11.7 %all-to-all-start.2 = ((bf16[16,16,128]{2,1,0:T(8,128)(2,1)}), bf16[16,16,128]{2,1,0:T(8,128)(2,1)S(1)}, u32[]{:S(2)}, u32[]{:S(2)}) async-start(bf16[16,16,128]{2,1,0:T(8,128)(2,1)} %get-tuple-element.31), calls=%async_computation.2 | async-start | bytes 131072 | tf_op jit(solution)/shard_map/all_to_all | solution.py:496
  96.6 12.2 %copy-start.13 = (bf16[16,16,128]{2,1,0:T(8,128)(2,1)}, bf16[16,16,128]{2,1,0:T(8,128)(2,1)S(1)}, u32[]{:S(2)}) copy-start(bf16[16,16,128]{2,1,0:T(8,128)(2,1)S(1)} %all-to-all-done.2.refs_10_) | copy-start | bytes 196612
  96.6 26.9 %all-to-all-start.4 = ((bf16[32,32,128]{2,1,0:T(8,128)(2,1)}), bf16[32,32,128]{2,1,0:T(8,128)(2,1)S(1)}, u32[]{:S(2)}, u32[]{:S(2)}) async-start(bf16[32,32,128]{2,1,0:T(8,128)(2,1)} %bitcast.20), calls=%async_computation.4 | async-start | bytes 524288 | tf_op jit(solution)/shard_map/all_to_all | solution.py:496
  123.5 4.3 %copy-start.11 = (f32[16,128]{1,0:T(8,128)S(1)}, f32[16,128]{1,0:T(8,128)}, u32[]{:S(2)}) copy-start(f32[16,128]{1,0:T(8,128)} %get-tuple-element.38.small_ref) | copy-start | bytes 24580
  123.5 42.7 %all-to-all-start.3 = ((bf16[16,384,128]{2,1,0:T(8,128)(2,1)}), bf16[16,384,128]{2,1,0:T(8,128)(2,1)S(1)}, u32[]{:S(2)}, u32[]{:S(2)}) async-start(bf16[16,384,128]{2,1,0:T(8,128)(2,1)} %get-tuple-element.33), calls=%async_computation.3 | async-start | bytes 3145728 | tf_op jit(solution)/shard_map/all_to_all | solution.py:496
  127.8 4.5 %collective-permute-start = (bf16[64,128]{1,0:T(8,128)(2,1)S(1)}, bf16[64,128]{1,0:T(8,128)(2,1)S(1)}, u32[]{:S(2)}, u32[]{:S(2)}) collective-permute-start(bf16[64,128]{1,0:T(8,128)(2,1)S(1)} %pack_sum.1.own_ref), channel_id=1, source_target_pairs={{0,16},{16,0},{32,48},{48,32},{64,80},{80,64},{96,112},{112,96},{1... | collective-permute-start | bytes 49160 | tf_op jit(solution)/shard_map/ppermute | solution.py:609
  132.3 5.8 %collective-permute-start.1 = (bf16[96,128]{1,0:T(8,128)(2,1)S(1)}, bf16[96,128]{1,0:T(8,128)(2,1)S(1)}, u32[]{:S(2)}, u32[]{:S(2)}) collective-permute-start(bf16[96,128]{1,0:T(8,128)(2,1)S(1)} %join.4.own_ref), channel_id=1, source_target_pairs={{0,32},{16,48},{32,0},{48,16},{64,96},{80,112},{96,64},{112,80},{1... | collective-permute-start | bytes 73736 | tf_op jit(solution)/shard_map/ppermute | solution.py:609
  138.1 9.1 %collective-permute-start.2 = (bf16[160,128]{1,0:T(8,128)(2,1)S(1)}, bf16[160,128]{1,0:T(8,128)(2,1)S(1)}, u32[]{:S(2)}, u32[]{:S(2)}) collective-permute-start(bf16[160,128]{1,0:T(8,128)(2,1)S(1)} %join.5.own_ref), channel_id=1, source_target_pairs={{0,64},{16,80},{32,96},{48,112},{64,0},{80,16},{96,32},{112,48},{1... | collective-permute-start | bytes 122888 | tf_op jit(solution)/shard_map/ppermute | solution.py:609
  147.2 5.4 %collective-permute-start.3 = (bf16[288,128]{1,0:T(8,128)(2,1)S(1)}, bf16[288,128]{1,0:T(8,128)(2,1)S(1)}, u32[]{:S(2)}, u32[]{:S(2)}) collective-permute-start(bf16[288,128]{1,0:T(8,128)(2,1)S(1)} %join.6.own_ref), channel_id=1, source_target_pairs={{0,128},{16,144},{32,160},{48,176},{64,192},{80,208},{96,224},{112... | collective-permute-start | bytes 221192 | tf_op jit(solution)/shard_map/ppermute | solution.py:609
  152.6 7.6 %collective-permute-start.4 = (bf16[544,128]{1,0:T(8,128)(2,1)S(1)}, bf16[544,128]{1,0:T(8,128)(2,1)S(1)}, u32[]{:S(2)}, u32[]{:S(2)}) collective-permute-start(bf16[544,128]{1,0:T(8,128)(2,1)S(1)} %join.7.refs_1_), channel_id=1, source_target_pairs={{0,256},{16,272},{32,288},{48,304},{64,320},{80,336},{96,352},{112... | collective-permute-start | bytes 417800 | tf_op jit(solution)/shard_map/ppermute | solution.py:609
  166.2 7.2 %copy-start.1 = (bf16[16,384,128]{2,1,0:T(8,128)(2,1)}, bf16[16,384,128]{2,1,0:T(8,128)(2,1)S(1)}, u32[]{:S(2)}) copy-start(bf16[16,384,128]{2,1,0:T(8,128)(2,1)S(1)} %all-to-all-done.3.normed_ref.grad_ref._) | copy-start | bytes 4718596
  166.9 15.7 %all-to-all-start.5 = ((f32[16,16,128]{2,1,0:T(8,128)}), f32[16,16,128]{2,1,0:T(8,128)S(1)}, u32[]{:S(2)}, u32[]{:S(2)}) async-start(f32[16,16,128]{2,1,0:T(8,128)} %spread.1), calls=%async_computation.5 | async-start | bytes 262144 | tf_op jit(solution)/shard_map/all_to_all | solution.py:496
Sparse Core Ops, SparseCore 0:
  10.1 68.8 all-gather.5
  81.1 44.1 all-gather.3

commit v6 on v5

--- a/solution.py
+++ b/solution.py
@@ -10,7 +10,8 @@
 HEAD = 32
 FEAT = 256
 LANES = 128
-CHUNK = 256
+CHUNK = 512
+PIECES = CHUNK // LANES
 VMEM = 24 * 1024 * 1024
 ALL_VMEM = 60 * 1024 * 1024
 WIDTHS = (16, 32, 48, 64)
@@ -70,7 +71,7 @@
 
 def chunk_of(ref, part, width, j):
     rows = pl.ds(part * width, width)
-    return jnp.concatenate([ref[2 * j, rows, :], ref[2 * j + 1, rows, :]], axis=1)
+    return jnp.concatenate([ref[PIECES * j + i, rows, :] for i in range(PIECES)], axis=1)
 
 
 def part_of(ref, start, count):
@@ -246,7 +247,7 @@
     rows = [
         total[:, part * LANES : (part + 1) * LANES]
         for total in sums
-        for part in range(CHUNK // LANES)
+        for part in range(PIECES)
     ]
     rows = jnp.concatenate(rows, axis=0).astype(bf16)
     for peer in range(out_ref.shape[0]):
@@ -254,7 +255,8 @@
 
 
 def tokens_of(values, j):
-    return jnp.concatenate([values[2 * j : 2 * j + 1], values[2 * j + 1 : 2 * j + 2]], axis=1)
+    first = PIECES * j
+    return jnp.concatenate([values[first + i : first + i + 1] for i in range(PIECES)], axis=1)
 
 
 def inner_kernel(attention_ref, weight_ref, cotangent_ref, gain_ref,
@@ -269,7 +271,7 @@
         grad_normed_ref[:, lanes] = grad_normed
         attention = attention_ref[:, lanes].astype(f32)
         inner = jnp.sum(gain * grad_normed * attention, axis=0, keepdims=True)
-        for part in range(CHUNK // LANES):
+        for part in range(PIECES):
             rows.append(inner[:, part * LANES : (part + 1) * LANES])
     for i, row in enumerate(rows):
         rows_ref[step * len(rows) + i] = row
@@ -298,8 +300,8 @@
         attention = attention_ref[:, lanes].astype(f32)
         normed = (attention * gain * inv_rms).astype(bf16)
         gain_sum = add(gain_sum, grad_normed_ref[:, lanes] * attention * inv_rms)
-        for part in range(CHUNK // LANES):
-            normed_ref[2 * j + part] = normed[:, part * LANES : (part + 1) * LANES]
+        for part in range(PIECES):
+            normed_ref[PIECES * j + part] = normed[:, part * LANES : (part + 1) * LANES]
         weight = add(weight, dot(normed, cotangent_ref[pl.ds(j * CHUNK, CHUNK), :]))
     gain_out[...] = jnp.broadcast_to(jnp.sum(gain_sum, axis=1, keepdims=True), gain_out.shape)
     across = weight.shape[1] // LANES
@@ -332,8 +334,8 @@
     away = inverse * inverse * inverse * away
 
     def put(part, j, values):
-        for half in range(CHUNK // LANES):
-            out_ref[2 * j + half, pl.ds(part * width, width), :] = values[
+        for half in range(PIECES):
+            out_ref[PIECES * j + half, pl.ds(part * width, width), :] = values[
                 :, half * LANES : (half + 1) * LANES
             ]
 

time: 191 us -> 189 us (0.990)
  transfers between devices with their start and end apart: 13 -> 13, of which waited for: 11 -> 11; matrix products, arithmetic and copies ran while one was open for 1% -> 1% of each run, Pallas kernels for 20% -> 19%
where the time goes in v6:
time: 189 us; the launch traced here: 188 us
  starting transfers between devices  65.8 us (35%)
  waiting for transfers between devices  65.5 us (35%)
  Pallas kernels  36.8 us (19%)
  between operations  14.2 us (8%)
  local copies, waits for them, and re-layouts  6.04 us (3%)
    all_to_all x6, waiting for transfers between devices, swap(): return lax.all_to_all(blocks, axis, split_axis=0, concat_axis=0, tiled=True)  52.6 us
    all_to_all x6, starting transfers between devices, swap(): return lax.all_to_all(blocks, axis, split_axis=0, concat_axis=0, tiled=True)  43.1 us
    pallas_call x14, Pallas kernels, call(): pl.pallas_call(kernel, name=name, out_shape=[jax.ShapeDtypeStruct(shape,...  36.8 us
    ppermute x5, starting transfers between devices, local(): got = lax.ppermute(joined, 'dp', [(i, i ^ distance) for i in range(packs)])  22.6 us
    ppermute x5, waiting for transfers between devices, local(): got = lax.ppermute(joined, 'dp', [(i, i ^ distance) for i in range(packs)])  9.67 us
    unnamed x34, local copies, waits for them, and re-layouts  4.73 us
  transfers between devices with their start and end apart: 13, of which 11 were waited for; matrix products, arithmetic and copies ran while one was open for 1% of the time, Pallas kernels for 19%

profile of v6, /device:TPU:1, one launch (start us, length us, event | category | flops | bytes accessed | tf_op | source)
XLA Modules:
  0.0 188.4 jit_solution(18266310790873926434)
XLA Ops:
  7.2 0.0 all-gather.6.cloned.1.call-start
  7.2 0.7 all-gather.6.cloned.1.call-update
  7.9 0.7 copy.22
  8.6 1.3 copy-done.5
  9.9 1.4 prepare.1
  11.3 10.5 %all-to-all-start = ((bf16[16,304,128]{2,1,0:T(8,128)(2,1)}), bf16[16,304,128]{2,1,0:T(8,128)(2,1)S(1)}, u32[]{:S(2)}, u32[]{:S(2)}) async-start(bf16[16,304,128]{2,1,0:T(8,128)(2,1)} %prepare.1), calls=%async_computation | async-start | bytes 2490368 | tf_op jit(solution)/shard_map/all_to_all | solution.py:498
  21.8 0.0 all-gather.4.cloned.1.call-start
  21.9 0.1 dynamic_slice.10
  22.0 0.1 broadcast_in_dim.15
  22.0 0.1 broadcast_in_dim_reshape.9.refs_4_.refs_3_
  22.2 0.1 broadcast_in_dim_reshape.7.refs_2_
  22.2 0.8 dynamic-slice_bitcast_fusion
  23.0 0.1 copy.14.refs_5_.gain_ref.refs_11_
  23.1 0.1 constant_dynamic-slice_fusion
  23.2 0.1 copy.20
  23.3 38.8 %all-to-all-done.refs_0_ = bf16[16,304,128]{2,1,0:T(8,128)(2,1)S(1)} async-done(((bf16[16,304,128]{2,1,0:T(8,128)(2,1)}), bf16[16,304,128]{2,1,0:T(8,128)(2,1)S(1)}, u32[]{:S(2)}, u32[]{:S(2)}) %all-to-all-start) | async-done | bytes 1245216 | tf_op jit(solution)/shard_map/all_to_all | solution.py:498
  62.2 5.8 %forward.1 = (f32[104,2048]{1,0:T(8,128)S(1)}, bf16[192,2048]{1,0:T(8,128)(2,1)S(1)}, bf16[16,16,128]{2,1,0:T(8,128)(2,1)}, bf16[384,768]{1,0:T(8,128)(2,1)S(1)}, bf16[96,1152]{1,0:T(8,128)(2,1)}) custom-call(bf16[16,304,128]{2,1,0:T(8,128)(2,1)S(1)} %all-to-all-done.refs_0_, f32[96,16]{1,0:T(8,128)S(1)} %pad.9.refs_1_, ...), custom_call_target="tpu_custom_call" | custom-call | tf_op jit(solution)/shard_map/forward/pallas_call | solution.py:487
  68.0 0.9 copy-done.3
  68.9 0.9 copy-done.7
  69.8 0.8 copy-done.8
  70.6 0.0 all-gather.4.cloned.1.call-update
  70.7 5.9 %all-to-all-start.1 = ((bf16[16,16,128]{2,1,0:T(8,128)(2,1)}), bf16[16,16,128]{2,1,0:T(8,128)(2,1)S(1)}, u32[]{:S(2)}, u32[]{:S(2)}) async-start(bf16[16,16,128]{2,1,0:T(8,128)(2,1)} %get-tuple-element.28), calls=%async_computation.1 | async-start | bytes 131072 | tf_op jit(solution)/shard_map/all_to_all | solution.py:498
  76.5 2.5 %all-gather.6.cloned.1.call-done = bf16[1,2048,1152]{2,1,0:T(8,128)(2,1)} async-done(((bf16[1,128,1152]{2,1,0:T(8,128)(2,1)}), bf16[1,2048,1152]{2,1,0:T(8,128)(2,1)}) %all-gather.6.cloned.1.call-update) | async-done | bytes 4718608 | tf_op jit(solution)/shard_map/all_gather | solution.py:510
  79.0 4.3 %inner.1 = (f32[96,2048]{1,0:T(8,128)}, bf16[16,16,128]{2,1,0:T(8,128)(2,1)}) custom-call(bf16[192,2048]{1,0:T(8,128)(2,1)} %copy-done.3, bf16[96,1152]{1,0:T(8,128)(2,1)} %weight_ref.1, bf16[2048,1152]{1,0:T(8,128)(2,1)} %bitcast.18, f32[96,1]{1,0:T(8,128)} %copy-done.4), custom_call_target="tpu_custom_call" | custom-call | tf_op jit(solution)/shard_map/inner/pallas_call | solution.py:487
  83.4 1.0 all-to-all-done.1.squares_ref
  84.4 3.9 %all-to-all-start.2 = ((bf16[16,16,128]{2,1,0:T(8,128)(2,1)}), bf16[16,16,128]{2,1,0:T(8,128)(2,1)S(1)}, u32[]{:S(2)}, u32[]{:S(2)}) async-start(bf16[16,16,128]{2,1,0:T(8,128)(2,1)} %get-tuple-element.31), calls=%async_computation.2 | async-start | bytes 131072 | tf_op jit(solution)/shard_map/all_to_all | solution.py:498
  88.2 4.4 %normed.1 = (bf16[16,96,128]{2,1,0:T(8,128)(2,1)}, f32[16,128]{1,0:T(8,128)}, bf16[1024,128]{1,0:T(8,128)(2,1)}, f32[96,128]{1,0:T(8,128)}) custom-call(bf16[192,2048]{1,0:T(8,128)(2,1)} %copy-done.3, f32[96,2048]{1,0:T(8,128)} %get-tuple-element.27.grad_normed_ref.refs_8_, bf16[16,16,128]{2,1,0:T(8,128)(2,1)} %copy-done.14, f32[96,1]{1,0:T(8,128)} %copy-done.4, ...), custom_call_target="tpu_custom_call" | custom-call | tf_op jit(solution)/shard_map/normed/pallas_call | solution.py:487
  92.7 3.4 %all-to-all-done.2.refs_10_ = bf16[16,16,128]{2,1,0:T(8,128)(2,1)S(1)} async-done(((bf16[16,16,128]{2,1,0:T(8,128)(2,1)}), bf16[16,16,128]{2,1,0:T(8,128)(2,1)S(1)}, u32[]{:S(2)}, u32[]{:S(2)}) %all-to-all-start.2) | async-done | bytes 65568 | tf_op jit(solution)/shard_map/all_to_all | solution.py:498
  96.0 12.2 %all-to-all-start.4 = ((bf16[32,32,128]{2,1,0:T(8,128)(2,1)}), bf16[32,32,128]{2,1,0:T(8,128)(2,1)S(1)}, u32[]{:S(2)}, u32[]{:S(2)}) async-start(bf16[32,32,128]{2,1,0:T(8,128)(2,1)} %bitcast.20), calls=%async_computation.4 | async-start | bytes 524288 | tf_op jit(solution)/shard_map/all_to_all | solution.py:498
  108.3 13.5 %backward.1 = (bf16[16,384,128]{2,1,0:T(8,128)(2,1)}, f32[16,128]{1,0:T(8,128)}) custom-call(bf16[16,304,128]{2,1,0:T(8,128)(2,1)} %copy-done.2, f32[96,16]{1,0:T(8,128)} %copy-done.10, s32[1,96]{1,0:T(1,128)} %copy-done.12, s32[96,1]{1,0:T(8,128)} %copy-done.9, f32[104,2048]{1,0:T(8,128)} %copy-done.7, bf16[192,2048]{1,0:T(8,128)(2,1)} %copy-done.3, ...), custom_call_target="tpu_custom_call" | custom-call | tf_op jit(solution)/shard_map/backward/pallas_call | solution.py:487
  121.8 4.2 %all-to-all-start.3 = ((bf16[16,384,128]{2,1,0:T(8,128)(2,1)}), bf16[16,384,128]{2,1,0:T(8,128)(2,1)S(1)}, u32[]{:S(2)}, u32[]{:S(2)}) async-start(bf16[16,384,128]{2,1,0:T(8,128)(2,1)} %get-tuple-element.33), calls=%async_computation.3 | async-start | bytes 3145728 | tf_op jit(solution)/shard_map/all_to_all | solution.py:498
  126.0 3.2 %collective-permute-start = (bf16[64,128]{1,0:T(8,128)(2,1)S(1)}, bf16[64,128]{1,0:T(8,128)(2,1)S(1)}, u32[]{:S(2)}, u32[]{:S(2)}) collective-permute-start(bf16[64,128]{1,0:T(8,128)(2,1)S(1)} %pack_sum.1.own_ref), channel_id=1, source_target_pairs={{0,16},{16,0},{32,48},{48,32},{64,80},{80,64},{96,112},{112,96},{1... | collective-permute-start | bytes 49160 | tf_op jit(solution)/shard_map/ppermute | solution.py:611
  129.3 1.3 collective-permute-done.got_ref
  130.5 4.1 %collective-permute-start.1 = (bf16[96,128]{1,0:T(8,128)(2,1)S(1)}, bf16[96,128]{1,0:T(8,128)(2,1)S(1)}, u32[]{:S(2)}, u32[]{:S(2)}) collective-permute-start(bf16[96,128]{1,0:T(8,128)(2,1)S(1)} %join.4.own_ref), channel_id=1, source_target_pairs={{0,32},{16,48},{32,0},{48,16},{64,96},{80,112},{96,64},{112,80},{1... | collective-permute-start | bytes 73736 | tf_op jit(solution)/shard_map/ppermute | solution.py:611
  134.7 1.6 collective-permute-done.1.got_ref
  136.3 7.3 %collective-permute-start.2 = (bf16[160,128]{1,0:T(8,128)(2,1)S(1)}, bf16[160,128]{1,0:T(8,128)(2,1)S(1)}, u32[]{:S(2)}, u32[]{:S(2)}) collective-permute-start(bf16[160,128]{1,0:T(8,128)(2,1)S(1)} %join.5.own_ref), channel_id=1, source_target_pairs={{0,64},{16,80},{32,96},{48,112},{64,0},{80,16},{96,32},{112,48},{1... | collective-permute-start | bytes 122888 | tf_op jit(solution)/shard_map/ppermute | solution.py:611
  143.7 1.7 collective-permute-done.2.got_ref
  145.3 3.2 %collective-permute-start.3 = (bf16[288,128]{1,0:T(8,128)(2,1)S(1)}, bf16[288,128]{1,0:T(8,128)(2,1)S(1)}, u32[]{:S(2)}, u32[]{:S(2)}) collective-permute-start(bf16[288,128]{1,0:T(8,128)(2,1)S(1)} %join.6.own_ref), channel_id=1, source_target_pairs={{0,128},{16,144},{32,160},{48,176},{64,192},{80,208},{96,224},{112... | collective-permute-start | bytes 221192 | tf_op jit(solution)/shard_map/ppermute | solution.py:611
  148.5 2.2 %collective-permute-done.3.got_ref = bf16[288,128]{1,0:T(8,128)(2,1)S(1)} collective-permute-done((bf16[288,128]{1,0:T(8,128)(2,1)S(1)}, bf16[288,128]{1,0:T(8,128)(2,1)S(1)}, u32[]{:S(2)}, u32[]{:S(2)}) %collective-permute-start.3) | collective-permute-done | bytes 73760 | tf_op jit(solution)/shard_map/ppermute | solution.py:611
  150.8 4.7 %collective-permute-start.4 = (bf16[544,128]{1,0:T(8,128)(2,1)S(1)}, bf16[544,128]{1,0:T(8,128)(2,1)S(1)}, u32[]{:S(2)}, u32[]{:S(2)}) collective-permute-start(bf16[544,128]{1,0:T(8,128)(2,1)S(1)} %join.7.refs_1_), channel_id=1, source_target_pairs={{0,256},{16,272},{32,288},{48,304},{64,320},{80,336},{96,352},{112... | collective-permute-start | bytes 417800 | tf_op jit(solution)/shard_map/ppermute | solution.py:611
  155.4 2.9 %collective-permute-done.4.refs_2_ = bf16[544,128]{1,0:T(8,128)(2,1)S(1)} collective-permute-done((bf16[544,128]{1,0:T(8,128)(2,1)S(1)}, bf16[544,128]{1,0:T(8,128)(2,1)S(1)}, u32[]{:S(2)}, u32[]{:S(2)}) %collective-permute-start.4) | collective-permute-done | bytes 139296 | tf_op jit(solution)/shard_map/ppermute | solution.py:611
  158.4 0.8 unpack.1
  159.2 5.2 %all-to-all-done.3.normed_ref.grad_ref._ = bf16[16,384,128]{2,1,0:T(8,128)(2,1)S(1)} async-done(((bf16[16,384,128]{2,1,0:T(8,128)(2,1)}), bf16[16,384,128]{2,1,0:T(8,128)(2,1)S(1)}, u32[]{:S(2)}, u32[]{:S(2)}) %all-to-all-start.3) | async-done | bytes 1572896 | tf_op jit(solution)/shard_map/all_to_all | solution.py:498
  164.4 0.7 spread.1
  165.1 6.5 %all-to-all-start.5 = ((f32[16,16,128]{2,1,0:T(8,128)}), f32[16,16,128]{2,1,0:T(8,128)S(1)}, u32[]{:S(2)}, u32[]{:S(2)}) async-start(f32[16,16,128]{2,1,0:T(8,128)} %spread.1), calls=%async_computation.5 | async-start | bytes 262144 | tf_op jit(solution)/shard_map/all_to_all | solution.py:498
  171.6 4.9 %finish.1 = (bf16[128,1152]{1,0:T(8,128)(2,1)}, bf16[3,128,1536]{2,1,0:T(8,128)(2,1)}) custom-call(bf16[16,384,128]{2,1,0:T(8,128)(2,1)} %copy-done.1, bf16[16,384,128]{2,1,0:T(8,128)(2,1)} %copy-done.1, bf16[1536,1152]{1,0:T(8,128)(2,1)} %all-gather.4.cloned.1.call-done.weight_ref), custom_call_target="tpu_custom_call" | custom-call | tf_op jit(solution)/shard_map/finish/pallas_call | solution.py:487
  176.5 4.3 %all-to-all-done.5.small_ref = f32[16,16,128]{2,1,0:T(8,128)S(1)} async-done(((f32[16,16,128]{2,1,0:T(8,128)}), f32[16,16,128]{2,1,0:T(8,128)S(1)}, u32[]{:S(2)}, u32[]{:S(2)}) %all-to-all-start.5) | async-done | bytes 131104 | tf_op jit(solution)/shard_map/all_to_all | solution.py:498
  180.8 0.8 small.1
  (37 shorter events, 0.2 us)
Async XLA Ops:
  7.2 16.0 %copy-start = (f32[9,1536]{1,0:T(8,128)S(1)}, f32[9,1536]{1,0:T(8,128)}, u32[]{:S(2)}) copy-start(f32[9,1536]{1,0:T(8,128)} %param.11) | copy-start | bytes 165892
  7.2 71.8 %all-gather.6.cloned.1.call-start = ((), (), s32[]{:S(2)}) async-start(), calls=%async_computation.7 | async-start | bytes 5013504 | tf_op jit(solution)/shard_map/all_gather | solution.py:510
  8.6 1.3 copy-start.5
  11.3 10.6 %copy-start.15 = (s32[48]{0:T(128)S(1)}, s32[48]{0:T(128)}, u32[]{:S(2)}) copy-start(s32[48]{0:T(128)} %param.12) | copy-start | bytes 580
  11.3 50.9 %copy-start.6 = (bf16[96,1152]{1,0:T(8,128)(2,1)S(1)}, bf16[96,1152]{1,0:T(8,128)(2,1)}, u32[]{:S(2)}) copy-start(bf16[96,1152]{1,0:T(8,128)(2,1)} %weight_ref.1) | copy-start | bytes 663556
  11.3 50.8 %all-to-all-start = ((bf16[16,304,128]{2,1,0:T(8,128)(2,1)}), bf16[16,304,128]{2,1,0:T(8,128)(2,1)S(1)}, u32[]{:S(2)}, u32[]{:S(2)}) async-start(bf16[16,304,128]{2,1,0:T(8,128)(2,1)} %prepare.1), calls=%async_computation | async-start | bytes 2490368 | tf_op jit(solution)/shard_map/all_to_all | solution.py:498
  21.8 149.8 %all-gather.4.cloned.1.call-start = ((), (), s32[]{:S(2)}) async-start(), calls=%async_computation.6 | async-start | bytes 3760128 | tf_op jit(solution)/shard_map/all_gather | solution.py:540
  22.1 61.2 %copy-start.9 = (s32[96,1]{1,0:T(8,128)}, s32[96,1]{1,0:T(8,128)S(1)}, u32[]{:S(2)}) copy-start(s32[96,1]{1,0:T(8,128)S(1)} %broadcast_in_dim_reshape.9.refs_4_.refs_3_) | copy-start | bytes 1156
  22.2 61.1 %copy-start.12 = (s32[1,96]{1,0:T(1,128)}, s32[1,96]{1,0:T(1,128)S(1)}, u32[]{:S(2)}) copy-start(s32[1,96]{1,0:T(1,128)S(1)} %broadcast_in_dim_reshape.7.refs_2_) | copy-start | bytes 1156
  23.1 55.9 %copy-start.4 = (f32[96,1]{1,0:T(8,128)}, f32[96,1]{1,0:T(8,128)S(1)}, u32[]{:S(2)}) copy-start(f32[96,1]{1,0:T(8,128)S(1)} %copy.14.refs_5_.gain_ref.refs_11_) | copy-start | bytes 1156
  23.3 60.0 %copy-start.10 = (f32[96,16]{1,0:T(8,128)}, f32[96,16]{1,0:T(8,128)S(1)}, u32[]{:S(2)}) copy-start(f32[96,16]{1,0:T(8,128)S(1)} %pad.9.refs_1_) | copy-start | bytes 18436
  62.2 21.2 %copy-start.2 = (bf16[16,304,128]{2,1,0:T(8,128)(2,1)}, bf16[16,304,128]{2,1,0:T(8,128)(2,1)S(1)}, u32[]{:S(2)}) copy-start(bf16[16,304,128]{2,1,0:T(8,128)(2,1)S(1)} %all-to-all-done.refs_0_) | copy-start | bytes 3735556
  68.0 0.9 copy-start.3
  68.9 0.9 copy-start.7
  69.8 0.8 copy-start.8
  70.7 13.7 %all-to-all-start.1 = ((bf16[16,16,128]{2,1,0:T(8,128)(2,1)}), bf16[16,16,128]{2,1,0:T(8,128)(2,1)S(1)}, u32[]{:S(2)}, u32[]{:S(2)}) async-start(bf16[16,16,128]{2,1,0:T(8,128)(2,1)} %get-tuple-element.28), calls=%async_computation.1 | async-start | bytes 131072 | tf_op jit(solution)/shard_map/all_to_all | solution.py:498
  84.4 3.9 %copy-start.14 = (bf16[16,16,128]{2,1,0:T(8,128)(2,1)}, bf16[16,16,128]{2,1,0:T(8,128)(2,1)S(1)}, u32[]{:S(2)}) copy-start(bf16[16,16,128]{2,1,0:T(8,128)(2,1)S(1)} %all-to-all-done.1.squares_ref) | copy-start | bytes 196612
  84.4 11.7 %all-to-all-start.2 = ((bf16[16,16,128]{2,1,0:T(8,128)(2,1)}), bf16[16,16,128]{2,1,0:T(8,128)(2,1)S(1)}, u32[]{:S(2)}, u32[]{:S(2)}) async-start(bf16[16,16,128]{2,1,0:T(8,128)(2,1)} %get-tuple-element.31), calls=%async_computation.2 | async-start | bytes 131072 | tf_op jit(solution)/shard_map/all_to_all | solution.py:498
  96.0 12.2 %copy-start.13 = (bf16[16,16,128]{2,1,0:T(8,128)(2,1)}, bf16[16,16,128]{2,1,0:T(8,128)(2,1)S(1)}, u32[]{:S(2)}) copy-start(bf16[16,16,128]{2,1,0:T(8,128)(2,1)S(1)} %all-to-all-done.2.refs_10_) | copy-start | bytes 196612
  96.0 25.7 %all-to-all-start.4 = ((bf16[32,32,128]{2,1,0:T(8,128)(2,1)}), bf16[32,32,128]{2,1,0:T(8,128)(2,1)S(1)}, u32[]{:S(2)}, u32[]{:S(2)}) async-start(bf16[32,32,128]{2,1,0:T(8,128)(2,1)} %bitcast.20), calls=%async_computation.4 | async-start | bytes 524288 | tf_op jit(solution)/shard_map/all_to_all | solution.py:498
  121.8 4.2 %copy-start.11 = (f32[16,128]{1,0:T(8,128)S(1)}, f32[16,128]{1,0:T(8,128)}, u32[]{:S(2)}) copy-start(f32[16,128]{1,0:T(8,128)} %get-tuple-element.38.small_ref) | copy-start | bytes 24580
  121.8 42.6 %all-to-all-start.3 = ((bf16[16,384,128]{2,1,0:T(8,128)(2,1)}), bf16[16,384,128]{2,1,0:T(8,128)(2,1)S(1)}, u32[]{:S(2)}, u32[]{:S(2)}) async-start(bf16[16,384,128]{2,1,0:T(8,128)(2,1)} %get-tuple-element.33), calls=%async_computation.3 | async-start | bytes 3145728 | tf_op jit(solution)/shard_map/all_to_all | solution.py:498
  126.0 4.5 %collective-permute-start = (bf16[64,128]{1,0:T(8,128)(2,1)S(1)}, bf16[64,128]{1,0:T(8,128)(2,1)S(1)}, u32[]{:S(2)}, u32[]{:S(2)}) collective-permute-start(bf16[64,128]{1,0:T(8,128)(2,1)S(1)} %pack_sum.1.own_ref), channel_id=1, source_target_pairs={{0,16},{16,0},{32,48},{48,32},{64,80},{80,64},{96,112},{112,96},{1... | collective-permute-start | bytes 49160 | tf_op jit(solution)/shard_map/ppermute | solution.py:611
  130.5 5.8 %collective-permute-start.1 = (bf16[96,128]{1,0:T(8,128)(2,1)S(1)}, bf16[96,128]{1,0:T(8,128)(2,1)S(1)}, u32[]{:S(2)}, u32[]{:S(2)}) collective-permute-start(bf16[96,128]{1,0:T(8,128)(2,1)S(1)} %join.4.own_ref), channel_id=1, source_target_pairs={{0,32},{16,48},{32,0},{48,16},{64,96},{80,112},{96,64},{112,80},{1... | collective-permute-start | bytes 73736 | tf_op jit(solution)/shard_map/ppermute | solution.py:611
  136.3 9.0 %collective-permute-start.2 = (bf16[160,128]{1,0:T(8,128)(2,1)S(1)}, bf16[160,128]{1,0:T(8,128)(2,1)S(1)}, u32[]{:S(2)}, u32[]{:S(2)}) collective-permute-start(bf16[160,128]{1,0:T(8,128)(2,1)S(1)} %join.5.own_ref), channel_id=1, source_target_pairs={{0,64},{16,80},{32,96},{48,112},{64,0},{80,16},{96,32},{112,48},{1... | collective-permute-start | bytes 122888 | tf_op jit(solution)/shard_map/ppermute | solution.py:611
  145.3 5.4 %collective-permute-start.3 = (bf16[288,128]{1,0:T(8,128)(2,1)S(1)}, bf16[288,128]{1,0:T(8,128)(2,1)S(1)}, u32[]{:S(2)}, u32[]{:S(2)}) collective-permute-start(bf16[288,128]{1,0:T(8,128)(2,1)S(1)} %join.6.own_ref), channel_id=1, source_target_pairs={{0,128},{16,144},{32,160},{48,176},{64,192},{80,208},{96,224},{112... | collective-permute-start | bytes 221192 | tf_op jit(solution)/shard_map/ppermute | solution.py:611
  150.8 7.6 %collective-permute-start.4 = (bf16[544,128]{1,0:T(8,128)(2,1)S(1)}, bf16[544,128]{1,0:T(8,128)(2,1)S(1)}, u32[]{:S(2)}, u32[]{:S(2)}) collective-permute-start(bf16[544,128]{1,0:T(8,128)(2,1)S(1)} %join.7.refs_1_), channel_id=1, source_target_pairs={{0,256},{16,272},{32,288},{48,304},{64,320},{80,336},{96,352},{112... | collective-permute-start | bytes 417800 | tf_op jit(solution)/shard_map/ppermute | solution.py:611
  164.4 7.2 %copy-start.1 = (bf16[16,384,128]{2,1,0:T(8,128)(2,1)}, bf16[16,384,128]{2,1,0:T(8,128)(2,1)S(1)}, u32[]{:S(2)}) copy-start(bf16[16,384,128]{2,1,0:T(8,128)(2,1)S(1)} %all-to-all-done.3.normed_ref.grad_ref._) | copy-start | bytes 4718596
  165.1 15.7 %all-to-all-start.5 = ((f32[16,16,128]{2,1,0:T(8,128)}), f32[16,16,128]{2,1,0:T(8,128)S(1)}, u32[]{:S(2)}, u32[]{:S(2)}) async-start(f32[16,16,128]{2,1,0:T(8,128)} %spread.1), calls=%async_computation.5 | async-start | bytes 262144 | tf_op jit(solution)/shard_map/all_to_all | solution.py:498
Sparse Core Ops, SparseCore 0:
  10.1 68.8 all-gather.5
  81.1 44.2 all-gather.3
